TPU v7x, 32 devices: a whole 2x2x4 slice. The times are simulated.
32 devices in a mesh: clip: 8 (over z, x), patch: 4 (over y, core).
Axes of the slice: x: 2, y: 2, z: 4, core: 2. Of those that a mesh axis runs over, the one named last changes fastest.
Arguments:
- pixels: bfloat16 [128, 16, 64, 384], P(('clip', 'patch')), may hold values from -40 to 40
- destination: int32 [128, 1], P(('clip', 'patch')), may hold values from 0 to 7; in each aligned block of 4 rows (0 to 3, 4 to 7, ...) at most 2 rows name the same one
- embed_weight: bfloat16 [384, 128], replicated, may hold values from -0.3125 to 0.3125
- embed_gain: float32 [128], replicated, may hold values from 0.5 to 2
- mixing_weight: bfloat16 [9, 384, 256], replicated, may hold values from -0.109375 to 0.109375
- mixing_gain: float32 [256], replicated, may hold values from 0.5 to 2
- project_weight: bfloat16 [256, 512], replicated, may hold values from -0.375 to 0.375
- project_gain: float32 [512], replicated, may hold values from 0.25 to 1.75
Outputs:
- latents: bfloat16 [512, 8, 64, 512], P('clip', None, 'patch')
Inputs may be any that keep to these rules, and one draw needn't show every extreme that they name: `destination`: among the 4 clips of one owner device (aligned blocks of 4 rows) no tokenizer index occurs more than 2 times, and some index occurs exactly 2 times in some blocks.
All inputs are finite; a program needn't handle non-finite values.
Results may differ from a plain program's by a relative error of at most 0.0059.
Values may be sent and summed in bfloat16 or wider, within the bound.
No kernel may reach another device: no remote copies, remote signals or barrier semaphores. Data moves between devices by JAX's collectives and lax.ppermute only.
A program may use at most 128 MiB of HBM per device.

v0:
```python
import jax
import jax.numpy as jnp
from jax import lax
from jax.sharding import PartitionSpec as P

GRID = 8
GROUPS = 32
CAP = 2


def group_fold(per_channel):
    number, channels = per_channel.shape
    pooled = jnp.mean(
        per_channel.reshape(number, GROUPS, channels // GROUPS), axis=2, keepdims=True
    )
    return jnp.broadcast_to(pooled, (number, GROUPS, channels // GROUPS)).reshape(number, channels)


def group_norm(values, scales):
    average = group_fold(jnp.mean(values, axis=(1, 2)))
    centred = values - average[:, None, None, :]
    spread = group_fold(jnp.mean(centred * centred, axis=(1, 2)))
    return centred * lax.rsqrt(spread + 1e-05)[:, None, None, :] * scales


def neighbour_table(row_tap, col_tap):
    places = GRID * GRID
    target = jnp.arange(places, dtype=jnp.int32)
    row_src = target // GRID + (row_tap - 1)
    col_src = target % GRID + (col_tap - 1)
    inside = (row_src >= 0) & (row_src < GRID) & (col_src >= 0) & (col_src < GRID)
    source = row_src * GRID + col_src
    hits = (jnp.arange(places, dtype=jnp.int32)[None, :] == source[:, None]) & inside[:, None]
    return hits.astype(jnp.float32)


def encode(
    tubes, embed_weight, embed_gain, mixing_weight, mixing_gain, project_weight, project_gain
):
    number, frames, places, breadth = tubes.shape
    embedded = jnp.dot(tubes.reshape(-1, breadth), embed_weight, preferred_element_type=jnp.float32)
    embedded = embedded.reshape(number, frames, places, -1)
    first_act = jax.nn.silu(group_norm(embedded, embed_gain)).astype(jnp.bfloat16)
    channels = first_act.shape[-1]
    latent_frames = frames // 2
    paired = first_act.reshape(number, latent_frames, 2, places, channels)
    even_rows = paired[:, :, 0]
    odd_rows = paired[:, :, 1]
    prior_rows = jnp.concatenate(
        [jnp.zeros((number, 1, places, channels), jnp.bfloat16), odd_rows[:, :-1]], axis=1
    )
    even_rows = even_rows.reshape(-1, channels)
    odd_rows = odd_rows.reshape(-1, channels)
    prior_rows = prior_rows.reshape(-1, channels)
    outward = mixing_weight.shape[-1]
    summed = jnp.zeros((number * latent_frames, places, outward), jnp.float32)
    for row_tap in range(3):
        for col_tap in range(3):
            weight = mixing_weight[row_tap * 3 + col_tap]
            term = jnp.dot(prior_rows, weight[:channels], preferred_element_type=jnp.float32)
            term = term + jnp.dot(
                even_rows, weight[channels : 2 * channels], preferred_element_type=jnp.float32
            )
            term = term + jnp.dot(
                odd_rows, weight[2 * channels :], preferred_element_type=jnp.float32
            )
            term = term.reshape(number * latent_frames, places, outward)
            table = neighbour_table(row_tap, col_tap)
            summed = summed + jnp.matmul(table, term, precision=lax.Precision.HIGHEST)
    second = summed.reshape(number, latent_frames, places, outward)
    second_act = jax.nn.silu(group_norm(second, mixing_gain)).astype(jnp.bfloat16)
    projected = jnp.dot(
        second_act.reshape(-1, outward), project_weight, preferred_element_type=jnp.float32
    )
    projected = projected.reshape(number, latent_frames, places, -1)
    return group_norm(projected, project_gain).astype(jnp.bfloat16)


def on_device(
    pixels,
    destination,
    embed_weight,
    embed_gain,
    mixing_weight,
    mixing_gain,
    project_weight,
    project_gain,
):
    tokenizers = lax.axis_size("clip")
    positions = lax.axis_size("patch")
    owned = pixels.shape[0]
    targets = destination[:, 0]
    order = jnp.arange(owned, dtype=jnp.int32)
    same = targets[:, None] == targets[None, :]
    earlier = order[:, None] > order[None, :]
    ranks = jnp.sum((same & earlier).astype(jnp.int32), axis=1)
    local_slots = targets * CAP + ranks
    encoded = encode(
        pixels, embed_weight, embed_gain, mixing_weight, mixing_gain, project_weight, project_gain
    )
    latent_frames, places, channels = (encoded.shape[1], encoded.shape[2], encoded.shape[3])
    outgoing = (
        jnp.zeros((tokenizers * CAP, latent_frames, places, channels), jnp.bfloat16)
        .at[local_slots]
        .set(encoded)
    )
    share = places // positions
    arranged = outgoing.reshape(tokenizers, CAP, latent_frames, positions, share, channels)
    arranged = jnp.transpose(arranged, (0, 3, 1, 2, 4, 5)).reshape(
        tokenizers * positions * CAP, latent_frames, share, channels
    )
    arrived = lax.all_to_all(arranged, ("clip", "patch"), split_axis=0, concat_axis=0, tiled=True)
    arrived = arrived.reshape(tokenizers, positions, CAP, latent_frames, share, channels)
    arrived = jnp.transpose(arrived, (1, 0, 2, 3, 4, 5))
    return arrived.reshape(positions * tokenizers * CAP, latent_frames, share, channels)


def solution(mesh):
    return jax.shard_map(
        on_device,
        mesh=mesh,
        in_specs=(
            P(("clip", "patch"), None, None, None),
            P(("clip", "patch"), None),
            P(),
            P(),
            P(),
            P(),
            P(),
            P(),
        ),
        out_specs=P("clip", None, "patch", None),
        check_vma=False,
    )
```

profile of v0, /device:TPU:0, one launch (start us, length us, event | category | flops | bytes accessed | tf_op | source)
XLA Modules:
  0.0 264.7 jit_solution(8988252657009926734)
XLA Ops:
  0.0 1.9 copy-done
  1.9 3.2 %fusion.140 = (f32[4,128]{1,0:T(4,128)S(1)}, f32[4,16,64,128]{3,2,1,0:T(8,128)}) fusion(bf16[4,16,64,384]{3,2,1,0:T(8,128)(2,1)S(1)} %copy-done, bf16[384,128]{1,0:T(8,128)(2,1)} %param.10), kind=kOutput, calls=%fused_computation.214 | convolution fusion | flops 403176960 | bytes 5343232 | tf_op jit(solution)/shard_map/dot_general | solution.py:41
  5.5 2.0 multiply_reduce_fusion.1
  8.0 0.6 multiply_convert_fusion.2
  9.1 1.0 copy-done.4
  10.1 0.4 fusion.44
  10.5 0.4 fusion.40
  11.0 0.4 fusion.36
  11.4 0.4 fusion.32
  11.9 0.4 fusion.28
  12.3 0.4 fusion.24
  13.2 0.4 fusion.16
  13.6 0.4 fusion.12
  14.1 0.4 convolution_add_fusion.17
  14.5 0.4 convolution_add_fusion.15
  14.9 0.4 convolution_add_fusion.16
  15.8 0.4 convolution_add_fusion.13
  16.2 0.4 convolution_add_fusion.12
  16.6 0.4 convolution_add_fusion.11
  17.0 0.4 convolution_add_fusion.10
  17.5 0.4 convolution_add_fusion.9
  17.9 0.4 convolution_add_fusion.8
  18.3 0.4 convolution_add_fusion.7
  18.8 0.4 convolution_add_fusion.6
  19.2 0.4 convolution_add_fusion.5
  19.6 0.4 convolution_add_fusion.4
  20.0 0.4 convolution_add_fusion.3
  20.5 0.4 convolution_add_fusion.2
  20.9 0.4 convolution_add_fusion.1
  21.3 0.4 convolution_add_fusion
  21.7 1.1 fusion.75
  22.9 1.3 fusion.79
  24.2 1.1 fusion.83
  25.4 1.1 fusion.87
  26.5 1.1 fusion.91
  27.7 1.1 fusion.95
  28.8 1.1 fusion.99
  30.0 1.1 fusion.103
  31.1 3.6 %bitcast_reduce_fusion = (f32[32,256]{1,0:T(8,128)S(1)}, f32[64,32,256]{2,0,1:T(8,128)}) fusion(f32[32,64,256]{2,1,0:T(8,128)S(1)} %bitcast.244, s32[64]{0:T(128)S(1)} %fusion.135, pred[64]{0:T(512)(128)(4,1)S(1)} %and_and_fusion, f32[64,32,256]{2,0,1:T(8,128)S(1)} %fusion.103, f32[64,32,256]{2,0,1:T(8,128)S(1)} %fusion.99, f32[64,32,256]{2,0,1:T(8,128)S(1)} %fusion.95, ...), kind=kOutput, calls=%fused_computation.21 | convolution fusion | flops 407371776 | bytes 21004608 | tf_op jit(solution)/shard_map/dot_general | solution.py:69
  35.1 2.1 fusion.1
  37.7 2.9 %fusion.141 = (f32[4,512]{1,0:T(4,128)S(1)}, f32[4,8,64,512]{3,2,1,0:T(8,128)}) fusion(bf16[256,512]{1,0:T(8,128)(2,1)S(1)} %copy-done.7, f32[4,8,64,256]{3,2,1,0:T(8,128)S(1)} %bitcast.245, f32[256]{0:T(256)S(1)} %copy-done.8, f32[4,256]{1,0:T(4,128)S(1)} %rsqrt.36, f32[4,256]{1,0:T(4,128)S(1)} %sub.83), kind=kOutput, calls=%fused_computation.215 | convolution fusion | flops 542111744 | bytes 6571008 | tf_op jit(solution)/shard_map/dot_general | solution.py:72
  41.1 2.7 %multiply_reduce_fusion = f32[4,512]{1,0:T(4,128)S(1)} fusion(f32[4,8,64,512]{3,2,1,0:T(8,128)} %get-tuple-element.13, f32[4,512]{1,0:T(4,128)S(1)} %sub.90), kind=kLoop, calls=%fused_computation.2 | loop fusion | flops 3143680 | bytes 4210688 | tf_op jit(solution)/shard_map/reduce_sum | solution.py:22
  44.7 2.8 %multiply_convert_fusion = bf16[4,8,64,512]{3,2,1,0:T(8,128)(2,1)S(1)} fusion(f32[4,8,64,512]{3,2,1,0:T(8,128)} %get-tuple-element.13, f32[512]{0:T(512)S(1)} %copy-done.5, f32[4,512]{1,0:T(4,128)S(1)} %rsqrt.38, f32[4,512]{1,0:T(4,128)S(1)} %sub.90), kind=kLoop, calls=%fused_computation.1 | loop fusion | flops 4194304 | bytes 6309888 | tf_op jit(solution)/shard_map/convert_element_type | solution.py:76
  47.5 4.4 %broadcast_in_dim.14 = bf16[16,8,64,512]{3,2,1,0:T(8,128)(2,1)} broadcast(bf16[]{:T(256)} %constant.135.clone.1), dimensions={} | broadcast | bytes 8388610 | tf_op jit(solution)/shard_map/broadcast_in_dim | solution.py:103
  52.0 5.0 %scatter_fusion = bf16[16,8,64,512]{3,2,1,0:T(8,128)(2,1)} fusion(bf16[16,8,64,512]{3,2,1,0:T(8,128)(2,1)} %broadcast_in_dim.14, s32[4]{0:T(128)S(1)} %fusion.127, bf16[4,8,64,512]{3,2,1,0:T(8,128)(2,1)S(1)} %multiply_convert_fusion), kind=kCustom, calls=%fused_computation | custom fusion | bytes 6291472 | tf_op jit(solution)/shard_map/scatter | solution.py:105
  57.0 8.0 %copy.11 = bf16[8,4,2,8,16,512]{5,4,3,2,1,0:T(8,128)(2,1)} copy(bf16[8,4,2,8,16,512]{5,4,1,3,2,0:T(8,128)(2,1)} %bitcast.233) | data formatting | bytes 16777216 | tf_op jit(solution)/shard_map/transpose | solution.py:109
  65.0 190.9 %all_to_all.5 = bf16[64,8,16,512]{3,2,1,0:T(8,128)(2,1)} all-to-all(bf16[64,8,16,512]{3,2,1,0:T(8,128)(2,1)} %bitcast.234), channel_id=1, replica_groups=mesh['clip'=8,'patch'=4] {'clip','patch'}, dimensions={0} | all-to-all | bytes 16777216 | tf_op jit(solution)/shard_map/all_to_all | solution.py:112
  256.0 8.7 %copy.12 = bf16[4,8,2,8,16,512]{5,4,3,2,1,0:T(8,128)(2,1)} copy(bf16[4,8,2,8,16,512]{5,4,3,2,0,1:T(8,128)(2,1)} %bitcast.235) | data formatting | bytes 16777216 | tf_op jit(solution)/shard_map/transpose | solution.py:114
  (82 shorter events, 4.2 us)
Async XLA Ops:
  0.0 1.9 copy-start
  5.1 2.9 %copy-start.2 = (f32[4,16,64,128]{3,2,1,0:T(8,128)S(1)}, f32[4,16,64,128]{3,2,1,0:T(8,128)}, u32[]{:S(2)}) copy-start(f32[4,16,64,128]{3,2,1,0:T(8,128)} %get-tuple-element.9) | copy-start | bytes 6291460
  5.1 2.9 %copy-start.6 = (f32[128]{0:T(128)S(1)}, f32[128]{0:T(128)}, u32[]{:S(2)}) copy-start(f32[128]{0:T(128)} %param.11) | copy-start | bytes 1540
  8.6 1.5 copy-start.4
  34.7 3.0 %copy-start.3 = (f32[64,32,256]{2,0,1:T(8,128)S(1)}, f32[64,32,256]{2,0,1:T(8,128)}, u32[]{:S(2)}) copy-start(f32[64,32,256]{2,0,1:T(8,128)} %get-tuple-element.11) | copy-start | bytes 6291460
  34.7 3.0 %copy-start.7 = (bf16[256,512]{1,0:T(8,128)(2,1)S(1)}, bf16[256,512]{1,0:T(8,128)(2,1)}, u32[]{:S(2)}) copy-start(bf16[256,512]{1,0:T(8,128)(2,1)} %param.14) | copy-start | bytes 786436
  34.7 3.0 %copy-start.8 = (f32[256]{0:T(256)S(1)}, f32[256]{0:T(256)}, u32[]{:S(2)}) copy-start(f32[256]{0:T(256)} %param.13) | copy-start | bytes 3076
  41.1 3.2 %copy-start.9 = (s32[4,1]{0,1:T(1,128)S(1)}, s32[4,1]{0,1:T(1,128)}, u32[]{:S(2)}) copy-start(s32[4,1]{0,1:T(1,128)} %param.9) | copy-start | bytes 52
  41.1 3.6 %copy-start.5 = (f32[512]{0:T(512)S(1)}, f32[512]{0:T(512)}, u32[]{:S(2)}) copy-start(f32[512]{0:T(512)} %param.15) | copy-start | bytes 6148
  255.9 8.7 %copy-start.1 = (bf16[4,16,64,384]{3,2,1,0:T(8,128)(2,1)S(1)}, bf16[4,16,64,384]{3,2,1,0:T(8,128)(2,1)}, u32[]{:S(2)}) copy-start(bf16[4,16,64,384]{3,2,1,0:T(8,128)(2,1)} %param.8) | copy-start | bytes 9437188
where the time goes:
time: 265 us
  blocking collectives  191 us (72%)
  local copies, waits for them, and re-layouts  31.3 us (12%)
  matrix products  30.3 us (11%)
  other arithmetic  11.6 us (4%)
    all_to_all x1, blocking collectives, on_device(): lax.all_to_all(arranged, ('clip', 'patch'), split_axis=0, concat_axis=0,...  191 us
    dot_general x9, matrix products, encode(): summed = summed + jnp.matmul(table, term, precision=lax.Precision.HIGHEST)  12.9 us
    transpose x1, local copies, waits for them, and re-layouts, on_device(): arrived = jnp.transpose(arrived, (1, 0, 2, 3, 4, 5))  8.73 us
    transpose x1, local copies, waits for them, and re-layouts, on_device(): jnp.transpose(arranged, (0, 3, 1, 2, 4, 5))  8.05 us
    reduce_sum x4, other arithmetic, group_norm(): spread = group_fold(jnp.mean(centred * centred, axis=(1, 2)))  6.95 us

commit v1 on v0

v1 whole, which is shorter than its diff:
```python
import functools

import jax
import jax.numpy as jnp
import ml_dtypes
import numpy as np
from jax import lax
from jax.experimental import pallas as pl
from jax.experimental.pallas import tpu as pltpu
from jax.sharding import PartitionSpec as P

GRID = 8
GROUPS = 32
CAP = 2
TILE = 16
PARTS = 3
CHUNKS = 2
NAMES = 2 * PARTS * GROUPS
F32, BF16 = jnp.float32, jnp.bfloat16


def spread_table(latent, chunk):
    table = np.zeros((3, chunk, latent, 2 * latent, chunk), np.float32)
    places = np.arange(chunk)
    for tap in range(3):
        for step in range(latent):
            if 2 * step - 1 + tap >= 0:
                table[tap, places, step, 2 * step - 1 + tap, places] = 1
    return table.reshape(3 * chunk * latent, 2 * latent * chunk)


def swap_table(latent, share):
    table = np.zeros((latent, share, share, latent), np.float32)
    for step in range(latent):
        table[step, np.arange(share), np.arange(share), step] = 1
    return table.reshape(latent * share, latent * share)


def fold_table(channels, lanes):
    width = channels // GROUPS
    group = np.arange(lanes) // width
    return (group[:, None] == group[None, :]).astype(np.float32) / width


def pick_table(channels):
    table = np.zeros((channels, 256), np.float32)
    lanes = np.arange(NAMES)
    table[lanes % GROUPS * (channels // GROUPS), lanes] = 1
    return table


def place_table(channels):
    table = np.zeros((256, 2, channels), np.float32)
    lanes = np.arange(NAMES)
    of_group = lanes[:, None] % GROUPS == np.arange(channels)[None, :] // (channels // GROUPS)
    for which in range(2):
        mine = lanes // (PARTS * GROUPS) == which
        table[:NAMES, which] = of_group & mine[:, None]
    return table.reshape(256, 2 * channels)


def stacked(tables):
    rows = [np.pad(t, ((0, 0), (0, 256 - t.shape[1]))) for t in tables]
    starts = np.cumsum([0] + [r.shape[0] for r in rows])
    return np.concatenate(rows).astype(ml_dtypes.bfloat16), [int(s) for s in starts]


def split(row):
    parts = []
    for _ in range(PARTS):
        head = row.astype(BF16)
        parts.append(head)
        row = row - head.astype(F32)
    return parts


def fold(row, table):
    lanes = table.shape[0]
    halves = row.shape[1] // lanes
    parts = [part.astype(F32) for part in split(row)]
    rows = [part[:, h * lanes : (h + 1) * lanes] for h in range(halves) for part in parts]
    rows.append(jnp.zeros((TILE - len(rows), lanes), F32))
    out = jnp.dot(jnp.concatenate(rows, axis=0).astype(BF16), table, preferred_element_type=F32)
    sums = [jnp.sum(out[PARTS * h : PARTS * (h + 1)], axis=0, keepdims=True) for h in range(halves)]
    return jnp.concatenate(sums, axis=1)


def centre(values, table):
    share = 1.0 / values.shape[0]
    average = fold(jnp.sum(values, axis=0, keepdims=True) * share, table)
    centred = values - average
    power = fold(jnp.sum(centred * centred, axis=0, keepdims=True) * share, table)
    return average, centred, lax.rsqrt(power + 1e-05)


def silu(v):
    half = 0.5 * v
    return half + half * jnp.tanh(half)


def encode_kernel(named, x, w1, g1, w2, g2, w3, tables, *rest, starts, shares, owned):
    sends, (wide, act) = rest[:shares], rest[shares:]
    _, frames, places, breadth = x.shape
    latent = frames // 2
    c1, c2 = w1.shape[1], w2.shape[2]
    line = GRID * latent
    share = places * latent // shares
    spread = tables[starts[0] : starts[1]]
    swap = tables[starts[1] : starts[2], 0:share]
    fold1 = tables[starts[2] : starts[3], 0:c1]
    fold2 = tables[starts[3] : starts[4], 0:c2]
    fold3 = tables[starts[4] : starts[5]]
    pick = tables[starts[5] : starts[6]]
    chunk = spread.shape[1] // frames
    clip = pl.program_id(0)
    clips = pl.num_programs(0)

    @pl.when(clip == 0)
    def _():
        wide[0:line, :] = jnp.zeros((line, wide.shape[1]), BF16)
        wide[(GRID + 1) * line :, :] = jnp.zeros((line, wide.shape[1]), BF16)

    first = jnp.dot(x[0].reshape(frames * places, breadth), w1[...], preferred_element_type=F32)
    _, centred, scale = centre(first, fold1)
    act1 = silu(centred * (scale * g1[...])).astype(BF16).reshape(frames, places, c1)
    for q in range(places // chunk):
        block = act1[:, q * chunk : (q + 1) * chunk].reshape(frames * chunk, c1)
        taps = jnp.dot(spread, block, preferred_element_type=F32)
        taps = taps.reshape(3, chunk // GRID, GRID, latent, c1)
        edge = jnp.zeros((chunk // GRID, 1, latent, c1), F32)
        at = line + q * chunk * latent
        for a in range(3):
            for j in range(3):
                tap = taps[a]
                if j == 0:
                    tap = jnp.concatenate([edge, tap[:, : GRID - 1]], axis=1)
                if j == 2:
                    tap = jnp.concatenate([tap[:, 1:], edge], axis=1)
                tap = tap.reshape(chunk * latent, c1).astype(BF16)
                wide[at : at + chunk * latent, (3 * j + a) * c1 : (3 * j + a + 1) * c1] = tap
    rows = places * latent
    second = jnp.dot(wide[0:rows], w2[0], preferred_element_type=F32)
    for i in (1, 2):
        second += jnp.dot(wide[i * line : i * line + rows], w2[i], preferred_element_type=F32)
    _, centred, scale = centre(second, fold2)
    act2 = silu(centred * (scale * g2[...])).astype(BF16)
    act[...] = act2
    third = jnp.dot(act2, w3[...], preferred_element_type=F32)
    average, _, scale = centre(third, fold3)
    parts = [part.astype(F32) for part in split(average) + split(scale)]
    parts.append(jnp.zeros((TILE - len(parts), third.shape[1]), F32))
    picked = jnp.dot(jnp.concatenate(parts, axis=0).astype(BF16), pick, preferred_element_type=F32)
    lane = lax.broadcasted_iota(jnp.int32, (1, 256), 1)
    note = jnp.zeros((1, 256), F32)
    for k in range(2 * PARTS):
        note = jnp.where(lane // GROUPS == k, picked[k : k + 1], note)
    for k in range(owned):
        note = jnp.where(lane == NAMES + k, named[1 + k].astype(F32), note)
    row = lax.broadcasted_iota(jnp.int32, (TILE, 256), 0)
    body = sends[0].shape[0] - TILE
    for j in range(shares):
        q = named[0] ^ j
        part = act[pl.ds(pl.multiple_of(q * share, share), share), :]
        part = jnp.dot(swap, part, preferred_element_type=F32).astype(BF16)
        sends[j][pl.ds(pl.multiple_of(clip * share, share), share), :] = part

        @pl.when(clip == 0)
        def _():
            sends[j][body : body + TILE, :] = jnp.where(row == 0, note, 0.0).astype(BF16)

        @pl.when(clip > 0)
        def _():
            held = sends[j][body : body + TILE, :].astype(F32)
            sends[j][body : body + TILE, :] = jnp.where(row == clip, note, held).astype(BF16)


def encode(named, pixels, weights, start, count, shares):
    w1, g1, w2, g2, w3 = weights
    owned, frames, places, breadth = pixels.shape
    latent = frames // 2
    c1, c2, c3 = w1.shape[1], w2.shape[2], w3.shape[1]
    share = latent * places // shares
    tables, starts = stacked([
        spread_table(latent, 2 * GRID),
        swap_table(latent, places // shares),
        fold_table(c1, c1),
        fold_table(c2, c2),
        fold_table(c3, 256),
        pick_table(c3),
    ])
    operands = [w1, g1.reshape(1, c1), w2.reshape(3, 3 * w2.shape[1], c2), g2.reshape(1, c2), w3]
    operands.append(jnp.asarray(tables))
    whole = [pl.BlockSpec(o.shape, lambda i, s, n=o.ndim: (0,) * n) for o in operands]
    body = count * share + TILE
    flops = 2 * frames * places * breadth * c1 + 2 * latent * places * (27 * c1 * c2 + c2 * c3)
    return pl.pallas_call(
        functools.partial(encode_kernel, starts=starts, shares=shares, owned=owned),
        grid_spec=pltpu.PrefetchScalarGridSpec(
            num_scalar_prefetch=1,
            grid=(count,),
            in_specs=[pl.BlockSpec((1, frames, places, breadth), lambda i, s: (start + i, 0, 0, 0))] + whole,
            out_specs=[pl.BlockSpec((body, c2), lambda i, s: (0, 0))] * shares,
            scratch_shapes=[
                pltpu.VMEM(((GRID + 2) * GRID * latent, 9 * c1), BF16),
                pltpu.VMEM((places * latent, c2), BF16),
            ],
        ),
        out_shape=[jax.ShapeDtypeStruct((body, c2), BF16)] * shares,
        compiler_params=pltpu.CompilerParams(vmem_limit_bytes=40 * 1024 * 1024),
        cost_estimate=pl.CostEstimate(
            flops=count * flops, bytes_accessed=count * frames * places * breadth * 2, transcendentals=0
        ),
        name="encode",
    )(named, pixels, *operands)


def pack_kernel(table, sel, *rest, shares, per, share):
    half = sel.shape[0]
    held = [rest[g * shares : (g + 1) * shares] for g in range(CHUNKS)]
    outs = rest[CHUNKS * shares : CHUNKS * shares + half]
    notes, ready, note_sem, block_sem, out_sem = rest[CHUNKS * shares + half :]
    waits = []
    for g in range(CHUNKS):
        for j in range(shares):
            k = g * shares + j
            copy = pltpu.make_async_copy(
                held[g][j].at[pl.ds(per * share, TILE)], notes.at[pl.ds(k * TILE, TILE)], note_sem.at[k]
            )
            copy.start()
            waits.append(copy)
    blocks = []
    for s in range(half):
        for j in range(shares):
            for r in range(CAP):
                k = (s * shares + j) * CAP + r
                clip = table[1 + k]
                to = pl.multiple_of(((table[0] ^ j) * CAP + r) * share, share)
                for g in range(CHUNKS):

                    @pl.when(clip // per == g)
                    def _():
                        at = pl.multiple_of((clip - g * per) * share, share)
                        pltpu.make_async_copy(
                            held[g][j].at[pl.ds(at, share)], outs[s].at[pl.ds(to, share)], block_sem.at[k]
                        ).start()

                blocks.append(
                    pltpu.make_async_copy(
                        held[0][j].at[pl.ds(0, share)], outs[s].at[pl.ds(to, share)], block_sem.at[k]
                    )
                )
    for copy in waits:
        copy.wait()
    tail = shares * CAP * share
    for s in range(half):
        ready[s] = jnp.dot(sel[s], notes[...], preferred_element_type=F32).astype(BF16)
        copy = pltpu.make_async_copy(ready.at[s], outs[s].at[pl.ds(tail, TILE)], out_sem.at[s])
        copy.start()
        blocks.append(copy)
    for copy in blocks:
        copy.wait()


def pack(me, node, half, held, per, share):
    shares = len(held[0])
    body, channels = held[0][0].shape
    owned = CHUNKS * per
    names = jnp.stack([h[body - TILE, NAMES : NAMES + owned] for h in held[0]]).astype(jnp.int32)
    order = jnp.arange(owned, dtype=jnp.int32)
    same = names[:, :, None] == names[:, None, :]
    ranks = jnp.sum((same & (order[:, None] > order[None, :])).astype(jnp.int32), axis=2)
    tokenizer = node ^ jnp.arange(half, dtype=jnp.int32)
    hit = (names[None, :, None, :] == tokenizer[:, None, None, None]) & (
        ranks[None, :, None, :] == jnp.arange(CAP, dtype=jnp.int32)[None, None, :, None]
    )
    clip = jnp.sum(jnp.where(hit, order, 0), axis=3)
    table = jnp.concatenate([me.reshape(1), clip.reshape(-1)]).astype(jnp.int32)
    owner = jnp.arange(shares, dtype=jnp.int32)
    is_owner = owner[:, None] == (me ^ owner)[None, :]
    sel = hit[:, None] & is_owner[None, :, :, None, None]
    sel = sel.transpose(0, 1, 3, 2, 4).reshape(half, shares * CAP, shares, CHUNKS, per)
    sel = sel.transpose(0, 1, 3, 2, 4)
    sel = jnp.pad(sel, ((0, 0), (0, TILE - shares * CAP), (0, 0), (0, 0), (0, TILE - per)))
    sel = sel.reshape(half, TILE, CHUNKS * shares * TILE).astype(BF16)
    out_rows = shares * CAP * share + TILE
    anywhere = pl.BlockSpec(memory_space=pl.ANY)
    copies = half * shares * CAP
    return pl.pallas_call(
        functools.partial(pack_kernel, shares=shares, per=per, share=share),
        grid_spec=pltpu.PrefetchScalarGridSpec(
            num_scalar_prefetch=1,
            grid=(1,),
            in_specs=[pl.BlockSpec(sel.shape, lambda i, s: (0, 0, 0))] + [anywhere] * (CHUNKS * shares),
            out_specs=[anywhere] * half,
            scratch_shapes=[
                pltpu.VMEM((CHUNKS * shares * TILE, channels), BF16),
                pltpu.VMEM((half, TILE, channels), BF16),
                pltpu.SemaphoreType.DMA((CHUNKS * shares,)),
                pltpu.SemaphoreType.DMA((copies,)),
                pltpu.SemaphoreType.DMA((half,)),
            ],
        ),
        out_shape=[jax.ShapeDtypeStruct((out_rows, channels), BF16)] * half,
        compiler_params=pltpu.CompilerParams(vmem_limit_bytes=8 * 1024 * 1024),
        cost_estimate=pl.CostEstimate(flops=0, bytes_accessed=4 * copies * share * channels, transcendentals=0),
        name="pack",
    )(table, sel, *[h for chunk in held for h in chunk])


def finish_kernel(columns, w3, g3, place, *rest, count):
    taken, noted = rest[:count], rest[count : 2 * count]
    out, (mean, gain) = rest[-3], rest[-2:]
    k, p = pl.program_id(0), pl.program_id(1)
    c3 = w3.shape[1]
    _, _, cap, latent, share, _ = out.shape
    rows = latent * share
    for i in range(count):

        @pl.when(k == i)
        def _():
            @pl.when(p == 0)
            def _():
                wide = jnp.dot(noted[i][...], place[...], preferred_element_type=F32)
                mean[...] = wide[:, :c3]
                gain[...] = wide[:, c3:] * g3[...]

            third = jnp.dot(taken[i][...], w3[...], preferred_element_type=F32)
            for r in range(cap):
                at = pl.ds(p * cap + r, 1)
                token = (third[r * rows : (r + 1) * rows] - mean[at, :]) * gain[at, :]
                out[0, 0, r] = token.reshape(latent, share, c3).astype(BF16)


def finish(columns, arrays, w3, g3, shape, before=None):
    count = len(arrays)
    shares, _, cap, latent, share, c3 = shape
    rows = latent * share
    c2 = w3.shape[0]
    place = jnp.asarray(place_table(c3).astype(ml_dtypes.bfloat16))

    def block(i):
        return lambda k, p, s: (jnp.where(k == i, p, jnp.where(k < i, 0, shares - 1)), 0)

    last = shares * cap * rows // TILE
    specs = [pl.BlockSpec(o.shape, lambda k, p, s: (0, 0)) for o in (w3, g3, place)]
    specs += [pl.BlockSpec((cap * rows, c2), block(i)) for i in range(count)]
    specs += [pl.BlockSpec((TILE, c2), lambda k, p, s: (last, 0)) for i in range(count)]
    operands = [w3, g3, place, *arrays, *arrays]
    aliases = {}
    if before is not None:
        specs.append(pl.BlockSpec(memory_space=pl.ANY))
        aliases = {1 + len(operands): 0}
        operands.append(before)
    return pl.pallas_call(
        functools.partial(finish_kernel, count=count),
        grid_spec=pltpu.PrefetchScalarGridSpec(
            num_scalar_prefetch=1,
            grid=(count, shares),
            in_specs=specs,
            out_specs=pl.BlockSpec((1, 1, cap, latent, share, c3), lambda k, p, s: (p, s[k], 0, 0, 0, 0)),
            scratch_shapes=[pltpu.VMEM((TILE, c3), F32), pltpu.VMEM((TILE, c3), F32)],
        ),
        out_shape=jax.ShapeDtypeStruct(shape, BF16),
        input_output_aliases=aliases,
        compiler_params=pltpu.CompilerParams(vmem_limit_bytes=24 * 1024 * 1024),
        cost_estimate=pl.CostEstimate(
            flops=2 * count * shares * cap * rows * c2 * c3,
            bytes_accessed=count * shares * cap * rows * (c2 + c3) * 2,
            transcendentals=0,
        ),
        name="finish",
    )(columns, *operands)


def on_device(pixels, destination, embed_weight, embed_gain, mixing_weight, mixing_gain, project_weight, project_gain):
    nodes, shares = lax.axis_size("clip"), lax.axis_size("patch")
    node, me = lax.axis_index("clip").astype(jnp.int32), lax.axis_index("patch").astype(jnp.int32)
    half = nodes // 2
    owned, frames, places, _ = pixels.shape
    latent, c3 = frames // 2, project_weight.shape[1]
    per = owned // CHUNKS
    share = latent * places // shares
    weights = (embed_weight, embed_gain, mixing_weight, mixing_gain, project_weight)
    named = jnp.concatenate([me.reshape(1), destination[:, 0].astype(jnp.int32)])

    def to_share(array, j):
        if j == 0:
            return array
        return lax.ppermute(array, "patch", [(p, p ^ j) for p in range(shares)])

    def to_node(array, s):
        if s == 0:
            return array
        return lax.ppermute(array, "clip", [(c, c ^ s) for c in range(nodes)])

    def across(array, j):
        pairs = [(c * shares + p, (c ^ half) * shares + (p ^ j)) for c in range(nodes) for p in range(shares)]
        return lax.ppermute(array, ("clip", "patch"), pairs)

    near, far = [], []
    for g in range(CHUNKS):
        sends = encode(named, pixels, weights, g * per, per, shares)
        far.append([across(sends[j], j) for j in range(shares)])
        near.append([to_share(sends[j], j) for j in range(shares)])
    own = pack(me, node, half, near, per, share)
    own = [to_node(own[s], s) for s in range(half)]
    other = pack(me, node, half, far, per, share)
    other = [to_node(other[s], s) for s in range(half)]

    w3, g3 = project_weight, project_gain.reshape(1, c3)
    shape = (shares, nodes, CAP, latent, places // shares, c3)
    early = jnp.stack([node ^ s for s in range(half)] + [node ^ half])
    late = jnp.stack([node ^ half ^ s for s in range(1, half)])
    latents = finish(early, own + other[:1], w3, g3, shape)
    latents = finish(late, other[1:], w3, g3, shape, latents)
    return latents.reshape(shares * nodes * CAP, latent, places // shares, c3)


def solution(mesh):
    return jax.shard_map(
        on_device,
        mesh=mesh,
        in_specs=(
            P(("clip", "patch"), None, None, None),
            P(("clip", "patch"), None),
            P(),
            P(),
            P(),
            P(),
            P(),
            P(),
        ),
        out_specs=P("clip", None, "patch", None),
        check_vma=False,
    )
```

time: 265 us -> 144 us (0.54)
  blocking collectives: 191 us -> 0 us
  Pallas kernels: 0 us -> 48.2 us
  waiting for transfers between devices: 0 us -> 45.6 us
  matrix products: 30.3 us -> 0 us
  starting transfers between devices: 0 us -> 25.2 us
  local copies, waits for them, and re-layouts: 31.3 us -> 21.5 us
  other arithmetic: 11.6 us -> 2.74 us
    all_to_all x1 -> x0, blocking collectives: 191 us -> none  [on_device(): lax.all_to_all(arranged, ('clip', 'patch'), split_axis=0, concat_axis=0,...]
    pallas_call x0 -> x6, Pallas kernels: none -> 48.2 us  [the longest x2 21.7 us: encode(): pl.pallas_call(functools.partial(encode_kernel, starts=starts, shares=sha...]
    ppermute x0 -> x20, waiting for transfers between devices: none -> 45.6 us  [the longest x8 23.2 us: across(): return lax.ppermute(array, ('clip', 'patch'), pairs)]
    dot_general x38 -> x0, matrix products: 30.3 us -> none  [the longest x9 12.9 us: encode(): summed = summed + jnp.matmul(table, term, precision=lax.Precision.HIGHEST)]
    ppermute x0 -> x20, starting transfers between devices: none -> 25.2 us  [the longest x8 13.2 us: across(): return lax.ppermute(array, ('clip', 'patch'), pairs)]
    transpose x2 -> x0, local copies, waits for them, and re-layouts: 16.8 us -> none  [the longest x1 8.73 us: on_device(): arrived = jnp.transpose(arrived, (1, 0, 2, 3, 4, 5))]
    unnamed x20 -> x44, local copies, waits for them, and re-layouts: 2.9 us -> 15.9 us
    reduce_sum x12 -> x3, other arithmetic: 7.9 us -> 0.73 us  [the longest x2 0.45 us: pack(): clip = jnp.sum(jnp.where(hit, order, 0), axis=3)]
  transfers between devices with their start and end apart: 0 -> 20, of which waited for: 0 -> 6; matrix products, arithmetic and copies ran while one was open for 0% -> 5% of each run, Pallas kernels for 0% -> 18%
where the time goes in v1:
time: 144 us; the launch traced here: 143 us
  Pallas kernels  48.2 us (33%)
  waiting for transfers between devices  45.6 us (32%)
  starting transfers between devices  25.2 us (18%)
  local copies, waits for them, and re-layouts  21.5 us (15%)
  other arithmetic  2.74 us (2%)
    ppermute x8, waiting for transfers between devices, across(): return lax.ppermute(array, ('clip', 'patch'), pairs)  23.2 us
    ppermute x6, waiting for transfers between devices, to_node(): return lax.ppermute(array, 'clip', [(c, c ^ s) for c in range(nodes)])  22.3 us
    pallas_call x2, Pallas kernels, encode(): pl.pallas_call(functools.partial(encode_kernel, starts=starts, shares=sha...  21.7 us
    pallas_call x2, Pallas kernels, finish(): pl.pallas_call(functools.partial(finish_kernel, count=count), grid_spec=p...  20.5 us
    unnamed x44, local copies, waits for them, and re-layouts  15.9 us
    ppermute x8, starting transfers between devices, across(): return lax.ppermute(array, ('clip', 'patch'), pairs)  13.2 us
    ppermute x6, starting transfers between devices, to_node(): return lax.ppermute(array, 'clip', [(c, c ^ s) for c in range(nodes)])  7.1 us
    pallas_call x2, Pallas kernels, pack(): pl.pallas_call(functools.partial(pack_kernel, shares=shares, per=per, sha...  5.97 us
  transfers between devices with their start and end apart: 20, of which 6 were waited for; matrix products, arithmetic and copies ran while one was open for 5% of the time, Pallas kernels for 18%

profile of v1, /device:TPU:0, one launch (start us, length us, event | category | flops | bytes accessed | tf_op | source)
XLA Modules:
  0.0 143.3 jit_solution(351468913090280009)
XLA Ops:
  0.0 0.7 pad_add_fusion.1.named
  0.7 0.9 copy-done.2
  1.7 1.9 %copy-done.15 = bf16[4,16,64,384]{3,2,1,0:T(8,128)(2,1)S(1)} copy-done((bf16[4,16,64,384]{3,2,1,0:T(8,128)(2,1)S(1)}, bf16[4,16,64,384]{3,2,1,0:T(8,128)(2,1)}, u32[]{:S(2)}) %copy-start.15) | copy-done | bytes 3145752
  3.6 1.5 %copy-done.16 = bf16[9,384,256]{2,1,0:T(8,128)(2,1)S(1)} copy-done((bf16[9,384,256]{2,1,0:T(8,128)(2,1)S(1)}, bf16[9,384,256]{2,1,0:T(8,128)(2,1)}, u32[]{:S(2)}) %copy-start.16) | copy-done | bytes 1769496
  5.0 0.9 copy-done.17
  5.9 0.7 copy-done.18
  6.6 0.7 copy-done.19
  7.3 1.2 copy-done.20
  8.4 10.5 %encode.2 = (bf16[272,256]{1,0:T(8,128)(2,1)S(1)}, bf16[272,256]{1,0:T(8,128)(2,1)S(1)}, bf16[272,256]{1,0:T(8,128)(2,1)S(1)}, bf16[272,256]{1,0:T(8,128)(2,1)S(1)}) custom-call(s32[5]{0:T(128)S(1)} %pad_add_fusion.1.named, bf16[4,16,64,384]{3,2,1,0:T(8,128)(2,1)S(1)} %copy-done.15, bf16[384,128]{1,0:T(8,128)(2,1)S(1)} %copy-done.17, f32[1,128]{1,0:T(1,128)S(1)} %bitcast.29, ...), custom_call_target="tpu_custom_call" | custom-call | flops 2281701376 | bytes 1572864 | tf_op jit(solution)/shard_map/encode/pallas_call | solution.py:196
  19.0 0.5 collective-permute-start.11
  19.5 3.7 %collective-permute-start.1 = (bf16[272,256]{1,0:T(8,128)(2,1)S(1)}, bf16[272,256]{1,0:T(8,128)(2,1)S(1)}, u32[]{:S(2)}, u32[]{:S(2)}) collective-permute-start(bf16[272,256]{1,0:T(8,128)(2,1)S(1)} %get-tuple-element.22), channel_id=1, source_target_pairs={{0,17},{1,16},{2,19},{3,18},{4,21},{5,20},{6,23},{7,22},{8,25},{9,... | collective-permute-start | bytes 417800 | tf_op jit(solution)/shard_map/ppermute | solution.py:398
  23.2 1.5 %collective-permute-start.12 = (bf16[272,256]{1,0:T(8,128)(2,1)S(1)}, bf16[272,256]{1,0:T(8,128)(2,1)S(1)}, u32[]{:S(2)}, u32[]{:S(2)}) collective-permute-start(bf16[272,256]{1,0:T(8,128)(2,1)S(1)} %get-tuple-element.23), channel_id=1, source_target_pairs={{0,2},{1,3},{2,0},{3,1},{4,6},{5,7},{6,4},{7,5},{8,10},{9,11},{10,... | collective-permute-start | bytes 417800 | tf_op jit(solution)/shard_map/ppermute | solution.py:389
  24.7 0.9 collective-permute-start.13
  25.7 11.2 %encode.3 = (bf16[272,256]{1,0:T(8,128)(2,1)S(1)}, bf16[272,256]{1,0:T(8,128)(2,1)S(1)}, bf16[272,256]{1,0:T(8,128)(2,1)}, bf16[272,256]{1,0:T(8,128)(2,1)S(1)}) custom-call(s32[5]{0:T(128)S(1)} %pad_add_fusion.1.named, bf16[4,16,64,384]{3,2,1,0:T(8,128)(2,1)S(1)} %copy-done.15, bf16[384,128]{1,0:T(8,128)(2,1)S(1)} %copy-done.17, f32[1,128]{1,0:T(1,128)S(1)} %bitcast.30, ...), custom_call_target="tpu_custom_call" | custom-call | flops 2281701376 | bytes 1572864 | tf_op jit(solution)/shard_map/encode/pallas_call | solution.py:196
  36.9 3.1 %collective-permute-start.3 = (bf16[272,256]{1,0:T(8,128)(2,1)S(1)}, bf16[272,256]{1,0:T(8,128)(2,1)S(1)}, u32[]{:S(2)}, u32[]{:S(2)}) collective-permute-start(bf16[272,256]{1,0:T(8,128)(2,1)S(1)} %get-tuple-element.24), channel_id=1, source_target_pairs={{0,19},{1,18},{2,17},{3,16},{4,23},{5,22},{6,21},{7,20},{8,27},{9,... | collective-permute-start | bytes 417800 | tf_op jit(solution)/shard_map/ppermute | solution.py:398
  40.8 1.7 %collective-permute-start.15 = (bf16[272,256]{1,0:T(8,128)(2,1)}, bf16[272,256]{1,0:T(8,128)(2,1)S(1)}, u32[]{:S(2)}, u32[]{:S(2)}) collective-permute-start(bf16[272,256]{1,0:T(8,128)(2,1)} %get-tuple-element.27), channel_id=1, source_target_pairs={{0,2},{1,3},{2,0},{3,1},{4,6},{5,7},{6,4},{7,5},{8,10},{9,11},{10,... | collective-permute-start | bytes 417800 | tf_op jit(solution)/shard_map/ppermute | solution.py:389
  42.7 6.9 %collective-permute-done.3.rest_3_ = bf16[272,256]{1,0:T(8,128)(2,1)S(1)} collective-permute-done((bf16[272,256]{1,0:T(8,128)(2,1)S(1)}, bf16[272,256]{1,0:T(8,128)(2,1)S(1)}, u32[]{:S(2)}, u32[]{:S(2)}) %collective-permute-start.3) | collective-permute-done | bytes 139296 | tf_op jit(solution)/shard_map/ppermute | solution.py:398
  49.7 3.6 %collective-permute-done.rest_0_ = bf16[272,256]{1,0:T(8,128)(2,1)S(1)} collective-permute-done((bf16[272,256]{1,0:T(8,128)(2,1)S(1)}, bf16[272,256]{1,0:T(8,128)(2,1)S(1)}, u32[]{:S(2)}, u32[]{:S(2)}) %collective-permute-start) | collective-permute-done | bytes 139296 | tf_op jit(solution)/shard_map/ppermute | solution.py:398
  53.4 0.3 convert_reduce_fusion
  54.3 0.5 copy.41
  54.8 0.5 copy.36
  55.5 0.7 pad_convert_fusion
  56.9 3.0 %pack.3 = (bf16[1040,256]{1,0:T(8,128)(2,1)S(1)}, bf16[1040,256]{1,0:T(8,128)(2,1)}, bf16[1040,256]{1,0:T(8,128)(2,1)}, bf16[1040,256]{1,0:T(8,128)(2,1)}) custom-call(s32[33]{0:T(128)S(1)} %pad_add_fusion.3.table, bf16[4,16,128]{2,1,0:T(8,128)(2,1)S(1)} %reshape.294.sel, bf16[272,256]{1,0:T(8,128)(2,1)S(1)} %get-tuple-element.21.rest_0_, ...), custom_call_target="tpu_custom_call" | custom-call | bytes 4194304 | tf_op jit(solution)/shard_map/pack/pallas_call | solution.py:288
  59.9 1.6 %collective-permute-start.17 = (bf16[1040,256]{1,0:T(8,128)(2,1)}, bf16[1040,256]{1,0:T(8,128)(2,1)S(1)}, u32[]{:S(2)}, u32[]{:S(2)}) collective-permute-start(bf16[1040,256]{1,0:T(8,128)(2,1)} %get-tuple-element.33), channel_id=1, source_target_pairs={{0,4},{4,0},{8,12},{12,8},{16,20},{20,16},{24,28},{28,24},{1,5},{5... | collective-permute-start | bytes 1597448 | tf_op jit(solution)/shard_map/ppermute | solution.py:394
  61.4 1.5 %collective-permute-start.5 = (bf16[272,256]{1,0:T(8,128)(2,1)S(1)}, bf16[272,256]{1,0:T(8,128)(2,1)S(1)}, u32[]{:S(2)}, u32[]{:S(2)}) collective-permute-start(bf16[272,256]{1,0:T(8,128)(2,1)S(1)} %get-tuple-element.26), channel_id=1, source_target_pairs={{0,17},{1,16},{2,19},{3,18},{4,21},{5,20},{6,23},{7,22},{8,25},{9,... | collective-permute-start | bytes 417800 | tf_op jit(solution)/shard_map/ppermute | solution.py:398
  63.0 1.7 %collective-permute-start.6 = (bf16[272,256]{1,0:T(8,128)(2,1)}, bf16[272,256]{1,0:T(8,128)(2,1)S(1)}, u32[]{:S(2)}, u32[]{:S(2)}) collective-permute-start(bf16[272,256]{1,0:T(8,128)(2,1)} %get-tuple-element.27), channel_id=1, source_target_pairs={{0,18},{1,19},{2,16},{3,17},{4,22},{5,23},{6,20},{7,21},{8,26},{9,... | collective-permute-start | bytes 417800 | tf_op jit(solution)/shard_map/ppermute | solution.py:398
  64.6 3.0 %collective-permute-start.7 = (bf16[272,256]{1,0:T(8,128)(2,1)S(1)}, bf16[272,256]{1,0:T(8,128)(2,1)S(1)}, u32[]{:S(2)}, u32[]{:S(2)}) collective-permute-start(bf16[272,256]{1,0:T(8,128)(2,1)S(1)} %get-tuple-element.28), channel_id=1, source_target_pairs={{0,19},{1,18},{2,17},{3,16},{4,23},{5,22},{6,21},{7,20},{8,27},{9,... | collective-permute-start | bytes 417800 | tf_op jit(solution)/shard_map/ppermute | solution.py:398
  67.6 12.7 %collective-permute-done.4.rest_4_ = bf16[272,256]{1,0:T(8,128)(2,1)S(1)} collective-permute-done((bf16[272,256]{1,0:T(8,128)(2,1)S(1)}, bf16[272,256]{1,0:T(8,128)(2,1)S(1)}, u32[]{:S(2)}, u32[]{:S(2)}) %collective-permute-start.4) | collective-permute-done | bytes 139296 | tf_op jit(solution)/shard_map/ppermute | solution.py:398
  80.3 0.7 copy-done.6
  81.0 0.6 copy-done.8
  81.7 2.0 %collective-permute-start.19 = (bf16[1040,256]{1,0:T(8,128)(2,1)}, bf16[1040,256]{1,0:T(8,128)(2,1)S(1)}, u32[]{:S(2)}, u32[]{:S(2)}) collective-permute-start(bf16[1040,256]{1,0:T(8,128)(2,1)} %get-tuple-element.35), channel_id=1, source_target_pairs={{0,12},{4,8},{8,4},{12,0},{16,28},{20,24},{24,20},{28,16},{1,13},{... | collective-permute-start | bytes 1597448 | tf_op jit(solution)/shard_map/ppermute | solution.py:394
  84.1 1.6 %copy.37 = bf16[4,16,2,4,16]{4,3,2,1,0:T(4,128)(2,1)} copy(bf16[4,16,2,4,16]{4,1,3,2,0:T(8,128)(2,1)} %get-tuple-element.46) | data formatting | bytes 32768 | tf_op jit(solution)/shard_map/convert_element_type | solution.py:284
  85.7 1.0 reshape.293.sel
  86.8 0.7 copy-done.10
  87.5 0.6 copy-done.12
  88.1 0.9 copy-done.5
  89.1 0.9 copy-done.7
  90.0 0.9 copy-done.9
  90.9 0.9 copy-done.11
  91.8 0.9 copy-done.13
  92.7 3.0 %pack.2 = (bf16[1040,256]{1,0:T(8,128)(2,1)S(1)}, bf16[1040,256]{1,0:T(8,128)(2,1)}, bf16[1040,256]{1,0:T(8,128)(2,1)}, bf16[1040,256]{1,0:T(8,128)(2,1)}) custom-call(s32[33]{0:T(128)S(1)} %pad_add_fusion.2.table, bf16[4,16,128]{2,1,0:T(8,128)(2,1)S(1)} %reshape.293.sel, bf16[272,256]{1,0:T(8,128)(2,1)S(1)} %copy-done.5, ...), custom_call_target="tpu_custom_call" | custom-call | bytes 4194304 | tf_op jit(solution)/shard_map/pack/pallas_call | solution.py:288
  95.7 1.6 %collective-permute-start.8 = (bf16[1040,256]{1,0:T(8,128)(2,1)}, bf16[1040,256]{1,0:T(8,128)(2,1)S(1)}, u32[]{:S(2)}, u32[]{:S(2)}) collective-permute-start(bf16[1040,256]{1,0:T(8,128)(2,1)} %get-tuple-element.29), channel_id=1, source_target_pairs={{0,4},{4,0},{8,12},{12,8},{16,20},{20,16},{24,28},{28,24},{1,5},{5... | collective-permute-start | bytes 1597448 | tf_op jit(solution)/shard_map/ppermute | solution.py:394
  97.3 2.0 %collective-permute-start.10 = (bf16[1040,256]{1,0:T(8,128)(2,1)}, bf16[1040,256]{1,0:T(8,128)(2,1)}, u32[]{:S(2)}, u32[]{:S(2)}) collective-permute-start(bf16[1040,256]{1,0:T(8,128)(2,1)} %get-tuple-element.31), channel_id=1, source_target_pairs={{0,12},{4,8},{8,4},{12,0},{16,28},{20,24},{24,20},{28,16},{1,13},{... | collective-permute-start | bytes 1597448 | tf_op jit(solution)/shard_map/ppermute | solution.py:394
  99.6 11.6 %collective-permute-done.19.rest_3_.rest_8_ = bf16[1040,256]{1,0:T(8,128)(2,1)S(1)} collective-permute-done((bf16[1040,256]{1,0:T(8,128)(2,1)}, bf16[1040,256]{1,0:T(8,128)(2,1)S(1)}, u32[]{:S(2)}, u32[]{:S(2)}) %collective-permute-start.19) | collective-permute-done | bytes 532512 | tf_op jit(solution)/shard_map/ppermute | solution.py:394
  111.2 1.0 copy-done
  112.3 11.3 %finish.2.rest_6_ = bf16[4,8,2,8,16,512]{5,4,3,2,1,0:T(8,128)(2,1)} custom-call(s32[5]{0:T(128)S(1)} %stack.46.columns, bf16[256,512]{1,0:T(8,128)(2,1)S(1)} %copy-done.3, f32[1,512]{1,0:T(1,128)S(1)} %bitcast.23, bf16[256,1024]{1,0:T(8,128)(2,1)S(1)} %copy-done, bf16[1040,256]{1,0:T(8,128)(2,1)S(1)} %get-tuple-element.32.rest_0_.rest_5_, ...), custom_call_target="tpu_custom_call" | custom-call | flops 1342177280 | bytes 7864320 | tf_op jit(solution)/shard_map/finish/pallas_call | solution.py:354
  123.5 10.5 %collective-permute-done.10.rest_2_.rest_5_ = bf16[1040,256]{1,0:T(8,128)(2,1)} collective-permute-done((bf16[1040,256]{1,0:T(8,128)(2,1)}, bf16[1040,256]{1,0:T(8,128)(2,1)}, u32[]{:S(2)}, u32[]{:S(2)}) %collective-permute-start.10) | collective-permute-done | bytes 532512 | tf_op jit(solution)/shard_map/ppermute | solution.py:394
  134.1 9.3 %finish.3 = bf16[4,8,2,8,16,512]{5,4,3,2,1,0:T(8,128)(2,1)} custom-call(s32[3]{0:T(128)S(1)} %pad_add_fusion.columns, bf16[256,512]{1,0:T(8,128)(2,1)S(1)} %copy-done.3, f32[1,512]{1,0:T(1,128)S(1)} %bitcast.24, bf16[256,1024]{1,0:T(8,128)(2,1)S(1)} %copy-done.1, ...), custom_call_target="tpu_custom_call", output_to_operand_aliasing={{}: (10, {})} | custom-call | flops 805306368 | bytes 4718592 | tf_op jit(solution)/shard_map/finish/pallas_call | solution.py:354
  (90 shorter events, 3.6 us)
Async XLA Ops:
  0.7 0.9 copy-start.2
  1.7 1.9 %copy-start.15 = (bf16[4,16,64,384]{3,2,1,0:T(8,128)(2,1)S(1)}, bf16[4,16,64,384]{3,2,1,0:T(8,128)(2,1)}, u32[]{:S(2)}) copy-start(bf16[4,16,64,384]{3,2,1,0:T(8,128)(2,1)} %x.7) | copy-start | bytes 9437188
  3.6 1.5 %copy-start.16 = (bf16[9,384,256]{2,1,0:T(8,128)(2,1)S(1)}, bf16[9,384,256]{2,1,0:T(8,128)(2,1)}, u32[]{:S(2)}) copy-start(bf16[9,384,256]{2,1,0:T(8,128)(2,1)} %param.16) | copy-start | bytes 5308420
  5.0 0.9 copy-start.17
  5.9 0.7 copy-start.18
  6.6 0.7 copy-start.19
  7.3 1.2 copy-start.20
  8.4 17.3 %copy-start.21 = (bf16[1664,256]{1,0:T(8,128)(2,1)S(1)}, bf16[1664,256]{1,0:T(8,128)(2,1)}, u32[]{:S(2)}) copy-start(bf16[1664,256]{1,0:T(8,128)(2,1)} %constant.28.clone.tables) | copy-start | bytes 2555908
  8.4 102.8 %copy-start.3 = (bf16[256,512]{1,0:T(8,128)(2,1)S(1)}, bf16[256,512]{1,0:T(8,128)(2,1)}, u32[]{:S(2)}) copy-start(bf16[256,512]{1,0:T(8,128)(2,1)} %w3.7) | copy-start | bytes 786436
  8.4 102.8 %copy-start.14 = (f32[512]{0:T(512)S(1)}, f32[512]{0:T(512)}, u32[]{:S(2)}) copy-start(f32[512]{0:T(512)} %param.19) | copy-start | bytes 6148
  19.0 17.9 %collective-permute-start.11 = (bf16[272,256]{1,0:T(8,128)(2,1)S(1)}, bf16[272,256]{1,0:T(8,128)(2,1)S(1)}, u32[]{:S(2)}, u32[]{:S(2)}) collective-permute-start(bf16[272,256]{1,0:T(8,128)(2,1)S(1)} %get-tuple-element.22), channel_id=1, source_target_pairs={{0,1},{1,0},{2,3},{3,2},{4,5},{5,4},{6,7},{7,6},{8,9},{9,8},{10,11... | collective-permute-start | bytes 417800 | tf_op jit(solution)/shard_map/ppermute | solution.py:389
  19.5 20.6 %collective-permute-start.1 = (bf16[272,256]{1,0:T(8,128)(2,1)S(1)}, bf16[272,256]{1,0:T(8,128)(2,1)S(1)}, u32[]{:S(2)}, u32[]{:S(2)}) collective-permute-start(bf16[272,256]{1,0:T(8,128)(2,1)S(1)} %get-tuple-element.22), channel_id=1, source_target_pairs={{0,17},{1,16},{2,19},{3,18},{4,21},{5,20},{6,23},{7,22},{8,25},{9,... | collective-permute-start | bytes 417800 | tf_op jit(solution)/shard_map/ppermute | solution.py:398
  23.2 17.4 %collective-permute-start.12 = (bf16[272,256]{1,0:T(8,128)(2,1)S(1)}, bf16[272,256]{1,0:T(8,128)(2,1)S(1)}, u32[]{:S(2)}, u32[]{:S(2)}) collective-permute-start(bf16[272,256]{1,0:T(8,128)(2,1)S(1)} %get-tuple-element.23), channel_id=1, source_target_pairs={{0,2},{1,3},{2,0},{3,1},{4,6},{5,7},{6,4},{7,5},{8,10},{9,11},{10,... | collective-permute-start | bytes 417800 | tf_op jit(solution)/shard_map/ppermute | solution.py:389
  24.7 16.1 %collective-permute-start.2 = (bf16[272,256]{1,0:T(8,128)(2,1)S(1)}, bf16[272,256]{1,0:T(8,128)(2,1)S(1)}, u32[]{:S(2)}, u32[]{:S(2)}) collective-permute-start(bf16[272,256]{1,0:T(8,128)(2,1)S(1)} %get-tuple-element.23), channel_id=1, source_target_pairs={{0,18},{1,19},{2,16},{3,17},{4,22},{5,23},{6,20},{7,21},{8,26},{9,... | collective-permute-start | bytes 417800 | tf_op jit(solution)/shard_map/ppermute | solution.py:398
  24.7 17.8 %collective-permute-start.13 = (bf16[272,256]{1,0:T(8,128)(2,1)S(1)}, bf16[272,256]{1,0:T(8,128)(2,1)S(1)}, u32[]{:S(2)}, u32[]{:S(2)}) collective-permute-start(bf16[272,256]{1,0:T(8,128)(2,1)S(1)} %get-tuple-element.24), channel_id=1, source_target_pairs={{0,3},{1,2},{2,1},{3,0},{4,7},{5,6},{6,5},{7,4},{8,11},{9,10},{10,... | collective-permute-start | bytes 417800 | tf_op jit(solution)/shard_map/ppermute | solution.py:389
  36.9 12.7 %collective-permute-start.3 = (bf16[272,256]{1,0:T(8,128)(2,1)S(1)}, bf16[272,256]{1,0:T(8,128)(2,1)S(1)}, u32[]{:S(2)}, u32[]{:S(2)}) collective-permute-start(bf16[272,256]{1,0:T(8,128)(2,1)S(1)} %get-tuple-element.24), channel_id=1, source_target_pairs={{0,19},{1,18},{2,17},{3,16},{4,23},{5,22},{6,21},{7,20},{8,27},{9,... | collective-permute-start | bytes 417800 | tf_op jit(solution)/shard_map/ppermute | solution.py:398
  40.0 13.3 %collective-permute-start = (bf16[272,256]{1,0:T(8,128)(2,1)S(1)}, bf16[272,256]{1,0:T(8,128)(2,1)S(1)}, u32[]{:S(2)}, u32[]{:S(2)}) collective-permute-start(bf16[272,256]{1,0:T(8,128)(2,1)S(1)} %get-tuple-element.21.rest_0_), channel_id=1, source_target_pairs={{0,16},{1,17},{2,18},{3,19},{4,20},{5,21},{6,22},{7,23},{8,24},{9,... | collective-permute-start | bytes 417800 | tf_op jit(solution)/shard_map/ppermute | solution.py:398
  40.6 16.3 %collective-permute-start.14 = (bf16[272,256]{1,0:T(8,128)(2,1)S(1)}, bf16[272,256]{1,0:T(8,128)(2,1)S(1)}, u32[]{:S(2)}, u32[]{:S(2)}) collective-permute-start(bf16[272,256]{1,0:T(8,128)(2,1)S(1)} %get-tuple-element.26), channel_id=1, source_target_pairs={{0,1},{1,0},{2,3},{3,2},{4,5},{5,4},{6,7},{7,6},{8,9},{9,8},{10,11... | collective-permute-start | bytes 417800 | tf_op jit(solution)/shard_map/ppermute | solution.py:389
  40.8 16.1 %collective-permute-start.15 = (bf16[272,256]{1,0:T(8,128)(2,1)}, bf16[272,256]{1,0:T(8,128)(2,1)S(1)}, u32[]{:S(2)}, u32[]{:S(2)}) collective-permute-start(bf16[272,256]{1,0:T(8,128)(2,1)} %get-tuple-element.27), channel_id=1, source_target_pairs={{0,2},{1,3},{2,0},{3,1},{4,6},{5,7},{6,4},{7,5},{8,10},{9,11},{10,... | collective-permute-start | bytes 417800 | tf_op jit(solution)/shard_map/ppermute | solution.py:389
  42.5 14.3 %collective-permute-start.16 = (bf16[272,256]{1,0:T(8,128)(2,1)S(1)}, bf16[272,256]{1,0:T(8,128)(2,1)S(1)}, u32[]{:S(2)}, u32[]{:S(2)}) collective-permute-start(bf16[272,256]{1,0:T(8,128)(2,1)S(1)} %get-tuple-element.28), channel_id=1, source_target_pairs={{0,3},{1,2},{2,1},{3,0},{4,7},{5,6},{6,5},{7,4},{8,11},{9,10},{10,... | collective-permute-start | bytes 417800 | tf_op jit(solution)/shard_map/ppermute | solution.py:389
  53.3 3.6 %copy-start.4 = (bf16[272,256]{1,0:T(8,128)(2,1)}, bf16[272,256]{1,0:T(8,128)(2,1)S(1)}, u32[]{:S(2)}) copy-start(bf16[272,256]{1,0:T(8,128)(2,1)S(1)} %collective-permute-done.rest_0_) | copy-start | bytes 417796
  59.9 37.4 %collective-permute-start.17 = (bf16[1040,256]{1,0:T(8,128)(2,1)}, bf16[1040,256]{1,0:T(8,128)(2,1)S(1)}, u32[]{:S(2)}, u32[]{:S(2)}) collective-permute-start(bf16[1040,256]{1,0:T(8,128)(2,1)} %get-tuple-element.33), channel_id=1, source_target_pairs={{0,4},{4,0},{8,12},{12,8},{16,20},{20,16},{24,28},{28,24},{1,5},{5... | collective-permute-start | bytes 1597448 | tf_op jit(solution)/shard_map/ppermute | solution.py:394
  61.4 18.9 %collective-permute-start.4 = (bf16[272,256]{1,0:T(8,128)(2,1)S(1)}, bf16[272,256]{1,0:T(8,128)(2,1)S(1)}, u32[]{:S(2)}, u32[]{:S(2)}) collective-permute-start(bf16[272,256]{1,0:T(8,128)(2,1)S(1)} %get-tuple-element.25.rest_4_), channel_id=1, source_target_pairs={{0,16},{1,17},{2,18},{3,19},{4,20},{5,21},{6,22},{7,23},{8,24},{9,... | collective-permute-start | bytes 417800 | tf_op jit(solution)/shard_map/ppermute | solution.py:398
  61.4 19.6 %collective-permute-start.5 = (bf16[272,256]{1,0:T(8,128)(2,1)S(1)}, bf16[272,256]{1,0:T(8,128)(2,1)S(1)}, u32[]{:S(2)}, u32[]{:S(2)}) collective-permute-start(bf16[272,256]{1,0:T(8,128)(2,1)S(1)} %get-tuple-element.26), channel_id=1, source_target_pairs={{0,17},{1,16},{2,19},{3,18},{4,21},{5,20},{6,23},{7,22},{8,25},{9,... | collective-permute-start | bytes 417800 | tf_op jit(solution)/shard_map/ppermute | solution.py:398
  63.0 23.9 %collective-permute-start.6 = (bf16[272,256]{1,0:T(8,128)(2,1)}, bf16[272,256]{1,0:T(8,128)(2,1)S(1)}, u32[]{:S(2)}, u32[]{:S(2)}) collective-permute-start(bf16[272,256]{1,0:T(8,128)(2,1)} %get-tuple-element.27), channel_id=1, source_target_pairs={{0,18},{1,19},{2,16},{3,17},{4,22},{5,23},{6,20},{7,21},{8,26},{9,... | collective-permute-start | bytes 417800 | tf_op jit(solution)/shard_map/ppermute | solution.py:398
  64.6 22.8 %collective-permute-start.7 = (bf16[272,256]{1,0:T(8,128)(2,1)S(1)}, bf16[272,256]{1,0:T(8,128)(2,1)S(1)}, u32[]{:S(2)}, u32[]{:S(2)}) collective-permute-start(bf16[272,256]{1,0:T(8,128)(2,1)S(1)} %get-tuple-element.28), channel_id=1, source_target_pairs={{0,19},{1,18},{2,17},{3,16},{4,23},{5,22},{6,21},{7,20},{8,27},{9,... | collective-permute-start | bytes 417800 | tf_op jit(solution)/shard_map/ppermute | solution.py:398
  80.3 0.7 copy-start.6
  81.0 18.6 %collective-permute-start.18 = (bf16[1040,256]{1,0:T(8,128)(2,1)}, bf16[1040,256]{1,0:T(8,128)(2,1)S(1)}, u32[]{:S(2)}, u32[]{:S(2)}) collective-permute-start(bf16[1040,256]{1,0:T(8,128)(2,1)} %get-tuple-element.34), channel_id=1, source_target_pairs={{0,8},{4,12},{8,0},{12,4},{16,24},{20,28},{24,16},{28,20},{1,9},{5... | collective-permute-start | bytes 1597448 | tf_op jit(solution)/shard_map/ppermute | solution.py:394
  81.0 0.7 copy-start.8
  81.7 29.6 %collective-permute-start.19 = (bf16[1040,256]{1,0:T(8,128)(2,1)}, bf16[1040,256]{1,0:T(8,128)(2,1)S(1)}, u32[]{:S(2)}, u32[]{:S(2)}) collective-permute-start(bf16[1040,256]{1,0:T(8,128)(2,1)} %get-tuple-element.35), channel_id=1, source_target_pairs={{0,12},{4,8},{8,4},{12,0},{16,28},{20,24},{24,20},{28,16},{1,13},{... | collective-permute-start | bytes 1597448 | tf_op jit(solution)/shard_map/ppermute | solution.py:394
  86.8 0.7 copy-start.10
  87.5 0.6 copy-start.12
  88.1 0.9 copy-start.5
  89.0 0.9 copy-start.7
  90.0 0.9 copy-start.9
  90.9 0.9 copy-start.11
  91.8 0.9 copy-start.13
  95.7 27.9 %collective-permute-start.8 = (bf16[1040,256]{1,0:T(8,128)(2,1)}, bf16[1040,256]{1,0:T(8,128)(2,1)S(1)}, u32[]{:S(2)}, u32[]{:S(2)}) collective-permute-start(bf16[1040,256]{1,0:T(8,128)(2,1)} %get-tuple-element.29), channel_id=1, source_target_pairs={{0,4},{4,0},{8,12},{12,8},{16,20},{20,16},{24,28},{28,24},{1,5},{5... | collective-permute-start | bytes 1597448 | tf_op jit(solution)/shard_map/ppermute | solution.py:394
  97.3 26.3 %collective-permute-start.9 = (bf16[1040,256]{1,0:T(8,128)(2,1)}, bf16[1040,256]{1,0:T(8,128)(2,1)}, u32[]{:S(2)}, u32[]{:S(2)}) collective-permute-start(bf16[1040,256]{1,0:T(8,128)(2,1)} %get-tuple-element.30), channel_id=1, source_target_pairs={{0,8},{4,12},{8,0},{12,4},{16,24},{20,28},{24,16},{28,20},{1,9},{5... | collective-permute-start | bytes 1597448 | tf_op jit(solution)/shard_map/ppermute | solution.py:394
  97.3 36.8 %collective-permute-start.10 = (bf16[1040,256]{1,0:T(8,128)(2,1)}, bf16[1040,256]{1,0:T(8,128)(2,1)}, u32[]{:S(2)}, u32[]{:S(2)}) collective-permute-start(bf16[1040,256]{1,0:T(8,128)(2,1)} %get-tuple-element.31), channel_id=1, source_target_pairs={{0,12},{4,8},{8,4},{12,0},{16,28},{20,24},{24,20},{28,16},{1,13},{... | collective-permute-start | bytes 1597448 | tf_op jit(solution)/shard_map/ppermute | solution.py:394
  111.2 1.0 copy-start
  112.3 21.8 %copy-start.1 = (bf16[256,1024]{1,0:T(8,128)(2,1)S(1)}, bf16[256,1024]{1,0:T(8,128)(2,1)}, u32[]{:S(2)}) copy-start(bf16[256,1024]{1,0:T(8,128)(2,1)} %constant.29.clone.place) | copy-start | bytes 1572868

commit v2 on v1

v2 whole, which is shorter than its diff:
```python
import functools

import jax
import jax.numpy as jnp
import ml_dtypes
import numpy as np
from jax import lax
from jax.experimental import pallas as pl
from jax.experimental.pallas import tpu as pltpu
from jax.sharding import PartitionSpec as P

GRID = 8
GROUPS = 32
CAP = 2
TILE = 16
PARTS = 3
BATCH = 2
NAMES = 2 * PARTS * GROUPS
F32, BF16 = jnp.float32, jnp.bfloat16


def spread_table(latent, chunk):
    table = np.zeros((3, chunk, latent, 2 * latent, chunk), np.float32)
    places = np.arange(chunk)
    for tap in range(3):
        for step in range(latent):
            if 2 * step - 1 + tap >= 0:
                table[tap, places, step, 2 * step - 1 + tap, places] = 1
    return table.reshape(3 * chunk * latent, 2 * latent * chunk)


def swap_table(latent, share):
    table = np.zeros((latent, share, share, latent), np.float32)
    for step in range(latent):
        table[step, np.arange(share), np.arange(share), step] = 1
    return table.reshape(latent * share, latent * share)


def fold_table(channels, lanes):
    width = channels // GROUPS
    group = np.arange(lanes) // width
    return (group[:, None] == group[None, :]).astype(np.float32) / width


def pick_table(channels):
    table = np.zeros((channels, 256), np.float32)
    lanes = np.arange(NAMES)
    table[lanes % GROUPS * (channels // GROUPS), lanes] = 1
    return table


def place_table(channels):
    table = np.zeros((256, 2, channels), np.float32)
    lanes = np.arange(NAMES)
    of_group = lanes[:, None] % GROUPS == np.arange(channels)[None, :] // (channels // GROUPS)
    for which in range(2):
        mine = lanes // (PARTS * GROUPS) == which
        table[:NAMES, which] = of_group & mine[:, None]
    return table.reshape(256, 2 * channels)


def stacked(tables):
    rows = [np.pad(t, ((0, 0), (0, 256 - t.shape[1]))) for t in tables]
    starts = np.cumsum([0] + [r.shape[0] for r in rows])
    return np.concatenate(rows).astype(ml_dtypes.bfloat16), [int(s) for s in starts]


def split(row):
    parts = []
    for _ in range(PARTS):
        head = row.astype(BF16)
        parts.append(head.astype(F32))
        row = row - head.astype(F32)
    return parts


def fold(rows, table):
    lanes = table.shape[0]
    halves = rows[0].shape[1] // lanes
    stack = []
    for row in rows:
        parts = split(row)
        stack += [part[:, h * lanes : (h + 1) * lanes] for h in range(halves) for part in parts]
    spare = -len(stack) % TILE
    if spare:
        stack.append(jnp.zeros((spare, lanes), F32))
    out = jnp.dot(jnp.concatenate(stack, axis=0).astype(BF16), table, preferred_element_type=F32)
    sums = []
    for k in range(0, len(rows) * halves, halves):
        at = [PARTS * (k + h) for h in range(halves)]
        sums.append(jnp.concatenate([jnp.sum(out[i : i + PARTS], axis=0, keepdims=True) for i in at], axis=1))
    return sums


def centre(values, table):
    share = 1.0 / values[0].shape[0]
    averages = fold([jnp.sum(v, axis=0, keepdims=True) * share for v in values], table)
    centred = [v - average for v, average in zip(values, averages)]
    powers = fold([jnp.sum(v * v, axis=0, keepdims=True) * share for v in centred], table)
    return averages, centred, [lax.rsqrt(power + 1e-05) for power in powers]


def silu(v):
    half = 0.5 * v
    return half + half * jnp.tanh(half)


def encode_kernel(named, x, *rest, starts, shares, owned):
    given, rest = rest[:6], rest[6:]
    sends, rest = rest[:shares], rest[shares:]
    (w1, g1, w2, g2, w3, tables), (wide, act, sems) = rest[:6], rest[6:]
    me = lax.axis_index("patch").astype(jnp.int32)
    copies = [pltpu.make_async_copy(a, b, sems.at[i]) for i, (a, b) in enumerate(zip(given, rest[:6]))]
    step = pl.program_id(0)

    def arrive(*which):
        @pl.when(step == 0)
        def _():
            for i in which:
                copies[i].wait()

    batch, frames, places, breadth = x.shape
    latent = frames // 2
    c1, c2 = w1.shape[1], w2.shape[2]
    line = GRID * latent
    share = places * latent // shares
    chunk = 2 * GRID
    rows = places * latent

    @pl.when(step == 0)
    def _():
        for i in (0, 5, 1, 2, 3, 4):
            copies[i].start()
        for b in range(batch):
            wide[b, 0:line, :] = jnp.zeros((line, wide.shape[2]), BF16)
            wide[b, (GRID + 1) * line :, :] = jnp.zeros((line, wide.shape[2]), BF16)

    arrive(0, 5, 1)
    spread = tables[starts[0] : starts[1]]
    swap = tables[starts[1] : starts[2], 0:share]
    fold1 = tables[starts[2] : starts[3], 0:c1]
    fold2 = tables[starts[3] : starts[4], 0:c2]
    fold3 = tables[starts[4] : starts[5]]
    pick = tables[starts[5] : starts[6]]
    first = [
        jnp.dot(x[b].reshape(frames * places, breadth), w1[...], preferred_element_type=F32) for b in range(batch)
    ]
    _, centred, scales = centre(first, fold1)
    for b in range(batch):
        act1 = silu(centred[b] * (scales[b] * g1[...])).astype(BF16).reshape(frames, places, c1)
        for q in range(places // chunk):
            block = act1[:, q * chunk : (q + 1) * chunk].reshape(frames * chunk, c1)
            taps = jnp.dot(spread, block, preferred_element_type=F32)
            taps = taps.reshape(3, chunk // GRID, GRID, latent, c1)
            edge = jnp.zeros((chunk // GRID, 1, latent, c1), F32)
            at = line + q * chunk * latent
            for a in range(3):
                for j in range(3):
                    tap = taps[a]
                    if j == 0:
                        tap = jnp.concatenate([edge, tap[:, : GRID - 1]], axis=1)
                    if j == 2:
                        tap = jnp.concatenate([tap[:, 1:], edge], axis=1)
                    tap = tap.reshape(chunk * latent, c1).astype(BF16)
                    wide[b, at : at + chunk * latent, (3 * j + a) * c1 : (3 * j + a + 1) * c1] = tap
    arrive(2, 3, 4)
    second = []
    for b in range(batch):
        total = jnp.dot(wide[b, 0:rows], w2[0], preferred_element_type=F32)
        for i in (1, 2):
            total += jnp.dot(wide[b, i * line : i * line + rows], w2[i], preferred_element_type=F32)
        second.append(total)
    _, centred, scales = centre(second, fold2)
    third = []
    for b in range(batch):
        act2 = silu(centred[b] * (scales[b] * g2[...])).astype(BF16)
        act[b] = act2
        third.append(jnp.dot(act2, w3[...], preferred_element_type=F32))
    averages, _, scales = centre(third, fold3)
    lane = lax.broadcasted_iota(jnp.int32, (1, 256), 1)
    row = lax.broadcasted_iota(jnp.int32, (TILE, 256), 0)
    notes = jnp.zeros((TILE, 256), F32)
    for b in range(batch):
        parts = split(averages[b]) + split(scales[b])
        parts.append(jnp.zeros((TILE - len(parts), third[b].shape[1]), F32))
        picked = jnp.dot(jnp.concatenate(parts, axis=0).astype(BF16), pick, preferred_element_type=F32)
        note = jnp.zeros((1, 256), F32)
        for k in range(2 * PARTS):
            note = jnp.where(lane // GROUPS == k, picked[k : k + 1], note)
        for k in range(owned):
            note = jnp.where(lane == NAMES + k, named[k].astype(F32), note)
        notes = jnp.where(row == step * batch + b, note, notes)
    body = sends[0].shape[0] - TILE
    for j in range(shares):
        q = me ^ j
        for b in range(batch):
            part = act[b, pl.ds(pl.multiple_of(q * share, share), share), :]
            part = jnp.dot(swap, part, preferred_element_type=F32).astype(BF16)
            sends[j][pl.ds(pl.multiple_of((step * batch + b) * share, share), share), :] = part

        @pl.when(step == 0)
        def _():
            sends[j][body : body + TILE, :] = notes.astype(BF16)

        @pl.when(step > 0)
        def _():
            held = sends[j][body : body + TILE, :].astype(F32)
            sends[j][body : body + TILE, :] = (held + notes).astype(BF16)


def encode(named, pixels, weights, shares):
    w1, g1, w2, g2, w3 = weights
    owned, frames, places, breadth = pixels.shape
    latent = frames // 2
    c1, c2, c3 = w1.shape[1], w2.shape[2], w3.shape[1]
    share = latent * places // shares
    tables, starts = stacked([
        spread_table(latent, 2 * GRID),
        swap_table(latent, places // shares),
        fold_table(c1, c1),
        fold_table(c2, c2),
        fold_table(c3, 256),
        pick_table(c3),
    ])
    operands = [w1, g1.reshape(1, c1), w2.reshape(3, 3 * w2.shape[1], c2), g2.reshape(1, c2), w3]
    operands.append(jnp.asarray(tables))
    body = owned * share + TILE
    flops = 2 * frames * places * breadth * c1 + 2 * latent * places * (27 * c1 * c2 + c2 * c3)
    return pl.pallas_call(
        functools.partial(encode_kernel, starts=starts, shares=shares, owned=owned),
        grid_spec=pltpu.PrefetchScalarGridSpec(
            num_scalar_prefetch=1,
            grid=(owned // BATCH,),
            in_specs=[pl.BlockSpec((BATCH, frames, places, breadth), lambda i, s: (i, 0, 0, 0))]
            + [pl.BlockSpec(memory_space=pltpu.HBM)] * len(operands),
            out_specs=[pl.BlockSpec((body, c2), lambda i, s: (0, 0))] * shares,
            scratch_shapes=[pltpu.VMEM(o.shape, o.dtype) for o in operands]
            + [
                pltpu.VMEM((BATCH, (GRID + 2) * GRID * latent, 9 * c1), BF16),
                pltpu.VMEM((BATCH, places * latent, c2), BF16),
                pltpu.SemaphoreType.DMA((len(operands),)),
            ],
        ),
        out_shape=[jax.ShapeDtypeStruct((body, c2), BF16)] * shares,
        compiler_params=pltpu.CompilerParams(vmem_limit_bytes=60 * 1024 * 1024),
        cost_estimate=pl.CostEstimate(
            flops=owned * flops, bytes_accessed=owned * frames * places * breadth * 2, transcendentals=0
        ),
        name="encode",
    )(named, pixels, *operands)


def pack_kernel(ints, *rest, half, shares, owned, share):
    held, outs = rest[:shares], rest[shares : shares + half]
    notes, ready, note_sem, block_sem, out_sem = rest[shares + half :]
    me = lax.axis_index("patch").astype(jnp.int32)
    node = lax.axis_index("clip").astype(jnp.int32)
    body = owned * share
    waits = []
    for k in range(shares):
        copy = pltpu.make_async_copy(
            held[k].at[pl.ds(body, TILE)], notes.at[pl.ds(k * TILE, TILE)], note_sem.at[k]
        )
        copy.start()
        waits.append(copy)
    blocks, picks = [], []
    for s in range(half):
        for j in range(shares):
            seen = jnp.int32(0)
            found = [jnp.int32(0)] * CAP
            for i in range(owned):
                mine = ints[j * owned + i] == (node ^ s)
                for r in range(CAP):
                    found[r] = jnp.where(mine & (seen == r), i, found[r])
                seen = seen + mine.astype(jnp.int32)
            for r in range(CAP):
                k = (s * shares + j) * CAP + r
                clip = found[r]
                row = (me ^ j) * CAP + r
                to = pl.multiple_of(row * share, share)
                picks.append((jnp.where(seen > r, row, -1), clip))
                start = pl.multiple_of(clip * share, share)
                copy = pltpu.make_async_copy(
                    held[j].at[pl.ds(start, share)], outs[s].at[pl.ds(to, share)], block_sem.at[k]
                )
                copy.start()
                blocks.append(copy)
    for copy in waits:
        copy.wait()
    width = shares * TILE
    rows = lax.broadcasted_iota(jnp.int32, (TILE, width), 0)
    columns = lax.broadcasted_iota(jnp.int32, (TILE, width), 1)
    for s in range(half):
        sel = jnp.zeros((TILE, width), jnp.bool_)
        for j in range(shares):
            for r in range(CAP):
                row, clip = picks[(s * shares + j) * CAP + r]
                sel = sel | ((rows == row) & (columns == j * TILE + clip))
        sel = jnp.where(sel, 1.0, 0.0).astype(BF16)
        ready[s] = jnp.dot(sel, notes[...], preferred_element_type=F32).astype(BF16)
        copy = pltpu.make_async_copy(ready.at[s], outs[s].at[pl.ds(shares * CAP * share, TILE)], out_sem.at[s])
        copy.start()
        blocks.append(copy)
    for copy in blocks:
        copy.wait()


def pack(half, held, owned, share):
    shares, channels = len(held), held[0].shape[1]
    ints = jnp.concatenate([h[owned * share, NAMES : NAMES + owned] for h in held]).astype(jnp.int32)
    out_rows = shares * CAP * share + TILE
    anywhere = pl.BlockSpec(memory_space=pl.ANY)
    copies = half * shares * CAP
    return pl.pallas_call(
        functools.partial(pack_kernel, half=half, shares=shares, owned=owned, share=share),
        grid_spec=pltpu.PrefetchScalarGridSpec(
            num_scalar_prefetch=1,
            grid=(1,),
            in_specs=[anywhere] * shares,
            out_specs=[anywhere] * half,
            scratch_shapes=[
                pltpu.VMEM((shares * TILE, channels), BF16),
                pltpu.VMEM((half, TILE, channels), BF16),
                pltpu.SemaphoreType.DMA((shares,)),
                pltpu.SemaphoreType.DMA((copies,)),
                pltpu.SemaphoreType.DMA((half,)),
            ],
        ),
        out_shape=[jax.ShapeDtypeStruct((out_rows, channels), BF16)] * half,
        compiler_params=pltpu.CompilerParams(vmem_limit_bytes=8 * 1024 * 1024),
        cost_estimate=pl.CostEstimate(flops=0, bytes_accessed=2 * copies * share * channels, transcendentals=0),
        name="pack",
    )(ints, *held)


def finish_kernel(columns, w3, g3, place, *rest, count):
    taken, out = rest[:count], rest[-1]
    c3 = w3.shape[1]
    shares, _, cap, latent, share, _ = out.shape
    rows = latent * share
    for i in range(count):

        @pl.when(pl.program_id(0) == i)
        def _():
            wide = jnp.dot(taken[i][shares * cap * rows :, :], place[...], preferred_element_type=F32)
            mean, gain = wide[:, :c3], wide[:, c3:] * g3[...]
            for p in range(shares):
                block = taken[i][p * cap * rows : (p + 1) * cap * rows, :]
                third = jnp.dot(block, w3[...], preferred_element_type=F32)
                for r in range(cap):
                    at = p * cap + r
                    token = (third[r * rows : (r + 1) * rows] - mean[at : at + 1]) * gain[at : at + 1]
                    out[p, 0, r] = token.reshape(latent, share, c3).astype(BF16)


def finish(columns, arrays, w3, g3, shape, before=None):
    count = len(arrays)
    shares, _, cap, latent, share, c3 = shape
    rows = latent * share
    c2 = w3.shape[0]
    place = jnp.asarray(place_table(c3).astype(ml_dtypes.bfloat16))
    operands = [w3, g3, place, *arrays]
    specs = [pl.BlockSpec(o.shape, lambda k, s: (0, 0)) for o in operands]
    aliases = {}
    if before is not None:
        specs.append(pl.BlockSpec(memory_space=pl.ANY))
        aliases = {1 + len(operands): 0}
        operands.append(before)
    return pl.pallas_call(
        functools.partial(finish_kernel, count=count),
        grid_spec=pltpu.PrefetchScalarGridSpec(
            num_scalar_prefetch=1,
            grid=(count,),
            in_specs=specs,
            out_specs=pl.BlockSpec((shares, 1, cap, latent, share, c3), lambda k, s: (0, s[k], 0, 0, 0, 0)),
        ),
        out_shape=jax.ShapeDtypeStruct(shape, BF16),
        input_output_aliases=aliases,
        compiler_params=pltpu.CompilerParams(vmem_limit_bytes=24 * 1024 * 1024),
        cost_estimate=pl.CostEstimate(
            flops=2 * count * shares * cap * rows * c2 * c3,
            bytes_accessed=count * shares * cap * rows * (c2 + c3) * 2,
            transcendentals=0,
        ),
        name="finish",
    )(columns, *operands)


def on_device(pixels, destination, embed_weight, embed_gain, mixing_weight, mixing_gain, project_weight, project_gain):
    nodes, shares = lax.axis_size("clip"), lax.axis_size("patch")
    node = lax.axis_index("clip").astype(jnp.int32)
    half = nodes // 2
    owned, frames, places, _ = pixels.shape
    latent, c3 = frames // 2, project_weight.shape[1]
    share = latent * places // shares
    weights = (embed_weight, embed_gain, mixing_weight, mixing_gain, project_weight)
    named = destination.reshape(owned)

    def to_share(array, j):
        if j == 0:
            return array
        return lax.ppermute(array, "patch", [(p, p ^ j) for p in range(shares)])

    def to_node(array, s):
        if s == 0:
            return array
        return lax.ppermute(array, "clip", [(c, c ^ s) for c in range(nodes)])

    sends = encode(named, pixels, weights, shares)
    near = [to_share(sends[j], j) for j in range(shares)]
    far = [to_node(near[j], half) for j in range(shares)]
    own = pack(half, near, owned, share)
    own = [to_node(own[s], s) for s in range(half)]
    other = pack(half, far, owned, share)
    other = [to_node(other[s], s) for s in range(half)]

    w3, g3 = project_weight, project_gain.reshape(1, c3)
    shape = (shares, nodes, CAP, latent, places // shares, c3)
    early = jnp.stack([node ^ s for s in range(half)] + [node ^ half])
    latents = finish(early, own + other[:1], w3, g3, shape)
    for s in range(1, half):
        latents = finish((node ^ half ^ s).reshape(1), other[s : s + 1], w3, g3, shape, latents)
    return latents.reshape(shares * nodes * CAP, latent, places // shares, c3)


def solution(mesh):
    return jax.shard_map(
        on_device,
        mesh=mesh,
        in_specs=(
            P(("clip", "patch"), None, None, None),
            P(("clip", "patch"), None),
            P(),
            P(),
            P(),
            P(),
            P(),
            P(),
        ),
        out_specs=P("clip", None, "patch", None),
        check_vma=False,
    )
```

time: 144 us -> 109 us (0.76)
  local copies, waits for them, and re-layouts: 21.5 us -> 4.18 us
  Pallas kernels: 48.2 us -> 34.5 us
  starting transfers between devices: 25.2 us -> 20.3 us
  waiting for transfers between devices: 45.6 us -> 49.6 us
  other arithmetic: 2.74 us -> 0.16 us
    ppermute x8 -> x0, waiting for transfers between devices: 23.2 us -> none  [across(): return lax.ppermute(array, ('clip', 'patch'), pairs)]
    ppermute x6 -> x10, waiting for transfers between devices: 22.3 us -> 44.2 us  [to_node(): return lax.ppermute(array, 'clip', [(c, c ^ s) for c in range(nodes)])]
    ppermute x8 -> x0, starting transfers between devices: 13.2 us -> none  [across(): return lax.ppermute(array, ('clip', 'patch'), pairs)]
    unnamed x44 -> x12, local copies, waits for them, and re-layouts: 15.9 us -> 2.81 us
    ppermute x6 -> x10, starting transfers between devices: 7.1 us -> 17.1 us  [to_node(): return lax.ppermute(array, 'clip', [(c, c ^ s) for c in range(nodes)])]
    pallas_call x2 -> x4, Pallas kernels: 20.5 us -> 10.7 us  [finish(): pl.pallas_call(functools.partial(finish_kernel, count=count), grid_spec=p...]
    ppermute x6 -> x3, waiting for transfers between devices: 0.02 us -> 5.35 us  [to_share(): return lax.ppermute(array, 'patch', [(p, p ^ j) for p in range(shares)])]
    pallas_call x2 -> x1, Pallas kernels: 21.7 us -> 17.3 us  [encode(): pl.pallas_call(functools.partial(encode_kernel, starts=starts, shares=sha...]
  transfers between devices with their start and end apart: 20 -> 13, of which waited for: 6 -> 9; matrix products, arithmetic and copies ran while one was open for 5% -> 1% of each run, Pallas kernels for 18% -> 14%
where the time goes in v2:
time: 109 us
  waiting for transfers between devices  49.6 us (46%)
  Pallas kernels  34.5 us (32%)
  starting transfers between devices  20.3 us (19%)
  local copies, waits for them, and re-layouts  4.18 us (4%)
    ppermute x10, waiting for transfers between devices, to_node(): return lax.ppermute(array, 'clip', [(c, c ^ s) for c in range(nodes)])  44.2 us
    pallas_call x1, Pallas kernels, encode(): pl.pallas_call(functools.partial(encode_kernel, starts=starts, shares=sha...  17.3 us
    ppermute x10, starting transfers between devices, to_node(): return lax.ppermute(array, 'clip', [(c, c ^ s) for c in range(nodes)])  17.1 us
    pallas_call x4, Pallas kernels, finish(): pl.pallas_call(functools.partial(finish_kernel, count=count), grid_spec=p...  10.7 us
    pallas_call x2, Pallas kernels, pack(): pl.pallas_call(functools.partial(pack_kernel, half=half, shares=shares, o...  6.53 us
    ppermute x3, waiting for transfers between devices, to_share(): return lax.ppermute(array, 'patch', [(p, p ^ j) for p in range(shares)])  5.35 us
    ppermute x3, starting transfers between devices, to_share(): return lax.ppermute(array, 'patch', [(p, p ^ j) for p in range(shares)])  3.17 us
    unnamed x12, local copies, waits for them, and re-layouts  2.81 us
  transfers between devices with their start and end apart: 13, of which 9 were waited for; matrix products, arithmetic and copies ran while one was open for 1% of the time, Pallas kernels for 14%

profile of v2, /device:TPU:0, one launch (start us, length us, event | category | flops | bytes accessed | tf_op | source)
XLA Modules:
  0.0 108.9 jit_solution(6779248834578713944)
XLA Ops:
  0.0 17.3 %encode.1 = (bf16[528,256]{1,0:T(8,128)(2,1)}, bf16[528,256]{1,0:T(8,128)(2,1)}, bf16[528,256]{1,0:T(8,128)(2,1)}, bf16[528,256]{1,0:T(8,128)(2,1)}) custom-call(s32[4]{0:T(128)} %bitcast.36, bf16[4,16,64,384]{3,2,1,0:T(8,128)(2,1)} %x.1, bf16[384,128]{1,0:T(8,128)(2,1)} %rest_0_.1, f32[1,128]{1,0:T(1,128)} %bitcast.37, bf16[3,1152,256]{2,1,0:T(8,128)(2,1)} %bitcast.34, ...), custom_call_target="tpu_custom_call" | custom-call | flops 4563402752 | bytes 3145728 | tf_op jit(solution)/shard_map/encode/pallas_call | solution.py:229
  17.3 2.5 %collective-permute-start.5 = (bf16[528,256]{1,0:T(8,128)(2,1)}, bf16[528,256]{1,0:T(8,128)(2,1)S(1)}, u32[]{:S(2)}, u32[]{:S(2)}) collective-permute-start(bf16[528,256]{1,0:T(8,128)(2,1)} %get-tuple-element.20), channel_id=1, source_target_pairs={{0,3},{1,2},{2,1},{3,0},{4,7},{5,6},{6,5},{7,4},{8,11},{9,10},{10,... | collective-permute-start | bytes 811016 | tf_op jit(solution)/shard_map/ppermute | solution.py:402
  19.8 0.6 collective-permute-start.3
  20.5 0.0 collective-permute-start.1
  20.5 2.8 %collective-permute-start = (bf16[528,256]{1,0:T(8,128)(2,1)}, bf16[528,256]{1,0:T(8,128)(2,1)S(1)}, u32[]{:S(2)}, u32[]{:S(2)}) collective-permute-start(bf16[528,256]{1,0:T(8,128)(2,1)} %get-tuple-element.17.rest_0_), channel_id=1, source_target_pairs={{0,16},{4,20},{8,24},{12,28},{16,0},{20,4},{24,8},{28,12},{1,17},{... | collective-permute-start | bytes 811016 | tf_op jit(solution)/shard_map/ppermute | solution.py:407
  23.3 0.8 slice_bitcast_fusion.7
  24.1 2.9 %collective-permute-done.5.rest_3_ = bf16[528,256]{1,0:T(8,128)(2,1)S(1)} collective-permute-done((bf16[528,256]{1,0:T(8,128)(2,1)}, bf16[528,256]{1,0:T(8,128)(2,1)S(1)}, u32[]{:S(2)}, u32[]{:S(2)}) %collective-permute-start.5) | collective-permute-done | bytes 270368 | tf_op jit(solution)/shard_map/ppermute | solution.py:402
  27.0 3.4 %collective-permute-start.6 = (bf16[528,256]{1,0:T(8,128)(2,1)S(1)}, bf16[528,256]{1,0:T(8,128)(2,1)S(1)}, u32[]{:S(2)}, u32[]{:S(2)}) collective-permute-start(bf16[528,256]{1,0:T(8,128)(2,1)S(1)} %collective-permute-done.5.rest_3_), channel_id=1, source_target_pairs={{0,16},{4,20},{8,24},{12,28},{16,0},{20,4},{24,8},{28,12},{1,17},{... | collective-permute-start | bytes 811016 | tf_op jit(solution)/shard_map/ppermute | solution.py:407
  30.4 0.1 slice_bitcast_fusion
  30.4 2.4 %collective-permute-done.3.rest_2_ = bf16[528,256]{1,0:T(8,128)(2,1)S(1)} collective-permute-done((bf16[528,256]{1,0:T(8,128)(2,1)}, bf16[528,256]{1,0:T(8,128)(2,1)S(1)}, u32[]{:S(2)}, u32[]{:S(2)}) %collective-permute-start.3) | collective-permute-done | bytes 270368 | tf_op jit(solution)/shard_map/ppermute | solution.py:402
  32.9 0.1 slice_bitcast_fusion.1
  32.9 0.0 collective-permute-done.1.rest_1_
  32.9 0.1 slice_bitcast_fusion.2
  33.0 0.1 maximum_convert_fusion.1.ints
  33.1 1.0 copy-done.4
  34.0 3.6 %pack.3 = (bf16[1040,256]{1,0:T(8,128)(2,1)S(1)}, bf16[1040,256]{1,0:T(8,128)(2,1)S(1)}, bf16[1040,256]{1,0:T(8,128)(2,1)}, bf16[1040,256]{1,0:T(8,128)(2,1)}) custom-call(s32[16]{0:T(128)S(1)} %maximum_convert_fusion.1.ints, bf16[528,256]{1,0:T(8,128)(2,1)S(1)} %copy-done.4, bf16[528,256]{1,0:T(8,128)(2,1)S(1)} %collective-permute-done.1.rest_1_, ...), custom_call_target="tpu_custom_call" | custom-call | bytes 2097152 | tf_op jit(solution)/shard_map/pack/pallas_call | solution.py:314
  37.7 2.3 %collective-permute-start.10 = (bf16[1040,256]{1,0:T(8,128)(2,1)S(1)}, bf16[1040,256]{1,0:T(8,128)(2,1)S(1)}, u32[]{:S(2)}, u32[]{:S(2)}) collective-permute-start(bf16[1040,256]{1,0:T(8,128)(2,1)S(1)} %get-tuple-element.25), channel_id=1, source_target_pairs={{0,4},{4,0},{8,12},{12,8},{16,20},{20,16},{24,28},{28,24},{1,5},{5... | collective-permute-start | bytes 1597448 | tf_op jit(solution)/shard_map/ppermute | solution.py:407
  40.0 1.6 %collective-permute-start.11 = (bf16[1040,256]{1,0:T(8,128)(2,1)}, bf16[1040,256]{1,0:T(8,128)(2,1)}, u32[]{:S(2)}, u32[]{:S(2)}) collective-permute-start(bf16[1040,256]{1,0:T(8,128)(2,1)} %get-tuple-element.26), channel_id=1, source_target_pairs={{0,8},{4,12},{8,0},{12,4},{16,24},{20,28},{24,16},{28,20},{1,9},{5... | collective-permute-start | bytes 1597448 | tf_op jit(solution)/shard_map/ppermute | solution.py:407
  41.6 0.0 collective-permute-start.12
  41.6 0.9 collective-permute-done.rest_0_
  42.5 2.1 %collective-permute-start.4 = (bf16[528,256]{1,0:T(8,128)(2,1)S(1)}, bf16[528,256]{1,0:T(8,128)(2,1)S(1)}, u32[]{:S(2)}, u32[]{:S(2)}) collective-permute-start(bf16[528,256]{1,0:T(8,128)(2,1)S(1)} %collective-permute-done.3.rest_2_), channel_id=1, source_target_pairs={{0,16},{4,20},{8,24},{12,28},{16,0},{20,4},{24,8},{28,12},{1,17},{... | collective-permute-start | bytes 811016 | tf_op jit(solution)/shard_map/ppermute | solution.py:407
  44.6 0.1 slice_bitcast_fusion.6
  44.7 3.7 %collective-permute-done.6.rest_3_ = bf16[528,256]{1,0:T(8,128)(2,1)S(1)} collective-permute-done((bf16[528,256]{1,0:T(8,128)(2,1)S(1)}, bf16[528,256]{1,0:T(8,128)(2,1)S(1)}, u32[]{:S(2)}, u32[]{:S(2)}) %collective-permute-start.6) | collective-permute-done | bytes 270368 | tf_op jit(solution)/shard_map/ppermute | solution.py:407
  48.4 0.0 collective-permute-start.2
  48.4 0.1 slice_bitcast_fusion.3
  48.5 23.1 %collective-permute-done.4.rest_2_ = bf16[528,256]{1,0:T(8,128)(2,1)S(1)} collective-permute-done((bf16[528,256]{1,0:T(8,128)(2,1)S(1)}, bf16[528,256]{1,0:T(8,128)(2,1)S(1)}, u32[]{:S(2)}, u32[]{:S(2)}) %collective-permute-start.4) | collective-permute-done | bytes 270368 | tf_op jit(solution)/shard_map/ppermute | solution.py:407
  71.5 0.1 slice_bitcast_fusion.4
  71.6 4.5 %collective-permute-done.2.rest_1_ = bf16[528,256]{1,0:T(8,128)(2,1)S(1)} collective-permute-done((bf16[528,256]{1,0:T(8,128)(2,1)S(1)}, bf16[528,256]{1,0:T(8,128)(2,1)S(1)}, u32[]{:S(2)}, u32[]{:S(2)}) %collective-permute-start.2) | collective-permute-done | bytes 270368 | tf_op jit(solution)/shard_map/ppermute | solution.py:407
  76.1 0.1 slice_bitcast_fusion.5
  76.2 0.1 maximum_convert_fusion.ints
  76.2 2.9 %pack.2 = (bf16[1040,256]{1,0:T(8,128)(2,1)S(1)}, bf16[1040,256]{1,0:T(8,128)(2,1)}, bf16[1040,256]{1,0:T(8,128)(2,1)}, bf16[1040,256]{1,0:T(8,128)(2,1)}) custom-call(s32[16]{0:T(128)S(1)} %maximum_convert_fusion.ints, bf16[528,256]{1,0:T(8,128)(2,1)S(1)} %collective-permute-done.rest_0_, bf16[528,256]{1,0:T(8,128)(2,1)S(1)} %collective-permute-done.2.rest_1_, ...), custom_call_target="tpu_custom_call" | custom-call | bytes 2097152 | tf_op jit(solution)/shard_map/pack/pallas_call | solution.py:314
  79.2 0.0 copy-start.2
  79.2 0.8 copy-done.2
  80.0 0.5 collective-permute-start.9
  80.5 3.5 %collective-permute-start.8 = (bf16[1040,256]{1,0:T(8,128)(2,1)}, bf16[1040,256]{1,0:T(8,128)(2,1)S(1)}, u32[]{:S(2)}, u32[]{:S(2)}) collective-permute-start(bf16[1040,256]{1,0:T(8,128)(2,1)} %get-tuple-element.22), channel_id=1, source_target_pairs={{0,8},{4,12},{8,0},{12,4},{16,24},{20,28},{24,16},{28,20},{1,9},{5... | collective-permute-start | bytes 1597448 | tf_op jit(solution)/shard_map/ppermute | solution.py:407
  84.0 0.0 collective-permute-done.10.rest_1_
  84.0 0.9 collective-permute-start.7
  84.9 0.1 stack.23.columns
  85.0 0.0 collective-permute-done.11.rest_2_
  85.0 0.0 collective-permute-done.12.rest_3_
  85.1 1.0 copy-done.3
  86.1 6.2 %finish.4.rest_1_ = bf16[4,8,2,8,16,512]{5,4,3,2,1,0:T(8,128)(2,1)} custom-call(s32[5]{0:T(128)S(1)} %stack.23.columns, bf16[256,512]{1,0:T(8,128)(2,1)S(1)} %copy-done.1, f32[1,512]{1,0:T(1,128)S(1)} %bitcast.30, bf16[256,1024]{1,0:T(8,128)(2,1)S(1)} %copy-done, bf16[1040,256]{1,0:T(8,128)(2,1)S(1)} %get-tuple-element.24.rest_0_, ...), custom_call_target="tpu_custom_call" | custom-call | flops 1342177280 | bytes 7864320 | tf_op jit(solution)/shard_map/finish/pallas_call | solution.py:369
  92.3 3.0 %collective-permute-done.9.rest_0_ = bf16[1040,256]{1,0:T(8,128)(2,1)S(1)} collective-permute-done((bf16[1040,256]{1,0:T(8,128)(2,1)}, bf16[1040,256]{1,0:T(8,128)(2,1)S(1)}, u32[]{:S(2)}, u32[]{:S(2)}) %collective-permute-start.9) | collective-permute-done | bytes 532512 | tf_op jit(solution)/shard_map/ppermute | solution.py:407
  95.4 1.5 %finish.5.rest_1_ = bf16[4,8,2,8,16,512]{5,4,3,2,1,0:T(8,128)(2,1)} custom-call(s32[1]{0:T(128)} %bitcast.11.columns, bf16[256,512]{1,0:T(8,128)(2,1)S(1)} %copy-done.1, f32[1,512]{1,0:T(1,128)S(1)} %bitcast.31, bf16[256,1024]{1,0:T(8,128)(2,1)S(1)} %copy-done, bf16[1040,256]{1,0:T(8,128)(2,1)S(1)} %collective-permute-done.9.rest_0_, ...), custom_call_target="tpu_custom_call", output_to_operand_aliasing={{}: (5, {})} | custom-call | flops 268435456 | bytes 1572864 | tf_op jit(solution)/shard_map/finish/pallas_call | solution.py:369
  96.9 0.4 collective-permute-done.8.rest_0_
  97.2 1.5 %finish.6.rest_1_ = bf16[4,8,2,8,16,512]{5,4,3,2,1,0:T(8,128)(2,1)} custom-call(s32[1]{0:T(128)} %bitcast.10.columns, bf16[256,512]{1,0:T(8,128)(2,1)S(1)} %copy-done.1, f32[1,512]{1,0:T(1,128)S(1)} %bitcast.32, bf16[256,1024]{1,0:T(8,128)(2,1)S(1)} %copy-done, bf16[1040,256]{1,0:T(8,128)(2,1)S(1)} %collective-permute-done.8.rest_0_, ...), custom_call_target="tpu_custom_call", output_to_operand_aliasing={{}: (5, {})} | custom-call | flops 268435456 | bytes 1572864 | tf_op jit(solution)/shard_map/finish/pallas_call | solution.py:369
  98.7 8.7 %collective-permute-done.7.rest_0_ = bf16[1040,256]{1,0:T(8,128)(2,1)S(1)} collective-permute-done((bf16[1040,256]{1,0:T(8,128)(2,1)}, bf16[1040,256]{1,0:T(8,128)(2,1)S(1)}, u32[]{:S(2)}, u32[]{:S(2)}) %collective-permute-start.7) | collective-permute-done | bytes 532512 | tf_op jit(solution)/shard_map/ppermute | solution.py:407
  107.4 1.5 %finish.7 = bf16[4,8,2,8,16,512]{5,4,3,2,1,0:T(8,128)(2,1)} custom-call(s32[1]{0:T(128)} %bitcast.columns, bf16[256,512]{1,0:T(8,128)(2,1)S(1)} %copy-done.1, f32[1,512]{1,0:T(1,128)S(1)} %bitcast.33, bf16[256,1024]{1,0:T(8,128)(2,1)S(1)} %copy-done, bf16[1040,256]{1,0:T(8,128)(2,1)S(1)} %collective-permute-done.7.rest_0_, ...), custom_call_target="tpu_custom_call", output_to_operand_aliasing={{}: (5, {})} | custom-call | flops 268435456 | bytes 1572864 | tf_op jit(solution)/shard_map/finish/pallas_call | solution.py:369
  (8 shorter events, 0.0 us)
Async XLA Ops:
  0.0 85.0 %copy-start = (bf16[256,1024]{1,0:T(8,128)(2,1)S(1)}, bf16[256,1024]{1,0:T(8,128)(2,1)}, u32[]{:S(2)}) copy-start(bf16[256,1024]{1,0:T(8,128)(2,1)} %constant.19.clone.place) | copy-start | bytes 1572868
  0.0 85.0 %copy-start.1 = (bf16[256,512]{1,0:T(8,128)(2,1)S(1)}, bf16[256,512]{1,0:T(8,128)(2,1)}, u32[]{:S(2)}) copy-start(bf16[256,512]{1,0:T(8,128)(2,1)} %w3.7) | copy-start | bytes 786436
  0.0 85.0 %copy-start.5 = (f32[512]{0:T(512)S(1)}, f32[512]{0:T(512)}, u32[]{:S(2)}) copy-start(f32[512]{0:T(512)} %param.20) | copy-start | bytes 6148
  17.3 9.7 %collective-permute-start.5 = (bf16[528,256]{1,0:T(8,128)(2,1)}, bf16[528,256]{1,0:T(8,128)(2,1)S(1)}, u32[]{:S(2)}, u32[]{:S(2)}) collective-permute-start(bf16[528,256]{1,0:T(8,128)(2,1)} %get-tuple-element.20), channel_id=1, source_target_pairs={{0,3},{1,2},{2,1},{3,0},{4,7},{5,6},{6,5},{7,4},{8,11},{9,10},{10,... | collective-permute-start | bytes 811016 | tf_op jit(solution)/shard_map/ppermute | solution.py:402
  19.8 13.0 %collective-permute-start.3 = (bf16[528,256]{1,0:T(8,128)(2,1)}, bf16[528,256]{1,0:T(8,128)(2,1)S(1)}, u32[]{:S(2)}, u32[]{:S(2)}) collective-permute-start(bf16[528,256]{1,0:T(8,128)(2,1)} %get-tuple-element.19), channel_id=1, source_target_pairs={{0,2},{1,3},{2,0},{3,1},{4,6},{5,7},{6,4},{7,5},{8,10},{9,11},{10,... | collective-permute-start | bytes 811016 | tf_op jit(solution)/shard_map/ppermute | solution.py:402
  20.5 12.5 %collective-permute-start.1 = (bf16[528,256]{1,0:T(8,128)(2,1)}, bf16[528,256]{1,0:T(8,128)(2,1)S(1)}, u32[]{:S(2)}, u32[]{:S(2)}) collective-permute-start(bf16[528,256]{1,0:T(8,128)(2,1)} %get-tuple-element.18), channel_id=1, source_target_pairs={{0,1},{1,0},{2,3},{3,2},{4,5},{5,4},{6,7},{7,6},{8,9},{9,8},{10,11... | collective-permute-start | bytes 811016 | tf_op jit(solution)/shard_map/ppermute | solution.py:402
  20.5 22.0 %collective-permute-start = (bf16[528,256]{1,0:T(8,128)(2,1)}, bf16[528,256]{1,0:T(8,128)(2,1)S(1)}, u32[]{:S(2)}, u32[]{:S(2)}) collective-permute-start(bf16[528,256]{1,0:T(8,128)(2,1)} %get-tuple-element.17.rest_0_), channel_id=1, source_target_pairs={{0,16},{4,20},{8,24},{12,28},{16,0},{20,4},{24,8},{28,12},{1,17},{... | collective-permute-start | bytes 811016 | tf_op jit(solution)/shard_map/ppermute | solution.py:407
  27.0 21.4 %collective-permute-start.6 = (bf16[528,256]{1,0:T(8,128)(2,1)S(1)}, bf16[528,256]{1,0:T(8,128)(2,1)S(1)}, u32[]{:S(2)}, u32[]{:S(2)}) collective-permute-start(bf16[528,256]{1,0:T(8,128)(2,1)S(1)} %collective-permute-done.5.rest_3_), channel_id=1, source_target_pairs={{0,16},{4,20},{8,24},{12,28},{16,0},{20,4},{24,8},{28,12},{1,17},{... | collective-permute-start | bytes 811016 | tf_op jit(solution)/shard_map/ppermute | solution.py:407
  33.1 1.0 copy-start.4
  37.7 46.3 %collective-permute-start.10 = (bf16[1040,256]{1,0:T(8,128)(2,1)S(1)}, bf16[1040,256]{1,0:T(8,128)(2,1)S(1)}, u32[]{:S(2)}, u32[]{:S(2)}) collective-permute-start(bf16[1040,256]{1,0:T(8,128)(2,1)S(1)} %get-tuple-element.25), channel_id=1, source_target_pairs={{0,4},{4,0},{8,12},{12,8},{16,20},{20,16},{24,28},{28,24},{1,5},{5... | collective-permute-start | bytes 1597448 | tf_op jit(solution)/shard_map/ppermute | solution.py:407
  40.0 45.0 %collective-permute-start.11 = (bf16[1040,256]{1,0:T(8,128)(2,1)}, bf16[1040,256]{1,0:T(8,128)(2,1)}, u32[]{:S(2)}, u32[]{:S(2)}) collective-permute-start(bf16[1040,256]{1,0:T(8,128)(2,1)} %get-tuple-element.26), channel_id=1, source_target_pairs={{0,8},{4,12},{8,0},{12,4},{16,24},{20,28},{24,16},{28,20},{1,9},{5... | collective-permute-start | bytes 1597448 | tf_op jit(solution)/shard_map/ppermute | solution.py:407
  41.6 43.4 %collective-permute-start.12 = (bf16[1040,256]{1,0:T(8,128)(2,1)}, bf16[1040,256]{1,0:T(8,128)(2,1)}, u32[]{:S(2)}, u32[]{:S(2)}) collective-permute-start(bf16[1040,256]{1,0:T(8,128)(2,1)} %get-tuple-element.27), channel_id=1, source_target_pairs={{0,12},{4,8},{8,4},{12,0},{16,28},{20,24},{24,20},{28,16},{1,13},{... | collective-permute-start | bytes 1597448 | tf_op jit(solution)/shard_map/ppermute | solution.py:407
  42.5 29.0 %collective-permute-start.4 = (bf16[528,256]{1,0:T(8,128)(2,1)S(1)}, bf16[528,256]{1,0:T(8,128)(2,1)S(1)}, u32[]{:S(2)}, u32[]{:S(2)}) collective-permute-start(bf16[528,256]{1,0:T(8,128)(2,1)S(1)} %collective-permute-done.3.rest_2_), channel_id=1, source_target_pairs={{0,16},{4,20},{8,24},{12,28},{16,0},{20,4},{24,8},{28,12},{1,17},{... | collective-permute-start | bytes 811016 | tf_op jit(solution)/shard_map/ppermute | solution.py:407
  48.4 27.7 %collective-permute-start.2 = (bf16[528,256]{1,0:T(8,128)(2,1)S(1)}, bf16[528,256]{1,0:T(8,128)(2,1)S(1)}, u32[]{:S(2)}, u32[]{:S(2)}) collective-permute-start(bf16[528,256]{1,0:T(8,128)(2,1)S(1)} %collective-permute-done.1.rest_1_), channel_id=1, source_target_pairs={{0,16},{4,20},{8,24},{12,28},{16,0},{20,4},{24,8},{28,12},{1,17},{... | collective-permute-start | bytes 811016 | tf_op jit(solution)/shard_map/ppermute | solution.py:407
  79.2 0.8 copy-start.2
  80.0 15.4 %collective-permute-start.9 = (bf16[1040,256]{1,0:T(8,128)(2,1)}, bf16[1040,256]{1,0:T(8,128)(2,1)S(1)}, u32[]{:S(2)}, u32[]{:S(2)}) collective-permute-start(bf16[1040,256]{1,0:T(8,128)(2,1)} %get-tuple-element.23), channel_id=1, source_target_pairs={{0,4},{4,0},{8,12},{12,8},{16,20},{20,16},{24,28},{28,24},{1,5},{5... | collective-permute-start | bytes 1597448 | tf_op jit(solution)/shard_map/ppermute | solution.py:407
  80.5 16.7 %collective-permute-start.8 = (bf16[1040,256]{1,0:T(8,128)(2,1)}, bf16[1040,256]{1,0:T(8,128)(2,1)S(1)}, u32[]{:S(2)}, u32[]{:S(2)}) collective-permute-start(bf16[1040,256]{1,0:T(8,128)(2,1)} %get-tuple-element.22), channel_id=1, source_target_pairs={{0,8},{4,12},{8,0},{12,4},{16,24},{20,28},{24,16},{28,20},{1,9},{5... | collective-permute-start | bytes 1597448 | tf_op jit(solution)/shard_map/ppermute | solution.py:407
  84.0 23.4 %collective-permute-start.7 = (bf16[1040,256]{1,0:T(8,128)(2,1)}, bf16[1040,256]{1,0:T(8,128)(2,1)S(1)}, u32[]{:S(2)}, u32[]{:S(2)}) collective-permute-start(bf16[1040,256]{1,0:T(8,128)(2,1)} %get-tuple-element.21), channel_id=1, source_target_pairs={{0,12},{4,8},{8,4},{12,0},{16,28},{20,24},{24,20},{28,16},{1,13},{... | collective-permute-start | bytes 1597448 | tf_op jit(solution)/shard_map/ppermute | solution.py:407
  85.0 1.0 copy-start.3

commit v3 on v2

--- a/solution.py
+++ b/solution.py
@@ -14,7 +14,7 @@
 CAP = 2
 TILE = 16
 PARTS = 3
-BATCH = 2
+BATCH = 4
 NAMES = 2 * PARTS * GROUPS
 F32, BF16 = jnp.float32, jnp.bfloat16
 
@@ -108,7 +108,7 @@
 def encode_kernel(named, x, *rest, starts, shares, owned):
     given, rest = rest[:6], rest[6:]
     sends, rest = rest[:shares], rest[shares:]
-    (w1, g1, w2, g2, w3, tables), (wide, act, sems) = rest[:6], rest[6:]
+    (w1, g1, w2, g2, w3, tables), (tubes, wide, act, sems, tube_sems) = rest[:6], rest[6:]
     me = lax.axis_index("patch").astype(jnp.int32)
     copies = [pltpu.make_async_copy(a, b, sems.at[i]) for i, (a, b) in enumerate(zip(given, rest[:6]))]
     step = pl.program_id(0)
@@ -119,7 +119,8 @@
             for i in which:
                 copies[i].wait()
 
-    batch, frames, places, breadth = x.shape
+    batch, frames, places, breadth = tubes.shape
+    loads = [pltpu.make_async_copy(x.at[step * batch + b], tubes.at[b], tube_sems.at[b]) for b in range(batch)]
     latent = frames // 2
     c1, c2 = w1.shape[1], w2.shape[2]
     line = GRID * latent
@@ -129,7 +130,21 @@
 
     @pl.when(step == 0)
     def _():
-        for i in (0, 5, 1, 2, 3, 4):
+        copies[0].start()
+
+    loads[0].start()
+
+    @pl.when(step == 0)
+    def _():
+        copies[5].start()
+        copies[1].start()
+
+    for load in loads[1:]:
+        load.start()
+
+    @pl.when(step == 0)
+    def _():
+        for i in (2, 3, 4):
             copies[i].start()
         for b in range(batch):
             wide[b, 0:line, :] = jnp.zeros((line, wide.shape[2]), BF16)
@@ -142,9 +157,10 @@
     fold2 = tables[starts[3] : starts[4], 0:c2]
     fold3 = tables[starts[4] : starts[5]]
     pick = tables[starts[5] : starts[6]]
-    first = [
-        jnp.dot(x[b].reshape(frames * places, breadth), w1[...], preferred_element_type=F32) for b in range(batch)
-    ]
+    first = []
+    for b in range(batch):
+        loads[b].wait()
+        first.append(jnp.dot(tubes[b].reshape(frames * places, breadth), w1[...], preferred_element_type=F32))
     _, centred, scales = centre(first, fold1)
     for b in range(batch):
         act1 = silu(centred[b] * (scales[b] * g1[...])).astype(BF16).reshape(frames, places, c1)
@@ -179,16 +195,18 @@
     averages, _, scales = centre(third, fold3)
     lane = lax.broadcasted_iota(jnp.int32, (1, 256), 1)
     row = lax.broadcasted_iota(jnp.int32, (TILE, 256), 0)
+    parts = [part for b in range(batch) for part in split(averages[b]) + split(scales[b])]
+    parts.append(jnp.zeros((-len(parts) % TILE, third[0].shape[1]), F32))
+    picked = jnp.dot(jnp.concatenate(parts, axis=0).astype(BF16), pick, preferred_element_type=F32)
+    names = jnp.zeros((1, 256), F32)
+    for k in range(owned):
+        names = jnp.where(lane == NAMES + k, named[k].astype(F32), names)
     notes = jnp.zeros((TILE, 256), F32)
     for b in range(batch):
-        parts = split(averages[b]) + split(scales[b])
-        parts.append(jnp.zeros((TILE - len(parts), third[b].shape[1]), F32))
-        picked = jnp.dot(jnp.concatenate(parts, axis=0).astype(BF16), pick, preferred_element_type=F32)
-        note = jnp.zeros((1, 256), F32)
+        note = names
         for k in range(2 * PARTS):
-            note = jnp.where(lane // GROUPS == k, picked[k : k + 1], note)
-        for k in range(owned):
-            note = jnp.where(lane == NAMES + k, named[k].astype(F32), note)
+            at = 2 * PARTS * b + k
+            note = jnp.where(lane // GROUPS == k, picked[at : at + 1], note)
         notes = jnp.where(row == step * batch + b, note, notes)
     body = sends[0].shape[0] - TILE
     for j in range(shares):
@@ -231,14 +249,15 @@
         grid_spec=pltpu.PrefetchScalarGridSpec(
             num_scalar_prefetch=1,
             grid=(owned // BATCH,),
-            in_specs=[pl.BlockSpec((BATCH, frames, places, breadth), lambda i, s: (i, 0, 0, 0))]
-            + [pl.BlockSpec(memory_space=pltpu.HBM)] * len(operands),
+            in_specs=[pl.BlockSpec(memory_space=pltpu.HBM)] * (1 + len(operands)),
             out_specs=[pl.BlockSpec((body, c2), lambda i, s: (0, 0))] * shares,
             scratch_shapes=[pltpu.VMEM(o.shape, o.dtype) for o in operands]
             + [
+                pltpu.VMEM((BATCH, frames, places, breadth), BF16),
                 pltpu.VMEM((BATCH, (GRID + 2) * GRID * latent, 9 * c1), BF16),
                 pltpu.VMEM((BATCH, places * latent, c2), BF16),
                 pltpu.SemaphoreType.DMA((len(operands),)),
+                pltpu.SemaphoreType.DMA((BATCH,)),
             ],
         ),
         out_shape=[jax.ShapeDtypeStruct((body, c2), BF16)] * shares,
@@ -250,22 +269,22 @@
     )(named, pixels, *operands)
 
 
-def pack_kernel(ints, *rest, half, shares, owned, share):
-    held, outs = rest[:shares], rest[shares : shares + half]
-    notes, ready, note_sem, block_sem, out_sem = rest[shares + half :]
+def pack_kernel(ints, *rest, half, jobs, pick, owned, share):
+    arrays = sum(len(job) for job in jobs)
+    held, outs = rest[:arrays], rest[arrays : arrays + len(jobs) * half]
+    notes, ready, note_sem, block_sem, out_sem = rest[arrays + len(jobs) * half :]
     me = lax.axis_index("patch").astype(jnp.int32)
     node = lax.axis_index("clip").astype(jnp.int32)
+    owners = len(jobs[0])
     body = owned * share
     waits = []
-    for k in range(shares):
-        copy = pltpu.make_async_copy(
-            held[k].at[pl.ds(body, TILE)], notes.at[pl.ds(k * TILE, TILE)], note_sem.at[k]
-        )
+    for k in range(owners):
+        copy = pltpu.make_async_copy(held[k].at[pl.ds(body, TILE)], notes.at[pl.ds(k * TILE, TILE)], note_sem.at[k])
         copy.start()
         waits.append(copy)
     blocks, picks = [], []
     for s in range(half):
-        for j in range(shares):
+        for j in range(owners):
             seen = jnp.int32(0)
             found = [jnp.int32(0)] * CAP
             for i in range(owned):
@@ -274,90 +293,103 @@
                     found[r] = jnp.where(mine & (seen == r), i, found[r])
                 seen = seen + mine.astype(jnp.int32)
             for r in range(CAP):
-                k = (s * shares + j) * CAP + r
                 clip = found[r]
-                row = (me ^ j) * CAP + r
+                row = pick(me ^ jobs[0][j]) * CAP + r
                 to = pl.multiple_of(row * share, share)
+                start = pl.multiple_of(clip * share, share)
                 picks.append((jnp.where(seen > r, row, -1), clip))
-                start = pl.multiple_of(clip * share, share)
-                copy = pltpu.make_async_copy(
-                    held[j].at[pl.ds(start, share)], outs[s].at[pl.ds(to, share)], block_sem.at[k]
-                )
-                copy.start()
-                blocks.append(copy)
+                for g in range(len(jobs)):
+                    copy = pltpu.make_async_copy(
+                        held[g * owners + j].at[pl.ds(start, share)],
+                        outs[g * half + s].at[pl.ds(to, share)],
+                        block_sem.at[len(blocks)],
+                    )
+                    copy.start()
+                    blocks.append(copy)
     for copy in waits:
         copy.wait()
-    width = shares * TILE
+    width = owners * TILE
     rows = lax.broadcasted_iota(jnp.int32, (TILE, width), 0)
     columns = lax.broadcasted_iota(jnp.int32, (TILE, width), 1)
     for s in range(half):
         sel = jnp.zeros((TILE, width), jnp.bool_)
-        for j in range(shares):
+        for j in range(owners):
             for r in range(CAP):
-                row, clip = picks[(s * shares + j) * CAP + r]
+                row, clip = picks[(s * owners + j) * CAP + r]
                 sel = sel | ((rows == row) & (columns == j * TILE + clip))
         sel = jnp.where(sel, 1.0, 0.0).astype(BF16)
         ready[s] = jnp.dot(sel, notes[...], preferred_element_type=F32).astype(BF16)
-        copy = pltpu.make_async_copy(ready.at[s], outs[s].at[pl.ds(shares * CAP * share, TILE)], out_sem.at[s])
-        copy.start()
-        blocks.append(copy)
+    for s in range(half):
+        for g in range(len(jobs)):
+            k = g * half + s
+            copy = pltpu.make_async_copy(
+                ready.at[s], outs[k].at[pl.ds(owners * CAP * share, TILE)], out_sem.at[k]
+            )
+            copy.start()
+            blocks.append(copy)
     for copy in blocks:
         copy.wait()
 
 
-def pack(half, held, owned, share):
-    shares, channels = len(held), held[0].shape[1]
-    ints = jnp.concatenate([h[owned * share, NAMES : NAMES + owned] for h in held]).astype(jnp.int32)
-    out_rows = shares * CAP * share + TILE
+def pack(half, held, jobs, pick, owned, share):
+    owners, channels = len(jobs[0]), held[0].shape[1]
+    names = [h[owned * share, NAMES : NAMES + owned] for h in held[:owners]]
+    ints = jnp.concatenate(names).astype(jnp.int32)
+    out_rows = owners * CAP * share + TILE
     anywhere = pl.BlockSpec(memory_space=pl.ANY)
-    copies = half * shares * CAP
-    return pl.pallas_call(
-        functools.partial(pack_kernel, half=half, shares=shares, owned=owned, share=share),
+    count = len(jobs) * half
+    copies = count * owners * CAP
+    outs = pl.pallas_call(
+        functools.partial(pack_kernel, half=half, jobs=jobs, pick=pick, owned=owned, share=share),
         grid_spec=pltpu.PrefetchScalarGridSpec(
             num_scalar_prefetch=1,
             grid=(1,),
-            in_specs=[anywhere] * shares,
-            out_specs=[anywhere] * half,
+            in_specs=[anywhere] * len(held),
+            out_specs=[anywhere] * count,
             scratch_shapes=[
-                pltpu.VMEM((shares * TILE, channels), BF16),
+                pltpu.VMEM((owners * TILE, channels), BF16),
                 pltpu.VMEM((half, TILE, channels), BF16),
-                pltpu.SemaphoreType.DMA((shares,)),
+                pltpu.SemaphoreType.DMA((owners,)),
                 pltpu.SemaphoreType.DMA((copies,)),
-                pltpu.SemaphoreType.DMA((half,)),
+                pltpu.SemaphoreType.DMA((count,)),
             ],
         ),
-        out_shape=[jax.ShapeDtypeStruct((out_rows, channels), BF16)] * half,
+        out_shape=[jax.ShapeDtypeStruct((out_rows, channels), BF16)] * count,
         compiler_params=pltpu.CompilerParams(vmem_limit_bytes=8 * 1024 * 1024),
         cost_estimate=pl.CostEstimate(flops=0, bytes_accessed=2 * copies * share * channels, transcendentals=0),
         name="pack",
     )(ints, *held)
-
-
-def finish_kernel(columns, w3, g3, place, *rest, count):
+    return [outs[g * half : (g + 1) * half] for g in range(len(jobs))]
+
+
+def finish_kernel(places, w3, g3, place, *rest, count):
     taken, out = rest[:count], rest[-1]
     c3 = w3.shape[1]
-    shares, _, cap, latent, share, _ = out.shape
+    lines, cores, _, cap, latent, share, _ = out.shape
     rows = latent * share
+    owners = [(y, core) for y in range(lines) for core in range(cores)]
     for i in range(count):
 
         @pl.when(pl.program_id(0) == i)
         def _():
-            wide = jnp.dot(taken[i][shares * cap * rows :, :], place[...], preferred_element_type=F32)
+            wide = jnp.dot(taken[i][len(owners) * cap * rows :, :], place[...], preferred_element_type=F32)
             mean, gain = wide[:, :c3], wide[:, c3:] * g3[...]
-            for p in range(shares):
+            for p, (y, core) in enumerate(owners):
                 block = taken[i][p * cap * rows : (p + 1) * cap * rows, :]
                 third = jnp.dot(block, w3[...], preferred_element_type=F32)
                 for r in range(cap):
                     at = p * cap + r
                     token = (third[r * rows : (r + 1) * rows] - mean[at : at + 1]) * gain[at : at + 1]
-                    out[p, 0, r] = token.reshape(latent, share, c3).astype(BF16)
-
-
-def finish(columns, arrays, w3, g3, shape, before=None):
-    count = len(arrays)
-    shares, _, cap, latent, share, c3 = shape
+                    out[y, core, 0, r] = token.reshape(latent, share, c3).astype(BF16)
+
+
+def finish(pieces, block, w3, g3, shape, before=None):
+    count = len(pieces)
+    cap, latent, share, c3 = shape[3:]
     rows = latent * share
     c2 = w3.shape[0]
+    arrays = [piece[3] for piece in pieces]
+    places = jnp.stack([jnp.asarray(piece[k], jnp.int32) for piece in pieces for k in range(3)])
     place = jnp.asarray(place_table(c3).astype(ml_dtypes.bfloat16))
     operands = [w3, g3, place, *arrays]
     specs = [pl.BlockSpec(o.shape, lambda k, s: (0, 0)) for o in operands]
@@ -366,24 +398,26 @@
         specs.append(pl.BlockSpec(memory_space=pl.ANY))
         aliases = {1 + len(operands): 0}
         operands.append(before)
+    blocks = count * block[0] * block[1] * cap
     return pl.pallas_call(
         functools.partial(finish_kernel, count=count),
         grid_spec=pltpu.PrefetchScalarGridSpec(
             num_scalar_prefetch=1,
             grid=(count,),
             in_specs=specs,
-            out_specs=pl.BlockSpec((shares, 1, cap, latent, share, c3), lambda k, s: (0, s[k], 0, 0, 0, 0)),
+            out_specs=pl.BlockSpec(
+                (*block, 1, cap, latent, share, c3),
+                lambda k, s: (s[3 * k], s[3 * k + 1], s[3 * k + 2], 0, 0, 0, 0),
+            ),
         ),
         out_shape=jax.ShapeDtypeStruct(shape, BF16),
         input_output_aliases=aliases,
         compiler_params=pltpu.CompilerParams(vmem_limit_bytes=24 * 1024 * 1024),
         cost_estimate=pl.CostEstimate(
-            flops=2 * count * shares * cap * rows * c2 * c3,
-            bytes_accessed=count * shares * cap * rows * (c2 + c3) * 2,
-            transcendentals=0,
+            flops=2 * blocks * rows * c2 * c3, bytes_accessed=blocks * rows * (c2 + c3) * 2, transcendentals=0
         ),
         name="finish",
-    )(columns, *operands)
+    )(places, *operands)
 
 
 def on_device(pixels, destination, embed_weight, embed_gain, mixing_weight, mixing_gain, project_weight, project_gain):
@@ -396,30 +430,43 @@
     weights = (embed_weight, embed_gain, mixing_weight, mixing_gain, project_weight)
     named = destination.reshape(owned)
 
-    def to_share(array, j):
-        if j == 0:
+    me = lax.axis_index("patch").astype(jnp.int32)
+    lines = shares // 2
+    w3, g3 = project_weight, project_gain.reshape(1, c3)
+    shape = (lines, 2, nodes, CAP, latent, places // shares, c3)
+
+    def send(array, s, j):
+        if s == 0 and j == 0:
             return array
-        return lax.ppermute(array, "patch", [(p, p ^ j) for p in range(shares)])
-
-    def to_node(array, s):
-        if s == 0:
-            return array
-        return lax.ppermute(array, "clip", [(c, c ^ s) for c in range(nodes)])
+        pairs = [(c * shares + p, (c ^ s) * shares + (p ^ j)) for c in range(nodes) for p in range(shares)]
+        return lax.ppermute(array, ("clip", "patch"), pairs)
 
     sends = encode(named, pixels, weights, shares)
-    near = [to_share(sends[j], j) for j in range(shares)]
-    far = [to_node(near[j], half) for j in range(shares)]
-    own = pack(half, near, owned, share)
-    own = [to_node(own[s], s) for s in range(half)]
-    other = pack(half, far, owned, share)
-    other = [to_node(other[s], s) for s in range(half)]
-
-    w3, g3 = project_weight, project_gain.reshape(1, c3)
-    shape = (shares, nodes, CAP, latent, places // shares, c3)
-    early = jnp.stack([node ^ s for s in range(half)] + [node ^ half])
-    latents = finish(early, own + other[:1], w3, g3, shape)
-    for s in range(1, half):
-        latents = finish((node ^ half ^ s).reshape(1), other[s : s + 1], w3, g3, shape, latents)
+    held = [sends[0::2], [send(array, 0, 1) for array in sends[1::2]]]
+    pairs = [[held[0][k], held[1][k]] for k in range(lines)]
+    own = pack(half, [a for pair in pairs for a in pair], [[0, 1]] * lines, lambda p: p % 2, owned, share)
+    crossed = [send(held[0][k], half, 2 * k) for k in range(lines)]
+    arrived = [[send(own[k][s], s, 2 * k) for s in range(half)] for k in range(lines)]
+    pieces = [((me // 2) ^ k, 0, node ^ s, arrived[k][s]) for k in range(lines) for s in range(half)]
+    def after(arrays, *earlier):
+        return lax.optimization_barrier((*arrays, *earlier))[: len(arrays)]
+
+    spread = [a for line in arrived[1:] for a in line]
+    beyond = after(held[1], *crossed, *[a for line in own for a in line], arrived[0][1])
+    beyond = [send(beyond[k], half, 2 * k) for k in range(lines)]
+    early, late = [], []
+    for b, far in enumerate((crossed, beyond)):
+        if b:
+            far = after(far, *spread, *arrived[0])
+        (other,) = pack(half, list(far), [[2 * k + b for k in range(lines)]], lambda p: p // 2, owned, share)
+        seconds = [send(other[s], s, 0) for s in range(half)]
+        arrivals = [(0, (me % 2) ^ b, node ^ half ^ s, seconds[s]) for s in range(half)]
+        early += arrivals if b == 0 else arrivals[:1]
+        late = arrivals[1:]
+    latents = finish(pieces, (1, 2), w3, g3, shape)
+    latents = finish(early, (lines, 1), w3, g3, shape, latents)
+    for piece in late:
+        latents = finish([piece], (lines, 1), w3, g3, shape, latents)
     return latents.reshape(shares * nodes * CAP, latent, places // shares, c3)
 
 

time: 109 us -> 105 us (0.963)
  waiting for transfers between devices: 49.6 us -> 39.8 us
  Pallas kernels: 34.5 us -> 37.4 us
  starting transfers between devices: 20.3 us -> 22.3 us
    ppermute x13 -> x19, waiting for transfers between devices: 49.6 us -> 39.8 us  [send(): return lax.ppermute(array, ('clip', 'patch'), pairs)]
    pallas_call x4 -> x5, Pallas kernels: 10.7 us -> 15 us  [finish(): pl.pallas_call(functools.partial(finish_kernel, count=count), grid_spec=p...]
    pallas_call x1, Pallas kernels: 17.3 us -> 14 us  [encode(): pl.pallas_call(functools.partial(encode_kernel, starts=starts, shares=sha...]
    ppermute x13 -> x19, starting transfers between devices: 20.3 us -> 22.3 us  [send(): return lax.ppermute(array, ('clip', 'patch'), pairs)]
    pallas_call x2 -> x3, Pallas kernels: 6.53 us -> 8.36 us  [pack(): pl.pallas_call(functools.partial(pack_kernel, half=half, jobs=jobs, pick=...]
    unnamed x12 -> x14, local copies, waits for them, and re-layouts: 2.81 us -> 3.32 us
  transfers between devices with their start and end apart: 13 -> 19, of which waited for: 9 -> 9; matrix products, arithmetic and copies ran while one was open for 1% -> 2% of each run, Pallas kernels for 14% -> 21%
where the time goes in v3:
time: 105 us
  waiting for transfers between devices  39.8 us (38%)
  Pallas kernels  37.4 us (36%)
  starting transfers between devices  22.3 us (21%)
  local copies, waits for them, and re-layouts  4.57 us (4%)
    ppermute x19, waiting for transfers between devices, send(): return lax.ppermute(array, ('clip', 'patch'), pairs)  39.8 us
    ppermute x19, starting transfers between devices, send(): return lax.ppermute(array, ('clip', 'patch'), pairs)  22.3 us
    pallas_call x5, Pallas kernels, finish(): pl.pallas_call(functools.partial(finish_kernel, count=count), grid_spec=p...  15 us
    pallas_call x1, Pallas kernels, encode(): pl.pallas_call(functools.partial(encode_kernel, starts=starts, shares=sha...  14 us
    pallas_call x3, Pallas kernels, pack(): pl.pallas_call(functools.partial(pack_kernel, half=half, jobs=jobs, pick=...  8.36 us
    unnamed x14, local copies, waits for them, and re-layouts  3.32 us
  transfers between devices with their start and end apart: 19, of which 9 were waited for; matrix products, arithmetic and copies ran while one was open for 2% of the time, Pallas kernels for 21%

profile of v3, /device:TPU:0, one launch (start us, length us, event | category | flops | bytes accessed | tf_op | source)
XLA Modules:
  0.0 104.7 jit_solution(10995775040008474621)
XLA Ops:
  0.0 14.0 %encode.1 = (bf16[528,256]{1,0:T(8,128)(2,1)}, bf16[528,256]{1,0:T(8,128)(2,1)}, bf16[528,256]{1,0:T(8,128)(2,1)}, bf16[528,256]{1,0:T(8,128)(2,1)}) custom-call(s32[4]{0:T(128)} %bitcast.37, bf16[4,16,64,384]{3,2,1,0:T(8,128)(2,1)} %x.1, bf16[384,128]{1,0:T(8,128)(2,1)} %rest_0_.1, f32[1,128]{1,0:T(1,128)} %bitcast.38, bf16[3,1152,256]{2,1,0:T(8,128)(2,1)} %bitcast.35, ...), custom_call_target="tpu_custom_call" | custom-call | flops 4563402752 | bytes 3145728 | tf_op jit(solution)/shard_map/encode/pallas_call | solution.py:247
  14.0 0.5 collective-permute-start
  14.5 0.1 collective-permute-start.1
  14.6 5.0 %collective-permute-start.3 = (bf16[528,256]{1,0:T(8,128)(2,1)}, bf16[528,256]{1,0:T(8,128)(2,1)S(1)}, u32[]{:S(2)}, u32[]{:S(2)}) collective-permute-start(bf16[528,256]{1,0:T(8,128)(2,1)} %get-tuple-element.32.rest_2_), channel_id=1, source_target_pairs={{0,18},{1,19},{2,16},{3,17},{4,22},{5,23},{6,20},{7,21},{8,26},{9,... | collective-permute-start | bytes 811016 | tf_op jit(solution)/shard_map/ppermute | solution.py:442
  19.6 0.3 collective-permute-start.2
  19.9 0.1 pad_add_fusion.2.places
  20.0 0.8 slice_bitcast_fusion.5
  20.8 0.1 maximum_convert_fusion.ints
  20.9 1.0 copy-done.2
  21.9 1.0 copy-done.3
  22.8 3.4 %pack.3 = (bf16[528,256]{1,0:T(8,128)(2,1)S(1)}, bf16[528,256]{1,0:T(8,128)(2,1)}, bf16[528,256]{1,0:T(8,128)(2,1)}, bf16[528,256]{1,0:T(8,128)(2,1)}, bf16[528,...) custom-call(s32[8]{0:T(128)S(1)} %maximum_convert_fusion.ints, ...), custom_call_target="tpu_custom_call" | custom-call | bytes 2097152 | tf_op jit(solution)/shard_map/pack/pallas_call | solution.py:342
  26.3 0.7 copy-done.5
  27.0 0.7 copy-done.6
  27.7 1.5 %collective-permute-start.4 = (bf16[528,256]{1,0:T(8,128)(2,1)}, bf16[528,256]{1,0:T(8,128)(2,1)S(1)}, u32[]{:S(2)}, u32[]{:S(2)}) collective-permute-start(bf16[528,256]{1,0:T(8,128)(2,1)} %get-tuple-element.34), channel_id=1, source_target_pairs={{0,4},{1,5},{2,6},{3,7},{4,0},{5,1},{6,2},{7,3},{8,12},{9,13},{10,... | collective-permute-start | bytes 811016 | tf_op jit(solution)/shard_map/ppermute | solution.py:442
  29.1 1.6 %collective-permute-start.11 = (bf16[528,256]{1,0:T(8,128)(2,1)}, bf16[528,256]{1,0:T(8,128)(2,1)S(1)}, u32[]{:S(2)}, u32[]{:S(2)}) collective-permute-start(bf16[528,256]{1,0:T(8,128)(2,1)} %get-tuple-element.35), channel_id=1, source_target_pairs={{0,8},{1,9},{2,10},{3,11},{4,12},{5,13},{6,14},{7,15},{8,0},{9,1},... | collective-permute-start | bytes 811016 | tf_op jit(solution)/shard_map/ppermute | solution.py:442
  30.7 0.4 collective-permute-start.12
  31.1 7.6 %collective-permute-done.3.rest_1_ = bf16[528,256]{1,0:T(8,128)(2,1)S(1)} collective-permute-done((bf16[528,256]{1,0:T(8,128)(2,1)}, bf16[528,256]{1,0:T(8,128)(2,1)S(1)}, u32[]{:S(2)}, u32[]{:S(2)}) %collective-permute-start.3) | collective-permute-done | bytes 270368 | tf_op jit(solution)/shard_map/ppermute | solution.py:442
  38.8 1.8 %collective-permute-start.7 = (bf16[528,256]{1,0:T(8,128)(2,1)}, bf16[528,256]{1,0:T(8,128)(2,1)S(1)}, u32[]{:S(2)}, u32[]{:S(2)}) collective-permute-start(bf16[528,256]{1,0:T(8,128)(2,1)} %get-tuple-element.37), channel_id=1, source_target_pairs={{0,2},{1,3},{2,0},{3,1},{4,6},{5,7},{6,4},{7,5},{8,10},{9,11},{10,... | collective-permute-start | bytes 811016 | tf_op jit(solution)/shard_map/ppermute | solution.py:442
  40.6 0.1 pad_add_fusion.3.places
  40.7 0.1 stack.80.places
  40.8 0.1 stack.87.places
  40.9 0.1 slice_bitcast_fusion
  40.9 3.1 %collective-permute-done.2.rest_0_ = bf16[528,256]{1,0:T(8,128)(2,1)S(1)} collective-permute-done((bf16[528,256]{1,0:T(8,128)(2,1)}, bf16[528,256]{1,0:T(8,128)(2,1)S(1)}, u32[]{:S(2)}, u32[]{:S(2)}) %collective-permute-start.2) | collective-permute-done | bytes 270368 | tf_op jit(solution)/shard_map/ppermute | solution.py:442
  44.1 1.4 %collective-permute-start.8 = (bf16[528,256]{1,0:T(8,128)(2,1)}, bf16[528,256]{1,0:T(8,128)(2,1)S(1)}, u32[]{:S(2)}, u32[]{:S(2)}) collective-permute-start(bf16[528,256]{1,0:T(8,128)(2,1)} %copy-done.6), channel_id=1, source_target_pairs={{0,6},{1,7},{2,4},{3,5},{4,2},{5,3},{6,0},{7,1},{8,14},{9,15},{10,... | collective-permute-start | bytes 811016 | tf_op jit(solution)/shard_map/ppermute | solution.py:442
  45.5 1.7 %collective-permute-start.9 = (bf16[528,256]{1,0:T(8,128)(2,1)}, bf16[528,256]{1,0:T(8,128)(2,1)S(1)}, u32[]{:S(2)}, u32[]{:S(2)}) collective-permute-start(bf16[528,256]{1,0:T(8,128)(2,1)} %copy-done.5), channel_id=1, source_target_pairs={{0,10},{1,11},{2,8},{3,9},{4,14},{5,15},{6,12},{7,13},{8,2},{9,3},... | collective-permute-start | bytes 811016 | tf_op jit(solution)/shard_map/ppermute | solution.py:442
  47.2 2.1 %collective-permute-done.11.rest_2_ = bf16[528,256]{1,0:T(8,128)(2,1)S(1)} collective-permute-done((bf16[528,256]{1,0:T(8,128)(2,1)}, bf16[528,256]{1,0:T(8,128)(2,1)S(1)}, u32[]{:S(2)}, u32[]{:S(2)}) %collective-permute-start.11) | collective-permute-done | bytes 270368 | tf_op jit(solution)/shard_map/ppermute | solution.py:442
  49.3 5.8 %collective-permute-done.12.rest_3_ = bf16[528,256]{1,0:T(8,128)(2,1)S(1)} collective-permute-done((bf16[528,256]{1,0:T(8,128)(2,1)}, bf16[528,256]{1,0:T(8,128)(2,1)S(1)}, u32[]{:S(2)}, u32[]{:S(2)}) %collective-permute-start.12) | collective-permute-done | bytes 270368 | tf_op jit(solution)/shard_map/ppermute | solution.py:442
  55.1 2.1 %collective-permute-start.5 = (bf16[528,256]{1,0:T(8,128)(2,1)S(1)}, bf16[528,256]{1,0:T(8,128)(2,1)S(1)}, u32[]{:S(2)}, u32[]{:S(2)}) collective-permute-start(bf16[528,256]{1,0:T(8,128)(2,1)S(1)} %collective-permute-done.rest_1_), channel_id=1, source_target_pairs={{0,16},{1,17},{2,18},{3,19},{4,20},{5,21},{6,22},{7,23},{8,24},{9,... | collective-permute-start | bytes 811016 | tf_op jit(solution)/shard_map/ppermute | solution.py:442
  57.2 0.5 collective-permute-start.6
  57.7 0.1 maximum_convert_fusion.2.ints
  57.8 2.5 %pack.5 = (bf16[528,256]{1,0:T(8,128)(2,1)S(1)}, bf16[528,256]{1,0:T(8,128)(2,1)S(1)}, bf16[528,256]{1,0:T(8,128)(2,1)S(1)}, bf16[528,256]{1,0:T(8,128)(2,1)S(1)}) custom-call(s32[8]{0:T(128)S(1)} %maximum_convert_fusion.2.ints, bf16[528,256]{1,0:T(8,128)(2,1)S(1)} %collective-permute-done.2.rest_0_, bf16[528,256]{1,0:T(8,128)(2,1)S(1)} %collective-permute-done.3.rest_1_), custom_call_target="tpu_custom_call" | custom-call | bytes 1048576 | tf_op jit(solution)/shard_map/pack/pallas_call | solution.py:342
  60.3 1.8 %collective-permute-start.16 = (bf16[528,256]{1,0:T(8,128)(2,1)S(1)}, bf16[528,256]{1,0:T(8,128)(2,1)S(1)}, u32[]{:S(2)}, u32[]{:S(2)}) collective-permute-start(bf16[528,256]{1,0:T(8,128)(2,1)S(1)} %get-tuple-element.49), channel_id=1, source_target_pairs={{0,4},{1,5},{2,6},{3,7},{4,0},{5,1},{6,2},{7,3},{8,12},{9,13},{10,... | collective-permute-start | bytes 811016 | tf_op jit(solution)/shard_map/ppermute | solution.py:442
  62.1 5.9 %collective-permute-done.9.rest_6_ = bf16[528,256]{1,0:T(8,128)(2,1)S(1)} collective-permute-done((bf16[528,256]{1,0:T(8,128)(2,1)}, bf16[528,256]{1,0:T(8,128)(2,1)S(1)}, u32[]{:S(2)}, u32[]{:S(2)}) %collective-permute-start.9) | collective-permute-done | bytes 270368 | tf_op jit(solution)/shard_map/ppermute | solution.py:442
  68.0 6.8 %collective-permute-done.10.rest_7_ = bf16[528,256]{1,0:T(8,128)(2,1)S(1)} collective-permute-done((bf16[528,256]{1,0:T(8,128)(2,1)S(1)}, bf16[528,256]{1,0:T(8,128)(2,1)S(1)}, u32[]{:S(2)}, u32[]{:S(2)}) %collective-permute-start.10) | collective-permute-done | bytes 270368 | tf_op jit(solution)/shard_map/ppermute | solution.py:442
  74.8 1.6 %collective-permute-done.5.rest_0_ = bf16[528,256]{1,0:T(8,128)(2,1)S(1)} collective-permute-done((bf16[528,256]{1,0:T(8,128)(2,1)S(1)}, bf16[528,256]{1,0:T(8,128)(2,1)S(1)}, u32[]{:S(2)}, u32[]{:S(2)}) %collective-permute-start.5) | collective-permute-done | bytes 270368 | tf_op jit(solution)/shard_map/ppermute | solution.py:442
  76.4 3.2 %collective-permute-done.6.rest_1_ = bf16[528,256]{1,0:T(8,128)(2,1)S(1)} collective-permute-done((bf16[528,256]{1,0:T(8,128)(2,1)S(1)}, bf16[528,256]{1,0:T(8,128)(2,1)S(1)}, u32[]{:S(2)}, u32[]{:S(2)}) %collective-permute-start.6) | collective-permute-done | bytes 270368 | tf_op jit(solution)/shard_map/ppermute | solution.py:442
  79.6 0.1 slice_bitcast_fusion.3
  79.6 0.1 maximum_convert_fusion.1.ints
  79.7 2.5 %pack.4 = (bf16[528,256]{1,0:T(8,128)(2,1)S(1)}, bf16[528,256]{1,0:T(8,128)(2,1)S(1)}, bf16[528,256]{1,0:T(8,128)(2,1)S(1)}, bf16[528,256]{1,0:T(8,128)(2,1)S(1)}) custom-call(s32[8]{0:T(128)S(1)} %maximum_convert_fusion.1.ints, bf16[528,256]{1,0:T(8,128)(2,1)S(1)} %collective-permute-done.5.rest_0_, bf16[528,256]{1,0:T(8,128)(2,1)S(1)} %collective-permute-done.6.rest_1_), custom_call_target="tpu_custom_call" | custom-call | bytes 1048576 | tf_op jit(solution)/shard_map/pack/pallas_call | solution.py:342
  82.2 2.3 %collective-permute-start.13 = (bf16[528,256]{1,0:T(8,128)(2,1)S(1)}, bf16[528,256]{1,0:T(8,128)(2,1)S(1)}, u32[]{:S(2)}, u32[]{:S(2)}) collective-permute-start(bf16[528,256]{1,0:T(8,128)(2,1)S(1)} %get-tuple-element.45), channel_id=1, source_target_pairs={{0,12},{1,13},{2,14},{3,15},{4,8},{5,9},{6,10},{7,11},{8,4},{9,5},... | collective-permute-start | bytes 811016 | tf_op jit(solution)/shard_map/ppermute | solution.py:442
  84.5 1.3 %collective-permute-start.15 = (bf16[528,256]{1,0:T(8,128)(2,1)S(1)}, bf16[528,256]{1,0:T(8,128)(2,1)S(1)}, u32[]{:S(2)}, u32[]{:S(2)}) collective-permute-start(bf16[528,256]{1,0:T(8,128)(2,1)S(1)} %get-tuple-element.47), channel_id=1, source_target_pairs={{0,4},{1,5},{2,6},{3,7},{4,0},{5,1},{6,2},{7,3},{8,12},{9,13},{10,... | collective-permute-start | bytes 811016 | tf_op jit(solution)/shard_map/ppermute | solution.py:442
  85.8 0.1 pad_add_fusion.places
  85.9 5.8 %finish.5.rest_5_ = bf16[2,2,8,2,8,16,512]{6,5,4,3,2,1,0:T(8,128)(2,1)} custom-call(s32[24]{0:T(128)S(1)} %stack.87.places, bf16[256,512]{1,0:T(8,128)(2,1)S(1)} %copy-done.1, f32[1,512]{1,0:T(1,128)S(1)} %bitcast.30, bf16[256,1024]{1,0:T(8,128)(2,1)S(1)} %copy-done, bf16[528,256]{1,0:T(8,128)(2,1)S(1)} %get-tuple-element.33.rest_0_, ...), custom_call_target="tpu_custom_call" | custom-call | flops 1073741824 | bytes 6291456 | tf_op jit(solution)/shard_map/finish/pallas_call | solution.py:402
  91.7 4.1 %finish.6.rest_1_ = bf16[2,2,8,2,8,16,512]{6,5,4,3,2,1,0:T(8,128)(2,1)} custom-call(s32[15]{0:T(128)S(1)} %stack.80.places, bf16[256,512]{1,0:T(8,128)(2,1)S(1)} %copy-done.1, f32[1,512]{1,0:T(1,128)S(1)} %bitcast.31, bf16[256,1024]{1,0:T(8,128)(2,1)S(1)} %copy-done, bf16[528,256]{1,0:T(8,128)(2,1)S(1)} %get-tuple-element.48.rest_0_, ...), custom_call_target="tpu_custom_call", output_to_operand_aliasing={{}: (9, {})} | custom-call | flops 671088640 | bytes 3932160 | tf_op jit(solution)/shard_map/finish/pallas_call | solution.py:402
  95.8 3.8 %collective-permute-done.15.rest_0_ = bf16[528,256]{1,0:T(8,128)(2,1)S(1)} collective-permute-done((bf16[528,256]{1,0:T(8,128)(2,1)S(1)}, bf16[528,256]{1,0:T(8,128)(2,1)S(1)}, u32[]{:S(2)}, u32[]{:S(2)}) %collective-permute-start.15) | collective-permute-done | bytes 270368 | tf_op jit(solution)/shard_map/ppermute | solution.py:442
  99.5 1.7 %finish.7.rest_1_ = bf16[2,2,8,2,8,16,512]{6,5,4,3,2,1,0:T(8,128)(2,1)} custom-call(s32[3]{0:T(128)S(1)} %pad_add_fusion.3.places, bf16[256,512]{1,0:T(8,128)(2,1)S(1)} %copy-done.1, f32[1,512]{1,0:T(1,128)S(1)} %bitcast.32, bf16[256,1024]{1,0:T(8,128)(2,1)S(1)} %copy-done, ...), custom_call_target="tpu_custom_call", output_to_operand_aliasing={{}: (5, {})} | custom-call | flops 134217728 | bytes 786432 | tf_op jit(solution)/shard_map/finish/pallas_call | solution.py:402
  101.2 1.7 %finish.8.rest_1_ = bf16[2,2,8,2,8,16,512]{6,5,4,3,2,1,0:T(8,128)(2,1)} custom-call(s32[3]{0:T(128)S(1)} %pad_add_fusion.2.places, bf16[256,512]{1,0:T(8,128)(2,1)S(1)} %copy-done.1, f32[1,512]{1,0:T(1,128)S(1)} %bitcast.33, bf16[256,1024]{1,0:T(8,128)(2,1)S(1)} %copy-done, ...), custom_call_target="tpu_custom_call", output_to_operand_aliasing={{}: (5, {})} | custom-call | flops 134217728 | bytes 786432 | tf_op jit(solution)/shard_map/finish/pallas_call | solution.py:402
  103.0 1.7 %finish.9 = bf16[2,2,8,2,8,16,512]{6,5,4,3,2,1,0:T(8,128)(2,1)} custom-call(s32[3]{0:T(128)S(1)} %pad_add_fusion.places, bf16[256,512]{1,0:T(8,128)(2,1)S(1)} %copy-done.1, f32[1,512]{1,0:T(1,128)S(1)} %bitcast.34, bf16[256,1024]{1,0:T(8,128)(2,1)S(1)} %copy-done, ...), custom_call_target="tpu_custom_call", output_to_operand_aliasing={{}: (5, {})} | custom-call | flops 134217728 | bytes 786432 | tf_op jit(solution)/shard_map/finish/pallas_call | solution.py:402
  (26 shorter events, 0.2 us)
Async XLA Ops:
  0.0 85.8 %copy-start = (bf16[256,1024]{1,0:T(8,128)(2,1)S(1)}, bf16[256,1024]{1,0:T(8,128)(2,1)}, u32[]{:S(2)}) copy-start(bf16[256,1024]{1,0:T(8,128)(2,1)} %constant.73.clone.place) | copy-start | bytes 1572868
  0.0 85.8 %copy-start.1 = (bf16[256,512]{1,0:T(8,128)(2,1)S(1)}, bf16[256,512]{1,0:T(8,128)(2,1)}, u32[]{:S(2)}) copy-start(bf16[256,512]{1,0:T(8,128)(2,1)} %w3.9) | copy-start | bytes 786436
  0.0 85.8 %copy-start.4 = (f32[512]{0:T(512)S(1)}, f32[512]{0:T(512)}, u32[]{:S(2)}) copy-start(f32[512]{0:T(512)} %param.21) | copy-start | bytes 6148
  14.0 6.7 %collective-permute-start = (bf16[528,256]{1,0:T(8,128)(2,1)}, bf16[528,256]{1,0:T(8,128)(2,1)S(1)}, u32[]{:S(2)}, u32[]{:S(2)}) collective-permute-start(bf16[528,256]{1,0:T(8,128)(2,1)} %get-tuple-element.29), channel_id=1, source_target_pairs={{0,1},{1,0},{2,3},{3,2},{4,5},{5,4},{6,7},{7,6},{8,9},{9,8},{10,11... | collective-permute-start | bytes 811016 | tf_op jit(solution)/shard_map/ppermute | solution.py:442
  14.5 6.4 %collective-permute-start.1 = (bf16[528,256]{1,0:T(8,128)(2,1)}, bf16[528,256]{1,0:T(8,128)(2,1)S(1)}, u32[]{:S(2)}, u32[]{:S(2)}) collective-permute-start(bf16[528,256]{1,0:T(8,128)(2,1)} %get-tuple-element.30), channel_id=1, source_target_pairs={{0,1},{1,0},{2,3},{3,2},{4,5},{5,4},{6,7},{7,6},{8,9},{9,8},{10,11... | collective-permute-start | bytes 811016 | tf_op jit(solution)/shard_map/ppermute | solution.py:442
  14.6 24.1 %collective-permute-start.3 = (bf16[528,256]{1,0:T(8,128)(2,1)}, bf16[528,256]{1,0:T(8,128)(2,1)S(1)}, u32[]{:S(2)}, u32[]{:S(2)}) collective-permute-start(bf16[528,256]{1,0:T(8,128)(2,1)} %get-tuple-element.32.rest_2_), channel_id=1, source_target_pairs={{0,18},{1,19},{2,16},{3,17},{4,22},{5,23},{6,20},{7,21},{8,26},{9,... | collective-permute-start | bytes 811016 | tf_op jit(solution)/shard_map/ppermute | solution.py:442
  19.6 24.5 %collective-permute-start.2 = (bf16[528,256]{1,0:T(8,128)(2,1)}, bf16[528,256]{1,0:T(8,128)(2,1)S(1)}, u32[]{:S(2)}, u32[]{:S(2)}) collective-permute-start(bf16[528,256]{1,0:T(8,128)(2,1)} %get-tuple-element.31.rest_0_), channel_id=1, source_target_pairs={{0,16},{1,17},{2,18},{3,19},{4,20},{5,21},{6,22},{7,23},{8,24},{9,... | collective-permute-start | bytes 811016 | tf_op jit(solution)/shard_map/ppermute | solution.py:442
  20.9 1.0 copy-start.2
  21.9 1.0 copy-start.3
  26.2 0.7 copy-start.5
  27.0 0.7 copy-start.6
  27.7 17.8 %collective-permute-start.4 = (bf16[528,256]{1,0:T(8,128)(2,1)}, bf16[528,256]{1,0:T(8,128)(2,1)S(1)}, u32[]{:S(2)}, u32[]{:S(2)}) collective-permute-start(bf16[528,256]{1,0:T(8,128)(2,1)} %get-tuple-element.34), channel_id=1, source_target_pairs={{0,4},{1,5},{2,6},{3,7},{4,0},{5,1},{6,2},{7,3},{8,12},{9,13},{10,... | collective-permute-start | bytes 811016 | tf_op jit(solution)/shard_map/ppermute | solution.py:442
  29.1 20.1 %collective-permute-start.11 = (bf16[528,256]{1,0:T(8,128)(2,1)}, bf16[528,256]{1,0:T(8,128)(2,1)S(1)}, u32[]{:S(2)}, u32[]{:S(2)}) collective-permute-start(bf16[528,256]{1,0:T(8,128)(2,1)} %get-tuple-element.35), channel_id=1, source_target_pairs={{0,8},{1,9},{2,10},{3,11},{4,12},{5,13},{6,14},{7,15},{8,0},{9,1},... | collective-permute-start | bytes 811016 | tf_op jit(solution)/shard_map/ppermute | solution.py:442
  30.7 24.3 %collective-permute-start.12 = (bf16[528,256]{1,0:T(8,128)(2,1)}, bf16[528,256]{1,0:T(8,128)(2,1)S(1)}, u32[]{:S(2)}, u32[]{:S(2)}) collective-permute-start(bf16[528,256]{1,0:T(8,128)(2,1)} %get-tuple-element.36), channel_id=1, source_target_pairs={{0,12},{1,13},{2,14},{3,15},{4,8},{5,9},{6,10},{7,11},{8,4},{9,5},... | collective-permute-start | bytes 811016 | tf_op jit(solution)/shard_map/ppermute | solution.py:442
  38.8 18.4 %collective-permute-start.7 = (bf16[528,256]{1,0:T(8,128)(2,1)}, bf16[528,256]{1,0:T(8,128)(2,1)S(1)}, u32[]{:S(2)}, u32[]{:S(2)}) collective-permute-start(bf16[528,256]{1,0:T(8,128)(2,1)} %get-tuple-element.37), channel_id=1, source_target_pairs={{0,2},{1,3},{2,0},{3,1},{4,6},{5,7},{6,4},{7,5},{8,10},{9,11},{10,... | collective-permute-start | bytes 811016 | tf_op jit(solution)/shard_map/ppermute | solution.py:442
  44.1 16.2 %collective-permute-start.8 = (bf16[528,256]{1,0:T(8,128)(2,1)}, bf16[528,256]{1,0:T(8,128)(2,1)S(1)}, u32[]{:S(2)}, u32[]{:S(2)}) collective-permute-start(bf16[528,256]{1,0:T(8,128)(2,1)} %copy-done.6), channel_id=1, source_target_pairs={{0,6},{1,7},{2,4},{3,5},{4,2},{5,3},{6,0},{7,1},{8,14},{9,15},{10,... | collective-permute-start | bytes 811016 | tf_op jit(solution)/shard_map/ppermute | solution.py:442
  45.5 22.5 %collective-permute-start.9 = (bf16[528,256]{1,0:T(8,128)(2,1)}, bf16[528,256]{1,0:T(8,128)(2,1)S(1)}, u32[]{:S(2)}, u32[]{:S(2)}) collective-permute-start(bf16[528,256]{1,0:T(8,128)(2,1)} %copy-done.5), channel_id=1, source_target_pairs={{0,10},{1,11},{2,8},{3,9},{4,14},{5,15},{6,12},{7,13},{8,2},{9,3},... | collective-permute-start | bytes 811016 | tf_op jit(solution)/shard_map/ppermute | solution.py:442
  49.3 25.5 %collective-permute-start.10 = (bf16[528,256]{1,0:T(8,128)(2,1)S(1)}, bf16[528,256]{1,0:T(8,128)(2,1)S(1)}, u32[]{:S(2)}, u32[]{:S(2)}) collective-permute-start(bf16[528,256]{1,0:T(8,128)(2,1)S(1)} %get-tuple-element.40), channel_id=1, source_target_pairs={{0,14},{1,15},{2,12},{3,13},{4,10},{5,11},{6,8},{7,9},{8,6},{9,7},... | collective-permute-start | bytes 811016 | tf_op jit(solution)/shard_map/ppermute | solution.py:442
  55.1 21.3 %collective-permute-start.5 = (bf16[528,256]{1,0:T(8,128)(2,1)S(1)}, bf16[528,256]{1,0:T(8,128)(2,1)S(1)}, u32[]{:S(2)}, u32[]{:S(2)}) collective-permute-start(bf16[528,256]{1,0:T(8,128)(2,1)S(1)} %collective-permute-done.rest_1_), channel_id=1, source_target_pairs={{0,16},{1,17},{2,18},{3,19},{4,20},{5,21},{6,22},{7,23},{8,24},{9,... | collective-permute-start | bytes 811016 | tf_op jit(solution)/shard_map/ppermute | solution.py:442
  57.2 22.4 %collective-permute-start.6 = (bf16[528,256]{1,0:T(8,128)(2,1)S(1)}, bf16[528,256]{1,0:T(8,128)(2,1)S(1)}, u32[]{:S(2)}, u32[]{:S(2)}) collective-permute-start(bf16[528,256]{1,0:T(8,128)(2,1)S(1)} %collective-permute-done.1.rest_3_), channel_id=1, source_target_pairs={{0,18},{1,19},{2,16},{3,17},{4,22},{5,23},{6,20},{7,21},{8,26},{9,... | collective-permute-start | bytes 811016 | tf_op jit(solution)/shard_map/ppermute | solution.py:442
  60.3 24.2 %collective-permute-start.16 = (bf16[528,256]{1,0:T(8,128)(2,1)S(1)}, bf16[528,256]{1,0:T(8,128)(2,1)S(1)}, u32[]{:S(2)}, u32[]{:S(2)}) collective-permute-start(bf16[528,256]{1,0:T(8,128)(2,1)S(1)} %get-tuple-element.49), channel_id=1, source_target_pairs={{0,4},{1,5},{2,6},{3,7},{4,0},{5,1},{6,2},{7,3},{8,12},{9,13},{10,... | collective-permute-start | bytes 811016 | tf_op jit(solution)/shard_map/ppermute | solution.py:442
  68.0 23.7 %collective-permute-start.17 = (bf16[528,256]{1,0:T(8,128)(2,1)S(1)}, bf16[528,256]{1,0:T(8,128)(2,1)S(1)}, u32[]{:S(2)}, u32[]{:S(2)}) collective-permute-start(bf16[528,256]{1,0:T(8,128)(2,1)S(1)} %get-tuple-element.50), channel_id=1, source_target_pairs={{0,8},{1,9},{2,10},{3,11},{4,12},{5,13},{6,14},{7,15},{8,0},{9,1},... | collective-permute-start | bytes 811016 | tf_op jit(solution)/shard_map/ppermute | solution.py:442
  74.8 16.9 %collective-permute-start.18 = (bf16[528,256]{1,0:T(8,128)(2,1)S(1)}, bf16[528,256]{1,0:T(8,128)(2,1)S(1)}, u32[]{:S(2)}, u32[]{:S(2)}) collective-permute-start(bf16[528,256]{1,0:T(8,128)(2,1)S(1)} %get-tuple-element.51), channel_id=1, source_target_pairs={{0,12},{1,13},{2,14},{3,15},{4,8},{5,9},{6,10},{7,11},{8,4},{9,5},... | collective-permute-start | bytes 811016 | tf_op jit(solution)/shard_map/ppermute | solution.py:442
  82.2 20.7 %collective-permute-start.13 = (bf16[528,256]{1,0:T(8,128)(2,1)S(1)}, bf16[528,256]{1,0:T(8,128)(2,1)S(1)}, u32[]{:S(2)}, u32[]{:S(2)}) collective-permute-start(bf16[528,256]{1,0:T(8,128)(2,1)S(1)} %get-tuple-element.45), channel_id=1, source_target_pairs={{0,12},{1,13},{2,14},{3,15},{4,8},{5,9},{6,10},{7,11},{8,4},{9,5},... | collective-permute-start | bytes 811016 | tf_op jit(solution)/shard_map/ppermute | solution.py:442
  84.5 16.8 %collective-permute-start.14 = (bf16[528,256]{1,0:T(8,128)(2,1)S(1)}, bf16[528,256]{1,0:T(8,128)(2,1)S(1)}, u32[]{:S(2)}, u32[]{:S(2)}) collective-permute-start(bf16[528,256]{1,0:T(8,128)(2,1)S(1)} %get-tuple-element.46), channel_id=1, source_target_pairs={{0,8},{1,9},{2,10},{3,11},{4,12},{5,13},{6,14},{7,15},{8,0},{9,1},... | collective-permute-start | bytes 811016 | tf_op jit(solution)/shard_map/ppermute | solution.py:442
  84.5 15.1 %collective-permute-start.15 = (bf16[528,256]{1,0:T(8,128)(2,1)S(1)}, bf16[528,256]{1,0:T(8,128)(2,1)S(1)}, u32[]{:S(2)}, u32[]{:S(2)}) collective-permute-start(bf16[528,256]{1,0:T(8,128)(2,1)S(1)} %get-tuple-element.47), channel_id=1, source_target_pairs={{0,4},{1,5},{2,6},{3,7},{4,0},{5,1},{6,2},{7,3},{8,12},{9,13},{10,... | collective-permute-start | bytes 811016 | tf_op jit(solution)/shard_map/ppermute | solution.py:442

commit v4 on v3

--- a/solution.py
+++ b/solution.py
@@ -271,19 +271,17 @@
 
 def pack_kernel(ints, *rest, half, jobs, pick, owned, share):
     arrays = sum(len(job) for job in jobs)
-    held, outs = rest[:arrays], rest[arrays : arrays + len(jobs) * half]
-    notes, ready, note_sem, block_sem, out_sem = rest[arrays + len(jobs) * half :]
+    held, outs = rest[:arrays], rest[arrays:]
     me = lax.axis_index("patch").astype(jnp.int32)
     node = lax.axis_index("clip").astype(jnp.int32)
     owners = len(jobs[0])
     body = owned * share
-    waits = []
-    for k in range(owners):
-        copy = pltpu.make_async_copy(held[k].at[pl.ds(body, TILE)], notes.at[pl.ds(k * TILE, TILE)], note_sem.at[k])
-        copy.start()
-        waits.append(copy)
-    blocks, picks = [], []
+    notes = jnp.concatenate([held[k][body : body + TILE, :] for k in range(owners)], axis=0)
+    width = owners * TILE
+    rows = lax.broadcasted_iota(jnp.int32, (TILE, width), 0)
+    columns = lax.broadcasted_iota(jnp.int32, (TILE, width), 1)
     for s in range(half):
+        sel = jnp.zeros((TILE, width), jnp.bool_)
         for j in range(owners):
             seen = jnp.int32(0)
             found = [jnp.int32(0)] * CAP
@@ -293,42 +291,16 @@
                     found[r] = jnp.where(mine & (seen == r), i, found[r])
                 seen = seen + mine.astype(jnp.int32)
             for r in range(CAP):
-                clip = found[r]
                 row = pick(me ^ jobs[0][j]) * CAP + r
-                to = pl.multiple_of(row * share, share)
-                start = pl.multiple_of(clip * share, share)
-                picks.append((jnp.where(seen > r, row, -1), clip))
+                to = pl.ds(pl.multiple_of(row * share, share), share)
+                at = pl.ds(pl.multiple_of(found[r] * share, share), share)
+                sel = sel | ((rows == jnp.where(seen > r, row, -1)) & (columns == j * TILE + found[r]))
                 for g in range(len(jobs)):
-                    copy = pltpu.make_async_copy(
-                        held[g * owners + j].at[pl.ds(start, share)],
-                        outs[g * half + s].at[pl.ds(to, share)],
-                        block_sem.at[len(blocks)],
-                    )
-                    copy.start()
-                    blocks.append(copy)
-    for copy in waits:
-        copy.wait()
-    width = owners * TILE
-    rows = lax.broadcasted_iota(jnp.int32, (TILE, width), 0)
-    columns = lax.broadcasted_iota(jnp.int32, (TILE, width), 1)
-    for s in range(half):
-        sel = jnp.zeros((TILE, width), jnp.bool_)
-        for j in range(owners):
-            for r in range(CAP):
-                row, clip = picks[(s * owners + j) * CAP + r]
-                sel = sel | ((rows == row) & (columns == j * TILE + clip))
+                    outs[g * half + s][to, :] = held[g * owners + j][at, :]
         sel = jnp.where(sel, 1.0, 0.0).astype(BF16)
-        ready[s] = jnp.dot(sel, notes[...], preferred_element_type=F32).astype(BF16)
-    for s in range(half):
+        ready = jnp.dot(sel, notes, preferred_element_type=F32).astype(BF16)
         for g in range(len(jobs)):
-            k = g * half + s
-            copy = pltpu.make_async_copy(
-                ready.at[s], outs[k].at[pl.ds(owners * CAP * share, TILE)], out_sem.at[k]
-            )
-            copy.start()
-            blocks.append(copy)
-    for copy in blocks:
-        copy.wait()
+            outs[g * half + s][owners * CAP * share :, :] = ready
 
 
 def pack(half, held, jobs, pick, owned, share):
@@ -336,27 +308,18 @@
     names = [h[owned * share, NAMES : NAMES + owned] for h in held[:owners]]
     ints = jnp.concatenate(names).astype(jnp.int32)
     out_rows = owners * CAP * share + TILE
-    anywhere = pl.BlockSpec(memory_space=pl.ANY)
     count = len(jobs) * half
-    copies = count * owners * CAP
     outs = pl.pallas_call(
         functools.partial(pack_kernel, half=half, jobs=jobs, pick=pick, owned=owned, share=share),
         grid_spec=pltpu.PrefetchScalarGridSpec(
             num_scalar_prefetch=1,
             grid=(1,),
-            in_specs=[anywhere] * len(held),
-            out_specs=[anywhere] * count,
-            scratch_shapes=[
-                pltpu.VMEM((owners * TILE, channels), BF16),
-                pltpu.VMEM((half, TILE, channels), BF16),
-                pltpu.SemaphoreType.DMA((owners,)),
-                pltpu.SemaphoreType.DMA((copies,)),
-                pltpu.SemaphoreType.DMA((count,)),
-            ],
+            in_specs=[pl.BlockSpec(h.shape, lambda i, s: (0, 0)) for h in held],
+            out_specs=[pl.BlockSpec((out_rows, channels), lambda i, s: (0, 0))] * count,
         ),
         out_shape=[jax.ShapeDtypeStruct((out_rows, channels), BF16)] * count,
-        compiler_params=pltpu.CompilerParams(vmem_limit_bytes=8 * 1024 * 1024),
-        cost_estimate=pl.CostEstimate(flops=0, bytes_accessed=2 * copies * share * channels, transcendentals=0),
+        compiler_params=pltpu.CompilerParams(vmem_limit_bytes=16 * 1024 * 1024),
+        cost_estimate=pl.CostEstimate(flops=0, bytes_accessed=2 * count * out_rows * channels, transcendentals=0),
         name="pack",
     )(ints, *held)
     return [outs[g * half : (g + 1) * half] for g in range(len(jobs))]
@@ -445,28 +408,25 @@
     held = [sends[0::2], [send(array, 0, 1) for array in sends[1::2]]]
     pairs = [[held[0][k], held[1][k]] for k in range(lines)]
     own = pack(half, [a for pair in pairs for a in pair], [[0, 1]] * lines, lambda p: p % 2, owned, share)
+    def after(arrays, *earlier):
+        return list(lax.optimization_barrier((*arrays, *earlier))[: len(arrays)])
+
     crossed = [send(held[0][k], half, 2 * k) for k in range(lines)]
     arrived = [[send(own[k][s], s, 2 * k) for s in range(half)] for k in range(lines)]
     pieces = [((me // 2) ^ k, 0, node ^ s, arrived[k][s]) for k in range(lines) for s in range(half)]
-    def after(arrays, *earlier):
-        return lax.optimization_barrier((*arrays, *earlier))[: len(arrays)]
-
-    spread = [a for line in arrived[1:] for a in line]
     beyond = after(held[1], *crossed, *[a for line in own for a in line], arrived[0][1])
     beyond = [send(beyond[k], half, 2 * k) for k in range(lines)]
     early, late = [], []
     for b, far in enumerate((crossed, beyond)):
         if b:
-            far = after(far, *spread, *arrived[0])
-        (other,) = pack(half, list(far), [[2 * k + b for k in range(lines)]], lambda p: p // 2, owned, share)
-        seconds = [send(other[s], s, 0) for s in range(half)]
-        arrivals = [(0, (me % 2) ^ b, node ^ half ^ s, seconds[s]) for s in range(half)]
+            far = after(far, *[a for line in arrived[1:] for a in line], *arrived[0])
+        (other,) = pack(half, far, [[2 * k + b for k in range(lines)]], lambda p: p // 2, owned, share)
+        arrivals = [(0, (me % 2) ^ b, node ^ half ^ s, send(other[s], s, 0)) for s in range(half)]
         early += arrivals if b == 0 else arrivals[:1]
         late = arrivals[1:]
     latents = finish(pieces, (1, 2), w3, g3, shape)
     latents = finish(early, (lines, 1), w3, g3, shape, latents)
-    for piece in late:
-        latents = finish([piece], (lines, 1), w3, g3, shape, latents)
+    latents = finish(late, (lines, 1), w3, g3, shape, latents)
     return latents.reshape(shares * nodes * CAP, latent, places // shares, c3)
 
 

time: 105 us -> 101 us (0.962)
  Pallas kernels: 37.4 us -> 33.2 us
  starting transfers between devices: 22.3 us -> 24.1 us
    pallas_call x3, Pallas kernels: 8.36 us -> 4.06 us  [pack(): pl.pallas_call(functools.partial(pack_kernel, half=half, jobs=jobs, pick=...]
    ppermute x19, starting transfers between devices: 22.3 us -> 24.1 us  [send(): return lax.ppermute(array, ('clip', 'patch'), pairs)]
    pallas_call x5 -> x3, Pallas kernels: 15 us -> 15.2 us  [finish(): pl.pallas_call(functools.partial(finish_kernel, count=count), grid_spec=p...]
  transfers between devices with their start and end apart: 19 -> 19, of which waited for: 9 -> 9; matrix products, arithmetic and copies ran while one was open for 2% -> 2% of each run, Pallas kernels for 21% -> 15%
where the time goes in v4:
time: 101 us
  waiting for transfers between devices  39.6 us (39%)
  Pallas kernels  33.2 us (33%)
  starting transfers between devices  24.1 us (24%)
  local copies, waits for them, and re-layouts  3.99 us (4%)
    ppermute x19, waiting for transfers between devices, send(): return lax.ppermute(array, ('clip', 'patch'), pairs)  39.6 us
    ppermute x19, starting transfers between devices, send(): return lax.ppermute(array, ('clip', 'patch'), pairs)  24.1 us
    pallas_call x3, Pallas kernels, finish(): pl.pallas_call(functools.partial(finish_kernel, count=count), grid_spec=p...  15.2 us
    pallas_call x1, Pallas kernels, encode(): pl.pallas_call(functools.partial(encode_kernel, starts=starts, shares=sha...  14 us
    pallas_call x3, Pallas kernels, pack(): pl.pallas_call(functools.partial(pack_kernel, half=half, jobs=jobs, pick=...  4.06 us
    unnamed x14, local copies, waits for them, and re-layouts  2.63 us
  transfers between devices with their start and end apart: 19, of which 9 were waited for; matrix products, arithmetic and copies ran while one was open for 2% of the time, Pallas kernels for 15%

profile of v4, /device:TPU:0, one launch (start us, length us, event | category | flops | bytes accessed | tf_op | source)
XLA Modules:
  0.0 101.2 jit_solution(6542806562770191617)
XLA Ops:
  0.0 14.0 %encode.1 = (bf16[528,256]{1,0:T(8,128)(2,1)}, bf16[528,256]{1,0:T(8,128)(2,1)}, bf16[528,256]{1,0:T(8,128)(2,1)}, bf16[528,256]{1,0:T(8,128)(2,1)}) custom-call(s32[4]{0:T(128)} %bitcast.35, bf16[4,16,64,384]{3,2,1,0:T(8,128)(2,1)} %x.1, bf16[384,128]{1,0:T(8,128)(2,1)} %rest_0_.1, f32[1,128]{1,0:T(1,128)} %bitcast.36, bf16[3,1152,256]{2,1,0:T(8,128)(2,1)} %bitcast.33, ...), custom_call_target="tpu_custom_call" | custom-call | flops 4563402752 | bytes 3145728 | tf_op jit(solution)/shard_map/encode/pallas_call | solution.py:247
  14.0 0.5 collective-permute-start
  14.5 0.1 collective-permute-start.1
  14.6 5.0 %collective-permute-start.3 = (bf16[528,256]{1,0:T(8,128)(2,1)}, bf16[528,256]{1,0:T(8,128)(2,1)S(1)}, u32[]{:S(2)}, u32[]{:S(2)}) collective-permute-start(bf16[528,256]{1,0:T(8,128)(2,1)} %get-tuple-element.32.rest_2_), channel_id=1, source_target_pairs={{0,18},{1,19},{2,16},{3,17},{4,22},{5,23},{6,20},{7,21},{8,26},{9,... | collective-permute-start | bytes 811016 | tf_op jit(solution)/shard_map/ppermute | solution.py:405
  19.6 0.3 collective-permute-start.2
  19.9 0.8 slice_bitcast_fusion.5
  20.7 0.0 collective-permute-done.rest_1_
  20.7 0.1 slice_bitcast_fusion.2
  20.8 0.1 maximum_convert_fusion.ints
  20.9 0.0 collective-permute-done.1.rest_3_
  20.9 1.0 copy-done.2
  21.8 1.0 copy-done.3
  22.8 0.8 pack.3
  23.6 1.5 %collective-permute-start.4 = (bf16[528,256]{1,0:T(8,128)(2,1)S(1)}, bf16[528,256]{1,0:T(8,128)(2,1)S(1)}, u32[]{:S(2)}, u32[]{:S(2)}) collective-permute-start(bf16[528,256]{1,0:T(8,128)(2,1)S(1)} %get-tuple-element.34), channel_id=1, source_target_pairs={{0,4},{1,5},{2,6},{3,7},{4,0},{5,1},{6,2},{7,3},{8,12},{9,13},{10,... | collective-permute-start | bytes 811016 | tf_op jit(solution)/shard_map/ppermute | solution.py:405
  25.1 1.6 %collective-permute-start.11 = (bf16[528,256]{1,0:T(8,128)(2,1)S(1)}, bf16[528,256]{1,0:T(8,128)(2,1)S(1)}, u32[]{:S(2)}, u32[]{:S(2)}) collective-permute-start(bf16[528,256]{1,0:T(8,128)(2,1)S(1)} %get-tuple-element.35), channel_id=1, source_target_pairs={{0,8},{1,9},{2,10},{3,11},{4,12},{5,13},{6,14},{7,15},{8,0},{9,1},... | collective-permute-start | bytes 811016 | tf_op jit(solution)/shard_map/ppermute | solution.py:405
  26.7 0.4 collective-permute-start.12
  27.1 11.7 %collective-permute-done.3.rest_1_ = bf16[528,256]{1,0:T(8,128)(2,1)S(1)} collective-permute-done((bf16[528,256]{1,0:T(8,128)(2,1)}, bf16[528,256]{1,0:T(8,128)(2,1)S(1)}, u32[]{:S(2)}, u32[]{:S(2)}) %collective-permute-start.3) | collective-permute-done | bytes 270368 | tf_op jit(solution)/shard_map/ppermute | solution.py:405
  38.8 1.8 %collective-permute-start.7 = (bf16[528,256]{1,0:T(8,128)(2,1)S(1)}, bf16[528,256]{1,0:T(8,128)(2,1)S(1)}, u32[]{:S(2)}, u32[]{:S(2)}) collective-permute-start(bf16[528,256]{1,0:T(8,128)(2,1)S(1)} %get-tuple-element.37), channel_id=1, source_target_pairs={{0,2},{1,3},{2,0},{3,1},{4,6},{5,7},{6,4},{7,5},{8,10},{9,11},{10,... | collective-permute-start | bytes 811016 | tf_op jit(solution)/shard_map/ppermute | solution.py:405
  40.6 0.1 slice_bitcast_fusion
  40.7 3.4 %collective-permute-done.2.rest_0_ = bf16[528,256]{1,0:T(8,128)(2,1)S(1)} collective-permute-done((bf16[528,256]{1,0:T(8,128)(2,1)}, bf16[528,256]{1,0:T(8,128)(2,1)S(1)}, u32[]{:S(2)}, u32[]{:S(2)}) %collective-permute-start.2) | collective-permute-done | bytes 270368 | tf_op jit(solution)/shard_map/ppermute | solution.py:405
  44.0 1.4 %collective-permute-start.8 = (bf16[528,256]{1,0:T(8,128)(2,1)S(1)}, bf16[528,256]{1,0:T(8,128)(2,1)S(1)}, u32[]{:S(2)}, u32[]{:S(2)}) collective-permute-start(bf16[528,256]{1,0:T(8,128)(2,1)S(1)} %get-tuple-element.38), channel_id=1, source_target_pairs={{0,6},{1,7},{2,4},{3,5},{4,2},{5,3},{6,0},{7,1},{8,14},{9,15},{10,... | collective-permute-start | bytes 811016 | tf_op jit(solution)/shard_map/ppermute | solution.py:405
  45.5 1.7 %collective-permute-start.9 = (bf16[528,256]{1,0:T(8,128)(2,1)S(1)}, bf16[528,256]{1,0:T(8,128)(2,1)S(1)}, u32[]{:S(2)}, u32[]{:S(2)}) collective-permute-start(bf16[528,256]{1,0:T(8,128)(2,1)S(1)} %get-tuple-element.39), channel_id=1, source_target_pairs={{0,10},{1,11},{2,8},{3,9},{4,14},{5,15},{6,12},{7,13},{8,2},{9,3},... | collective-permute-start | bytes 811016 | tf_op jit(solution)/shard_map/ppermute | solution.py:405
  47.2 1.2 %collective-permute-start.10 = (bf16[528,256]{1,0:T(8,128)(2,1)S(1)}, bf16[528,256]{1,0:T(8,128)(2,1)S(1)}, u32[]{:S(2)}, u32[]{:S(2)}) collective-permute-start(bf16[528,256]{1,0:T(8,128)(2,1)S(1)} %get-tuple-element.40), channel_id=1, source_target_pairs={{0,14},{1,15},{2,12},{3,13},{4,10},{5,11},{6,8},{7,9},{8,6},{9,7},... | collective-permute-start | bytes 811016 | tf_op jit(solution)/shard_map/ppermute | solution.py:405
  48.4 1.6 %collective-permute-done.12.rest_3_ = bf16[528,256]{1,0:T(8,128)(2,1)S(1)} collective-permute-done((bf16[528,256]{1,0:T(8,128)(2,1)S(1)}, bf16[528,256]{1,0:T(8,128)(2,1)S(1)}, u32[]{:S(2)}, u32[]{:S(2)}) %collective-permute-start.12) | collective-permute-done | bytes 270368 | tf_op jit(solution)/shard_map/ppermute | solution.py:405
  50.0 3.1 %collective-permute-start.5 = (bf16[528,256]{1,0:T(8,128)(2,1)S(1)}, bf16[528,256]{1,0:T(8,128)(2,1)S(1)}, u32[]{:S(2)}, u32[]{:S(2)}) collective-permute-start(bf16[528,256]{1,0:T(8,128)(2,1)S(1)} %collective-permute-done.rest_1_), channel_id=1, source_target_pairs={{0,16},{1,17},{2,18},{3,19},{4,20},{5,21},{6,22},{7,23},{8,24},{9,... | collective-permute-start | bytes 811016 | tf_op jit(solution)/shard_map/ppermute | solution.py:405
  53.1 0.1 slice_bitcast_fusion.1
  53.2 0.1 maximum_convert_fusion.2.ints
  53.3 1.6 %pack.5 = (bf16[528,256]{1,0:T(8,128)(2,1)S(1)}, bf16[528,256]{1,0:T(8,128)(2,1)S(1)}, bf16[528,256]{1,0:T(8,128)(2,1)}, bf16[528,256]{1,0:T(8,128)(2,1)}) custom-call(s32[8]{0:T(128)S(1)} %maximum_convert_fusion.2.ints, bf16[528,256]{1,0:T(8,128)(2,1)S(1)} %collective-permute-done.2.rest_0_, bf16[528,256]{1,0:T(8,128)(2,1)S(1)} %collective-permute-done.3.rest_1_), custom_call_target="tpu_custom_call" | custom-call | bytes 1081344 | tf_op jit(solution)/shard_map/pack/pallas_call | solution.py:312
  54.9 2.5 %collective-permute-done.8.rest_5_ = bf16[528,256]{1,0:T(8,128)(2,1)S(1)} collective-permute-done((bf16[528,256]{1,0:T(8,128)(2,1)S(1)}, bf16[528,256]{1,0:T(8,128)(2,1)S(1)}, u32[]{:S(2)}, u32[]{:S(2)}) %collective-permute-start.8) | collective-permute-done | bytes 270368 | tf_op jit(solution)/shard_map/ppermute | solution.py:405
  57.3 1.9 %collective-permute-start.16 = (bf16[528,256]{1,0:T(8,128)(2,1)S(1)}, bf16[528,256]{1,0:T(8,128)(2,1)S(1)}, u32[]{:S(2)}, u32[]{:S(2)}) collective-permute-start(bf16[528,256]{1,0:T(8,128)(2,1)S(1)} %get-tuple-element.49), channel_id=1, source_target_pairs={{0,4},{1,5},{2,6},{3,7},{4,0},{5,1},{6,2},{7,3},{8,12},{9,13},{10,... | collective-permute-start | bytes 811016 | tf_op jit(solution)/shard_map/ppermute | solution.py:405
  59.2 8.4 %collective-permute-done.9.rest_6_ = bf16[528,256]{1,0:T(8,128)(2,1)S(1)} collective-permute-done((bf16[528,256]{1,0:T(8,128)(2,1)S(1)}, bf16[528,256]{1,0:T(8,128)(2,1)S(1)}, u32[]{:S(2)}, u32[]{:S(2)}) %collective-permute-start.9) | collective-permute-done | bytes 270368 | tf_op jit(solution)/shard_map/ppermute | solution.py:405
  67.6 6.0 %collective-permute-done.10.rest_7_ = bf16[528,256]{1,0:T(8,128)(2,1)S(1)} collective-permute-done((bf16[528,256]{1,0:T(8,128)(2,1)S(1)}, bf16[528,256]{1,0:T(8,128)(2,1)S(1)}, u32[]{:S(2)}, u32[]{:S(2)}) %collective-permute-start.10) | collective-permute-done | bytes 270368 | tf_op jit(solution)/shard_map/ppermute | solution.py:405
  73.7 1.3 %collective-permute-done.6.rest_1_ = bf16[528,256]{1,0:T(8,128)(2,1)S(1)} collective-permute-done((bf16[528,256]{1,0:T(8,128)(2,1)S(1)}, bf16[528,256]{1,0:T(8,128)(2,1)S(1)}, u32[]{:S(2)}, u32[]{:S(2)}) %collective-permute-start.6) | collective-permute-done | bytes 270368 | tf_op jit(solution)/shard_map/ppermute | solution.py:405
  75.0 0.1 slice_bitcast_fusion.3
  75.1 0.1 maximum_convert_fusion.1.ints
  75.2 1.6 %pack.4 = (bf16[528,256]{1,0:T(8,128)(2,1)S(1)}, bf16[528,256]{1,0:T(8,128)(2,1)}, bf16[528,256]{1,0:T(8,128)(2,1)}, bf16[528,256]{1,0:T(8,128)(2,1)}) custom-call(s32[8]{0:T(128)S(1)} %maximum_convert_fusion.1.ints, bf16[528,256]{1,0:T(8,128)(2,1)S(1)} %collective-permute-done.5.rest_0_, bf16[528,256]{1,0:T(8,128)(2,1)S(1)} %collective-permute-done.6.rest_1_), custom_call_target="tpu_custom_call" | custom-call | bytes 1081344 | tf_op jit(solution)/shard_map/pack/pallas_call | solution.py:312
  76.8 0.7 copy-done.4
  77.5 0.6 collective-permute-start.13
  78.1 2.2 %collective-permute-start.14 = (bf16[528,256]{1,0:T(8,128)(2,1)}, bf16[528,256]{1,0:T(8,128)(2,1)}, u32[]{:S(2)}, u32[]{:S(2)}) collective-permute-start(bf16[528,256]{1,0:T(8,128)(2,1)} %get-tuple-element.46), channel_id=1, source_target_pairs={{0,8},{1,9},{2,10},{3,11},{4,12},{5,13},{6,14},{7,15},{8,0},{9,1},... | collective-permute-start | bytes 811016 | tf_op jit(solution)/shard_map/ppermute | solution.py:405
  80.3 0.7 collective-permute-start.15
  81.0 0.1 stack.34.places
  81.1 0.1 stack.72.places
  81.2 0.1 stack.79.places
  81.3 6.0 %finish.3.rest_5_ = bf16[2,2,8,2,8,16,512]{6,5,4,3,2,1,0:T(8,128)(2,1)} custom-call(s32[24]{0:T(128)S(1)} %stack.79.places, bf16[256,512]{1,0:T(8,128)(2,1)S(1)} %copy-done.1, f32[1,512]{1,0:T(1,128)S(1)} %bitcast.30, bf16[256,1024]{1,0:T(8,128)(2,1)S(1)} %copy-done, bf16[528,256]{1,0:T(8,128)(2,1)S(1)} %get-tuple-element.33.rest_0_, ...), custom_call_target="tpu_custom_call" | custom-call | flops 1073741824 | bytes 6291456 | tf_op jit(solution)/shard_map/finish/pallas_call | solution.py:365
  87.3 5.2 %finish.4.rest_3_ = bf16[2,2,8,2,8,16,512]{6,5,4,3,2,1,0:T(8,128)(2,1)} custom-call(s32[15]{0:T(128)S(1)} %stack.72.places, bf16[256,512]{1,0:T(8,128)(2,1)S(1)} %copy-done.1, f32[1,512]{1,0:T(1,128)S(1)} %bitcast.31, bf16[256,1024]{1,0:T(8,128)(2,1)S(1)} %copy-done, bf16[528,256]{1,0:T(8,128)(2,1)S(1)} %get-tuple-element.48.rest_0_, ...), custom_call_target="tpu_custom_call", output_to_operand_aliasing={{}: (9, {})} | custom-call | flops 671088640 | bytes 3932160 | tf_op jit(solution)/shard_map/finish/pallas_call | solution.py:365
  92.5 0.1 collective-permute-done.14.rest_1_
  92.5 4.7 %collective-permute-done.15.rest_2_ = bf16[528,256]{1,0:T(8,128)(2,1)} collective-permute-done((bf16[528,256]{1,0:T(8,128)(2,1)}, bf16[528,256]{1,0:T(8,128)(2,1)}, u32[]{:S(2)}, u32[]{:S(2)}) %collective-permute-start.15) | collective-permute-done | bytes 270368 | tf_op jit(solution)/shard_map/ppermute | solution.py:405
  97.2 4.0 %finish.5 = bf16[2,2,8,2,8,16,512]{6,5,4,3,2,1,0:T(8,128)(2,1)} custom-call(s32[9]{0:T(128)S(1)} %stack.34.places, bf16[256,512]{1,0:T(8,128)(2,1)S(1)} %copy-done.1, f32[1,512]{1,0:T(1,128)S(1)} %bitcast.32, bf16[256,1024]{1,0:T(8,128)(2,1)S(1)} %copy-done, bf16[528,256]{1,0:T(8,128)(2,1)} %collective-permute-done.13.rest_0_, ...), custom_call_target="tpu_custom_call", output_to_operand_aliasing={{}: (7, {})} | custom-call | flops 402653184 | bytes 2359296 | tf_op jit(solution)/shard_map/finish/pallas_call | solution.py:365
  (22 shorter events, 0.0 us)
Async XLA Ops:
  0.0 81.3 %copy-start = (bf16[256,1024]{1,0:T(8,128)(2,1)S(1)}, bf16[256,1024]{1,0:T(8,128)(2,1)}, u32[]{:S(2)}) copy-start(bf16[256,1024]{1,0:T(8,128)(2,1)} %constant.73.clone.place) | copy-start | bytes 1572868
  0.0 81.3 %copy-start.1 = (bf16[256,512]{1,0:T(8,128)(2,1)S(1)}, bf16[256,512]{1,0:T(8,128)(2,1)}, u32[]{:S(2)}) copy-start(bf16[256,512]{1,0:T(8,128)(2,1)} %w3.5) | copy-start | bytes 786436
  0.0 81.3 %copy-start.6 = (f32[512]{0:T(512)S(1)}, f32[512]{0:T(512)}, u32[]{:S(2)}) copy-start(f32[512]{0:T(512)} %param.19) | copy-start | bytes 6148
  14.0 6.7 %collective-permute-start = (bf16[528,256]{1,0:T(8,128)(2,1)}, bf16[528,256]{1,0:T(8,128)(2,1)S(1)}, u32[]{:S(2)}, u32[]{:S(2)}) collective-permute-start(bf16[528,256]{1,0:T(8,128)(2,1)} %get-tuple-element.29), channel_id=1, source_target_pairs={{0,1},{1,0},{2,3},{3,2},{4,5},{5,4},{6,7},{7,6},{8,9},{9,8},{10,11... | collective-permute-start | bytes 811016 | tf_op jit(solution)/shard_map/ppermute | solution.py:405
  14.5 6.3 %collective-permute-start.1 = (bf16[528,256]{1,0:T(8,128)(2,1)}, bf16[528,256]{1,0:T(8,128)(2,1)S(1)}, u32[]{:S(2)}, u32[]{:S(2)}) collective-permute-start(bf16[528,256]{1,0:T(8,128)(2,1)} %get-tuple-element.30), channel_id=1, source_target_pairs={{0,1},{1,0},{2,3},{3,2},{4,5},{5,4},{6,7},{7,6},{8,9},{9,8},{10,11... | collective-permute-start | bytes 811016 | tf_op jit(solution)/shard_map/ppermute | solution.py:405
  14.6 24.1 %collective-permute-start.3 = (bf16[528,256]{1,0:T(8,128)(2,1)}, bf16[528,256]{1,0:T(8,128)(2,1)S(1)}, u32[]{:S(2)}, u32[]{:S(2)}) collective-permute-start(bf16[528,256]{1,0:T(8,128)(2,1)} %get-tuple-element.32.rest_2_), channel_id=1, source_target_pairs={{0,18},{1,19},{2,16},{3,17},{4,22},{5,23},{6,20},{7,21},{8,26},{9,... | collective-permute-start | bytes 811016 | tf_op jit(solution)/shard_map/ppermute | solution.py:405
  19.6 24.5 %collective-permute-start.2 = (bf16[528,256]{1,0:T(8,128)(2,1)}, bf16[528,256]{1,0:T(8,128)(2,1)S(1)}, u32[]{:S(2)}, u32[]{:S(2)}) collective-permute-start(bf16[528,256]{1,0:T(8,128)(2,1)} %get-tuple-element.31.rest_0_), channel_id=1, source_target_pairs={{0,16},{1,17},{2,18},{3,19},{4,20},{5,21},{6,22},{7,23},{8,24},{9,... | collective-permute-start | bytes 811016 | tf_op jit(solution)/shard_map/ppermute | solution.py:405
  20.9 1.0 copy-start.2
  21.8 1.0 copy-start.3
  23.6 21.9 %collective-permute-start.4 = (bf16[528,256]{1,0:T(8,128)(2,1)S(1)}, bf16[528,256]{1,0:T(8,128)(2,1)S(1)}, u32[]{:S(2)}, u32[]{:S(2)}) collective-permute-start(bf16[528,256]{1,0:T(8,128)(2,1)S(1)} %get-tuple-element.34), channel_id=1, source_target_pairs={{0,4},{1,5},{2,6},{3,7},{4,0},{5,1},{6,2},{7,3},{8,12},{9,13},{10,... | collective-permute-start | bytes 811016 | tf_op jit(solution)/shard_map/ppermute | solution.py:405
  25.1 22.1 %collective-permute-start.11 = (bf16[528,256]{1,0:T(8,128)(2,1)S(1)}, bf16[528,256]{1,0:T(8,128)(2,1)S(1)}, u32[]{:S(2)}, u32[]{:S(2)}) collective-permute-start(bf16[528,256]{1,0:T(8,128)(2,1)S(1)} %get-tuple-element.35), channel_id=1, source_target_pairs={{0,8},{1,9},{2,10},{3,11},{4,12},{5,13},{6,14},{7,15},{8,0},{9,1},... | collective-permute-start | bytes 811016 | tf_op jit(solution)/shard_map/ppermute | solution.py:405
  26.7 23.3 %collective-permute-start.12 = (bf16[528,256]{1,0:T(8,128)(2,1)S(1)}, bf16[528,256]{1,0:T(8,128)(2,1)S(1)}, u32[]{:S(2)}, u32[]{:S(2)}) collective-permute-start(bf16[528,256]{1,0:T(8,128)(2,1)S(1)} %get-tuple-element.36), channel_id=1, source_target_pairs={{0,12},{1,13},{2,14},{3,15},{4,8},{5,9},{6,10},{7,11},{8,4},{9,5},... | collective-permute-start | bytes 811016 | tf_op jit(solution)/shard_map/ppermute | solution.py:405
  38.8 14.4 %collective-permute-start.7 = (bf16[528,256]{1,0:T(8,128)(2,1)S(1)}, bf16[528,256]{1,0:T(8,128)(2,1)S(1)}, u32[]{:S(2)}, u32[]{:S(2)}) collective-permute-start(bf16[528,256]{1,0:T(8,128)(2,1)S(1)} %get-tuple-element.37), channel_id=1, source_target_pairs={{0,2},{1,3},{2,0},{3,1},{4,6},{5,7},{6,4},{7,5},{8,10},{9,11},{10,... | collective-permute-start | bytes 811016 | tf_op jit(solution)/shard_map/ppermute | solution.py:405
  44.0 13.3 %collective-permute-start.8 = (bf16[528,256]{1,0:T(8,128)(2,1)S(1)}, bf16[528,256]{1,0:T(8,128)(2,1)S(1)}, u32[]{:S(2)}, u32[]{:S(2)}) collective-permute-start(bf16[528,256]{1,0:T(8,128)(2,1)S(1)} %get-tuple-element.38), channel_id=1, source_target_pairs={{0,6},{1,7},{2,4},{3,5},{4,2},{5,3},{6,0},{7,1},{8,14},{9,15},{10,... | collective-permute-start | bytes 811016 | tf_op jit(solution)/shard_map/ppermute | solution.py:405
  45.5 22.1 %collective-permute-start.9 = (bf16[528,256]{1,0:T(8,128)(2,1)S(1)}, bf16[528,256]{1,0:T(8,128)(2,1)S(1)}, u32[]{:S(2)}, u32[]{:S(2)}) collective-permute-start(bf16[528,256]{1,0:T(8,128)(2,1)S(1)} %get-tuple-element.39), channel_id=1, source_target_pairs={{0,10},{1,11},{2,8},{3,9},{4,14},{5,15},{6,12},{7,13},{8,2},{9,3},... | collective-permute-start | bytes 811016 | tf_op jit(solution)/shard_map/ppermute | solution.py:405
  47.2 26.5 %collective-permute-start.10 = (bf16[528,256]{1,0:T(8,128)(2,1)S(1)}, bf16[528,256]{1,0:T(8,128)(2,1)S(1)}, u32[]{:S(2)}, u32[]{:S(2)}) collective-permute-start(bf16[528,256]{1,0:T(8,128)(2,1)S(1)} %get-tuple-element.40), channel_id=1, source_target_pairs={{0,14},{1,15},{2,12},{3,13},{4,10},{5,11},{6,8},{7,9},{8,6},{9,7},... | collective-permute-start | bytes 811016 | tf_op jit(solution)/shard_map/ppermute | solution.py:405
  50.0 23.6 %collective-permute-start.5 = (bf16[528,256]{1,0:T(8,128)(2,1)S(1)}, bf16[528,256]{1,0:T(8,128)(2,1)S(1)}, u32[]{:S(2)}, u32[]{:S(2)}) collective-permute-start(bf16[528,256]{1,0:T(8,128)(2,1)S(1)} %collective-permute-done.rest_1_), channel_id=1, source_target_pairs={{0,16},{1,17},{2,18},{3,19},{4,20},{5,21},{6,22},{7,23},{8,24},{9,... | collective-permute-start | bytes 811016 | tf_op jit(solution)/shard_map/ppermute | solution.py:405
  53.1 21.9 %collective-permute-start.6 = (bf16[528,256]{1,0:T(8,128)(2,1)S(1)}, bf16[528,256]{1,0:T(8,128)(2,1)S(1)}, u32[]{:S(2)}, u32[]{:S(2)}) collective-permute-start(bf16[528,256]{1,0:T(8,128)(2,1)S(1)} %collective-permute-done.1.rest_3_), channel_id=1, source_target_pairs={{0,18},{1,19},{2,16},{3,17},{4,22},{5,23},{6,20},{7,21},{8,26},{9,... | collective-permute-start | bytes 811016 | tf_op jit(solution)/shard_map/ppermute | solution.py:405
  57.3 23.0 %collective-permute-start.16 = (bf16[528,256]{1,0:T(8,128)(2,1)S(1)}, bf16[528,256]{1,0:T(8,128)(2,1)S(1)}, u32[]{:S(2)}, u32[]{:S(2)}) collective-permute-start(bf16[528,256]{1,0:T(8,128)(2,1)S(1)} %get-tuple-element.49), channel_id=1, source_target_pairs={{0,4},{1,5},{2,6},{3,7},{4,0},{5,1},{6,2},{7,3},{8,12},{9,13},{10,... | collective-permute-start | bytes 811016 | tf_op jit(solution)/shard_map/ppermute | solution.py:405
  67.6 19.7 %collective-permute-start.17 = (bf16[528,256]{1,0:T(8,128)(2,1)}, bf16[528,256]{1,0:T(8,128)(2,1)}, u32[]{:S(2)}, u32[]{:S(2)}) collective-permute-start(bf16[528,256]{1,0:T(8,128)(2,1)} %get-tuple-element.50), channel_id=1, source_target_pairs={{0,8},{1,9},{2,10},{3,11},{4,12},{5,13},{6,14},{7,15},{8,0},{9,1},... | collective-permute-start | bytes 811016 | tf_op jit(solution)/shard_map/ppermute | solution.py:405
  73.7 13.7 %collective-permute-start.18 = (bf16[528,256]{1,0:T(8,128)(2,1)}, bf16[528,256]{1,0:T(8,128)(2,1)}, u32[]{:S(2)}, u32[]{:S(2)}) collective-permute-start(bf16[528,256]{1,0:T(8,128)(2,1)} %get-tuple-element.51), channel_id=1, source_target_pairs={{0,12},{1,13},{2,14},{3,15},{4,8},{5,9},{6,10},{7,11},{8,4},{9,5},... | collective-permute-start | bytes 811016 | tf_op jit(solution)/shard_map/ppermute | solution.py:405
  76.8 0.7 copy-start.4
  77.5 15.0 %collective-permute-start.13 = (bf16[528,256]{1,0:T(8,128)(2,1)}, bf16[528,256]{1,0:T(8,128)(2,1)}, u32[]{:S(2)}, u32[]{:S(2)}) collective-permute-start(bf16[528,256]{1,0:T(8,128)(2,1)} %get-tuple-element.45), channel_id=1, source_target_pairs={{0,4},{1,5},{2,6},{3,7},{4,0},{5,1},{6,2},{7,3},{8,12},{9,13},{10,... | collective-permute-start | bytes 811016 | tf_op jit(solution)/shard_map/ppermute | solution.py:405
  78.1 14.4 %collective-permute-start.14 = (bf16[528,256]{1,0:T(8,128)(2,1)}, bf16[528,256]{1,0:T(8,128)(2,1)}, u32[]{:S(2)}, u32[]{:S(2)}) collective-permute-start(bf16[528,256]{1,0:T(8,128)(2,1)} %get-tuple-element.46), channel_id=1, source_target_pairs={{0,8},{1,9},{2,10},{3,11},{4,12},{5,13},{6,14},{7,15},{8,0},{9,1},... | collective-permute-start | bytes 811016 | tf_op jit(solution)/shard_map/ppermute | solution.py:405
  80.3 16.9 %collective-permute-start.15 = (bf16[528,256]{1,0:T(8,128)(2,1)}, bf16[528,256]{1,0:T(8,128)(2,1)}, u32[]{:S(2)}, u32[]{:S(2)}) collective-permute-start(bf16[528,256]{1,0:T(8,128)(2,1)} %get-tuple-element.47), channel_id=1, source_target_pairs={{0,12},{1,13},{2,14},{3,15},{4,8},{5,9},{6,10},{7,11},{8,4},{9,5},... | collective-permute-start | bytes 811016 | tf_op jit(solution)/shard_map/ppermute | solution.py:405
  81.3 6.0 %copy-start.5 = (bf16[528,256]{1,0:T(8,128)(2,1)S(1)}, bf16[528,256]{1,0:T(8,128)(2,1)}, u32[]{:S(2)}) copy-start(bf16[528,256]{1,0:T(8,128)(2,1)} %copy-done.4) | copy-start | bytes 811012

commit v5 on v4

--- a/solution.py
+++ b/solution.py
@@ -261,12 +261,12 @@
             ],
         ),
         out_shape=[jax.ShapeDtypeStruct((body, c2), BF16)] * shares,
-        compiler_params=pltpu.CompilerParams(vmem_limit_bytes=60 * 1024 * 1024),
+        compiler_params=pltpu.CompilerParams(vmem_limit_bytes=44 * 1024 * 1024),
         cost_estimate=pl.CostEstimate(
             flops=owned * flops, bytes_accessed=owned * frames * places * breadth * 2, transcendentals=0
         ),
         name="encode",
-    )(named, pixels, *operands)
+    )(named, *[pltpu.with_memory_space_constraint(o, pltpu.HBM) for o in (pixels, *operands)])
 
 
 def pack_kernel(ints, *rest, half, jobs, pick, owned, share):
@@ -326,24 +326,31 @@
 
 
 def finish_kernel(places, w3, g3, place, *rest, count):
-    taken, out = rest[:count], rest[-1]
+    taken, (out, ready, sems) = rest[:count], rest[-3:]
     c3 = w3.shape[1]
-    lines, cores, _, cap, latent, share, _ = out.shape
+    _, lines, cores, _, cap, latent, share, _ = ready.shape
     rows = latent * share
-    owners = [(y, core) for y in range(lines) for core in range(cores)]
+    owners = [(line, core) for line in range(lines) for core in range(cores)]
+    tail = len(owners) * cap * rows
+    notes = jnp.concatenate([taken[i][tail : tail + TILE, :] for i in range(count)], axis=0)
+    wide = jnp.dot(notes, place[...], preferred_element_type=F32)
+    mean, gain = wide[:, :c3], wide[:, c3:] * g3[...]
+    copies = []
     for i in range(count):
-
-        @pl.when(pl.program_id(0) == i)
-        def _():
-            wide = jnp.dot(taken[i][len(owners) * cap * rows :, :], place[...], preferred_element_type=F32)
-            mean, gain = wide[:, :c3], wide[:, c3:] * g3[...]
-            for p, (y, core) in enumerate(owners):
-                block = taken[i][p * cap * rows : (p + 1) * cap * rows, :]
-                third = jnp.dot(block, w3[...], preferred_element_type=F32)
-                for r in range(cap):
-                    at = p * cap + r
-                    token = (third[r * rows : (r + 1) * rows] - mean[at : at + 1]) * gain[at : at + 1]
-                    out[y, core, 0, r] = token.reshape(latent, share, c3).astype(BF16)
+        for p, (line, core) in enumerate(owners):
+            block = taken[i][p * cap * rows : (p + 1) * cap * rows, :]
+            third = jnp.dot(block, w3[...], preferred_element_type=F32)
+            for r in range(cap):
+                at = i * TILE + p * cap + r
+                token = (third[r * rows : (r + 1) * rows] - mean[at : at + 1]) * gain[at : at + 1]
+                ready[i, line, core, 0, r] = token.reshape(latent, share, c3).astype(BF16)
+        spot = out.at[
+            pl.ds(places[3 * i] * lines, lines), pl.ds(places[3 * i + 1] * cores, cores), pl.ds(places[3 * i + 2], 1)
+        ]
+        copies.append(pltpu.make_async_copy(ready.at[i], spot, sems.at[i]))
+        copies[i].start()
+    for copy in copies:
+        copy.wait()
 
 
 def finish(pieces, block, w3, g3, shape, before=None):
@@ -366,12 +373,13 @@
         functools.partial(finish_kernel, count=count),
         grid_spec=pltpu.PrefetchScalarGridSpec(
             num_scalar_prefetch=1,
-            grid=(count,),
+            grid=(1,),
             in_specs=specs,
-            out_specs=pl.BlockSpec(
-                (*block, 1, cap, latent, share, c3),
-                lambda k, s: (s[3 * k], s[3 * k + 1], s[3 * k + 2], 0, 0, 0, 0),
-            ),
+            out_specs=pl.BlockSpec(memory_space=pl.ANY),
+            scratch_shapes=[
+                pltpu.VMEM((count, *block, 1, cap, latent, share, c3), BF16),
+                pltpu.SemaphoreType.DMA((count,)),
+            ],
         ),
         out_shape=jax.ShapeDtypeStruct(shape, BF16),
         input_output_aliases=aliases,
@@ -414,7 +422,7 @@
     crossed = [send(held[0][k], half, 2 * k) for k in range(lines)]
     arrived = [[send(own[k][s], s, 2 * k) for s in range(half)] for k in range(lines)]
     pieces = [((me // 2) ^ k, 0, node ^ s, arrived[k][s]) for k in range(lines) for s in range(half)]
-    beyond = after(held[1], *crossed, *[a for line in own for a in line], arrived[0][1])
+    beyond = after(held[1], *crossed, *[a for line in own for a in line], arrived[1][half - 1])
     beyond = [send(beyond[k], half, 2 * k) for k in range(lines)]
     early, late = [], []
     for b, far in enumerate((crossed, beyond)):

time: 101 us -> 98.1 us (0.971)
  Pallas kernels: 33.2 us -> 26.7 us
  starting transfers between devices: 24.1 us -> 28.3 us
  local copies, waits for them, and re-layouts: 3.99 us -> 2.03 us
    pallas_call x3, Pallas kernels: 15.2 us -> 9.7 us  [finish(): pl.pallas_call(functools.partial(finish_kernel, count=count), grid_spec=p...]
    ppermute x19, starting transfers between devices: 24.1 us -> 28.3 us  [send(): return lax.ppermute(array, ('clip', 'patch'), pairs)]
    unnamed x14 -> x12, local copies, waits for them, and re-layouts: 2.63 us -> 1.38 us
    pallas_call x1, Pallas kernels: 14 us -> 13 us  [encode(): pl.pallas_call(functools.partial(encode_kernel, starts=starts, shares=sha...]
  transfers between devices with their start and end apart: 19 -> 19, of which waited for: 9 -> 7; matrix products, arithmetic and copies ran while one was open for 2% -> 1% of each run, Pallas kernels for 15% -> 11%
where the time goes in v5:
time: 98.1 us; the launch traced here: 97.9 us
  waiting for transfers between devices  40.5 us (41%)
  starting transfers between devices  28.3 us (29%)
  Pallas kernels  26.7 us (27%)
  local copies, waits for them, and re-layouts  2.03 us (2%)
    ppermute x19, waiting for transfers between devices, send(): return lax.ppermute(array, ('clip', 'patch'), pairs)  40.5 us
    ppermute x19, starting transfers between devices, send(): return lax.ppermute(array, ('clip', 'patch'), pairs)  28.3 us
    pallas_call x1, Pallas kernels, encode(): pl.pallas_call(functools.partial(encode_kernel, starts=starts, shares=sha...  13 us
    pallas_call x3, Pallas kernels, finish(): pl.pallas_call(functools.partial(finish_kernel, count=count), grid_spec=p...  9.7 us
    pallas_call x3, Pallas kernels, pack(): pl.pallas_call(functools.partial(pack_kernel, half=half, jobs=jobs, pick=...  4.07 us
  transfers between devices with their start and end apart: 19, of which 7 were waited for; matrix products, arithmetic and copies ran while one was open for 1% of the time, Pallas kernels for 11%

profile of v5, /device:TPU:0, one launch (start us, length us, event | category | flops | bytes accessed | tf_op | source)
XLA Modules:
  0.0 97.9 jit_solution(10180506500767139368)
XLA Ops:
  0.0 0.7 copy-done.5
  0.7 13.0 %encode.1 = (bf16[528,256]{1,0:T(8,128)(2,1)S(1)}, bf16[528,256]{1,0:T(8,128)(2,1)S(1)}, bf16[528,256]{1,0:T(8,128)(2,1)S(1)}, bf16[528,256]{1,0:T(8,128)(2,1)S(1)}) custom-call(s32[4]{0:T(128)S(1)} %bitcast.33, bf16[4,16,64,384]{3,2,1,0:T(8,128)(2,1)} %x.1, bf16[384,128]{1,0:T(8,128)(2,1)} %rest_0_.1, f32[1,128]{1,0:T(1,128)} %bitcast.36, ...), custom_call_target="tpu_custom_call" | custom-call | flops 4563402752 | bytes 3145728 | tf_op jit(solution)/shard_map/encode/pallas_call | solution.py:247
  13.6 0.5 collective-permute-start
  14.2 0.1 collective-permute-start.1
  14.2 5.0 %collective-permute-start.3 = (bf16[528,256]{1,0:T(8,128)(2,1)S(1)}, bf16[528,256]{1,0:T(8,128)(2,1)S(1)}, u32[]{:S(2)}, u32[]{:S(2)}) collective-permute-start(bf16[528,256]{1,0:T(8,128)(2,1)S(1)} %get-tuple-element.32.rest_2_), channel_id=1, source_target_pairs={{0,18},{1,19},{2,16},{3,17},{4,22},{5,23},{6,20},{7,21},{8,26},{9,... | collective-permute-start | bytes 811016 | tf_op jit(solution)/shard_map/ppermute | solution.py:413
  19.2 0.3 collective-permute-start.2
  19.5 0.1 slice_bitcast_fusion.5
  19.6 0.0 collective-permute-done.rest_1_
  19.6 0.1 slice_bitcast_fusion.2
  19.7 0.1 maximum_convert_fusion.ints
  19.8 0.0 collective-permute-done.1.rest_3_
  19.8 0.8 pack.3
  20.6 2.5 %collective-permute-start.4 = (bf16[528,256]{1,0:T(8,128)(2,1)S(1)}, bf16[528,256]{1,0:T(8,128)(2,1)S(1)}, u32[]{:S(2)}, u32[]{:S(2)}) collective-permute-start(bf16[528,256]{1,0:T(8,128)(2,1)S(1)} %get-tuple-element.40), channel_id=1, source_target_pairs={{0,14},{1,15},{2,12},{3,13},{4,10},{5,11},{6,8},{7,9},{8,6},{9,7},... | collective-permute-start | bytes 811016 | tf_op jit(solution)/shard_map/ppermute | solution.py:413
  23.1 0.5 collective-permute-start.10
  23.6 0.2 collective-permute-start.11
  23.8 14.4 %collective-permute-done.3.rest_1_ = bf16[528,256]{1,0:T(8,128)(2,1)S(1)} collective-permute-done((bf16[528,256]{1,0:T(8,128)(2,1)S(1)}, bf16[528,256]{1,0:T(8,128)(2,1)S(1)}, u32[]{:S(2)}, u32[]{:S(2)}) %collective-permute-start.3) | collective-permute-done | bytes 270368 | tf_op jit(solution)/shard_map/ppermute | solution.py:413
  38.2 1.1 %collective-permute-start.12 = (bf16[528,256]{1,0:T(8,128)(2,1)S(1)}, bf16[528,256]{1,0:T(8,128)(2,1)S(1)}, u32[]{:S(2)}, u32[]{:S(2)}) collective-permute-start(bf16[528,256]{1,0:T(8,128)(2,1)S(1)} %get-tuple-element.36), channel_id=1, source_target_pairs={{0,12},{1,13},{2,14},{3,15},{4,8},{5,9},{6,10},{7,11},{8,4},{9,5},... | collective-permute-start | bytes 811016 | tf_op jit(solution)/shard_map/ppermute | solution.py:413
  39.3 0.1 slice_bitcast_fusion
  39.4 4.1 %collective-permute-done.2.rest_0_ = bf16[528,256]{1,0:T(8,128)(2,1)S(1)} collective-permute-done((bf16[528,256]{1,0:T(8,128)(2,1)S(1)}, bf16[528,256]{1,0:T(8,128)(2,1)S(1)}, u32[]{:S(2)}, u32[]{:S(2)}) %collective-permute-start.2) | collective-permute-done | bytes 270368 | tf_op jit(solution)/shard_map/ppermute | solution.py:413
  43.5 0.5 collective-permute-start.7
  44.0 0.0 collective-permute-done.4.rest_7_
  44.0 2.4 %collective-permute-start.8 = (bf16[528,256]{1,0:T(8,128)(2,1)S(1)}, bf16[528,256]{1,0:T(8,128)(2,1)S(1)}, u32[]{:S(2)}, u32[]{:S(2)}) collective-permute-start(bf16[528,256]{1,0:T(8,128)(2,1)S(1)} %get-tuple-element.38), channel_id=1, source_target_pairs={{0,6},{1,7},{2,4},{3,5},{4,2},{5,3},{6,0},{7,1},{8,14},{9,15},{10,... | collective-permute-start | bytes 811016 | tf_op jit(solution)/shard_map/ppermute | solution.py:413
  46.4 0.5 collective-permute-start.9
  47.0 0.2 collective-permute-done.11.rest_2_
  47.2 3.2 %collective-permute-start.5 = (bf16[528,256]{1,0:T(8,128)(2,1)S(1)}, bf16[528,256]{1,0:T(8,128)(2,1)S(1)}, u32[]{:S(2)}, u32[]{:S(2)}) collective-permute-start(bf16[528,256]{1,0:T(8,128)(2,1)S(1)} %collective-permute-done.rest_1_), channel_id=1, source_target_pairs={{0,16},{1,17},{2,18},{3,19},{4,20},{5,21},{6,22},{7,23},{8,24},{9,... | collective-permute-start | bytes 811016 | tf_op jit(solution)/shard_map/ppermute | solution.py:413
  50.4 8.1 %collective-permute-done.12.rest_3_ = bf16[528,256]{1,0:T(8,128)(2,1)S(1)} collective-permute-done((bf16[528,256]{1,0:T(8,128)(2,1)S(1)}, bf16[528,256]{1,0:T(8,128)(2,1)S(1)}, u32[]{:S(2)}, u32[]{:S(2)}) %collective-permute-start.12) | collective-permute-done | bytes 270368 | tf_op jit(solution)/shard_map/ppermute | solution.py:413
  58.5 3.9 %collective-permute-start.6 = (bf16[528,256]{1,0:T(8,128)(2,1)S(1)}, bf16[528,256]{1,0:T(8,128)(2,1)S(1)}, u32[]{:S(2)}, u32[]{:S(2)}) collective-permute-start(bf16[528,256]{1,0:T(8,128)(2,1)S(1)} %collective-permute-done.1.rest_3_), channel_id=1, source_target_pairs={{0,18},{1,19},{2,16},{3,17},{4,22},{5,23},{6,20},{7,21},{8,26},{9,... | collective-permute-start | bytes 811016 | tf_op jit(solution)/shard_map/ppermute | solution.py:413
  62.4 0.1 slice_bitcast_fusion.1
  62.5 0.1 maximum_convert_fusion.2.ints
  62.6 1.6 %pack.5 = (bf16[528,256]{1,0:T(8,128)(2,1)S(1)}, bf16[528,256]{1,0:T(8,128)(2,1)S(1)}, bf16[528,256]{1,0:T(8,128)(2,1)}, bf16[528,256]{1,0:T(8,128)(2,1)}) custom-call(s32[8]{0:T(128)S(1)} %maximum_convert_fusion.2.ints, bf16[528,256]{1,0:T(8,128)(2,1)S(1)} %collective-permute-done.2.rest_0_, bf16[528,256]{1,0:T(8,128)(2,1)S(1)} %collective-permute-done.3.rest_1_), custom_call_target="tpu_custom_call" | custom-call | bytes 1081344 | tf_op jit(solution)/shard_map/pack/pallas_call | solution.py:312
  64.1 0.6 collective-permute-start.16
  64.7 3.4 %collective-permute-start.17 = (bf16[528,256]{1,0:T(8,128)(2,1)}, bf16[528,256]{1,0:T(8,128)(2,1)}, u32[]{:S(2)}, u32[]{:S(2)}) collective-permute-start(bf16[528,256]{1,0:T(8,128)(2,1)} %get-tuple-element.50), channel_id=1, source_target_pairs={{0,8},{1,9},{2,10},{3,11},{4,12},{5,13},{6,14},{7,15},{8,0},{9,1},... | collective-permute-start | bytes 811016 | tf_op jit(solution)/shard_map/ppermute | solution.py:413
  68.1 0.1 collective-permute-start.18
  68.2 8.3 %collective-permute-done.6.rest_1_ = bf16[528,256]{1,0:T(8,128)(2,1)S(1)} collective-permute-done((bf16[528,256]{1,0:T(8,128)(2,1)S(1)}, bf16[528,256]{1,0:T(8,128)(2,1)S(1)}, u32[]{:S(2)}, u32[]{:S(2)}) %collective-permute-start.6) | collective-permute-done | bytes 270368 | tf_op jit(solution)/shard_map/ppermute | solution.py:413
  76.5 0.1 slice_bitcast_fusion.3
  76.6 0.1 maximum_convert_fusion.1.ints
  76.6 1.6 %pack.4 = (bf16[528,256]{1,0:T(8,128)(2,1)S(1)}, bf16[528,256]{1,0:T(8,128)(2,1)}, bf16[528,256]{1,0:T(8,128)(2,1)}, bf16[528,256]{1,0:T(8,128)(2,1)}) custom-call(s32[8]{0:T(128)S(1)} %maximum_convert_fusion.1.ints, bf16[528,256]{1,0:T(8,128)(2,1)S(1)} %collective-permute-done.5.rest_0_, bf16[528,256]{1,0:T(8,128)(2,1)S(1)} %collective-permute-done.6.rest_1_), custom_call_target="tpu_custom_call" | custom-call | bytes 1081344 | tf_op jit(solution)/shard_map/pack/pallas_call | solution.py:312
  78.3 0.7 copy-done.2
  79.0 1.5 %collective-permute-start.13 = (bf16[528,256]{1,0:T(8,128)(2,1)}, bf16[528,256]{1,0:T(8,128)(2,1)}, u32[]{:S(2)}, u32[]{:S(2)}) collective-permute-start(bf16[528,256]{1,0:T(8,128)(2,1)} %get-tuple-element.45), channel_id=1, source_target_pairs={{0,4},{1,5},{2,6},{3,7},{4,0},{5,1},{6,2},{7,3},{8,12},{9,13},{10,... | collective-permute-start | bytes 811016 | tf_op jit(solution)/shard_map/ppermute | solution.py:413
  80.5 2.0 %collective-permute-start.15 = (bf16[528,256]{1,0:T(8,128)(2,1)}, bf16[528,256]{1,0:T(8,128)(2,1)}, u32[]{:S(2)}, u32[]{:S(2)}) collective-permute-start(bf16[528,256]{1,0:T(8,128)(2,1)} %get-tuple-element.47), channel_id=1, source_target_pairs={{0,12},{1,13},{2,14},{3,15},{4,8},{5,9},{6,10},{7,11},{8,4},{9,5},... | collective-permute-start | bytes 811016 | tf_op jit(solution)/shard_map/ppermute | solution.py:413
  82.5 0.1 stack.34.places
  82.6 0.1 stack.72.places
  82.7 0.1 stack.79.places
  82.8 3.0 %finish.3.rest_5_ = bf16[2,2,8,2,8,16,512]{6,5,4,3,2,1,0:T(8,128)(2,1)} custom-call(s32[24]{0:T(128)S(1)} %stack.79.places, bf16[256,512]{1,0:T(8,128)(2,1)S(1)} %copy-done.1, f32[1,512]{1,0:T(1,128)S(1)} %bitcast.30, bf16[256,1024]{1,0:T(8,128)(2,1)S(1)} %copy-done, bf16[528,256]{1,0:T(8,128)(2,1)S(1)} %get-tuple-element.33.rest_0_, ...), custom_call_target="tpu_custom_call" | custom-call | flops 1073741824 | bytes 6291456 | tf_op jit(solution)/shard_map/finish/pallas_call | solution.py:372
  85.9 3.5 %finish.4.rest_3_ = bf16[2,2,8,2,8,16,512]{6,5,4,3,2,1,0:T(8,128)(2,1)} custom-call(s32[15]{0:T(128)S(1)} %stack.72.places, bf16[256,512]{1,0:T(8,128)(2,1)S(1)} %copy-done.1, f32[1,512]{1,0:T(1,128)S(1)} %bitcast.31, bf16[256,1024]{1,0:T(8,128)(2,1)S(1)} %copy-done, bf16[528,256]{1,0:T(8,128)(2,1)S(1)} %get-tuple-element.48.rest_0_, ...), custom_call_target="tpu_custom_call", output_to_operand_aliasing={{}: (9, {})} | custom-call | flops 671088640 | bytes 3932160 | tf_op jit(solution)/shard_map/finish/pallas_call | solution.py:372
  89.4 0.9 collective-permute-done.14.rest_1_
  90.2 4.5 %collective-permute-done.15.rest_2_ = bf16[528,256]{1,0:T(8,128)(2,1)} collective-permute-done((bf16[528,256]{1,0:T(8,128)(2,1)}, bf16[528,256]{1,0:T(8,128)(2,1)}, u32[]{:S(2)}, u32[]{:S(2)}) %collective-permute-start.15) | collective-permute-done | bytes 270368 | tf_op jit(solution)/shard_map/ppermute | solution.py:413
  94.7 3.2 %finish.5 = bf16[2,2,8,2,8,16,512]{6,5,4,3,2,1,0:T(8,128)(2,1)} custom-call(s32[9]{0:T(128)S(1)} %stack.34.places, bf16[256,512]{1,0:T(8,128)(2,1)S(1)} %copy-done.1, f32[1,512]{1,0:T(1,128)S(1)} %bitcast.32, bf16[256,1024]{1,0:T(8,128)(2,1)S(1)} %copy-done, bf16[528,256]{1,0:T(8,128)(2,1)} %collective-permute-done.13.rest_0_, ...), custom_call_target="tpu_custom_call", output_to_operand_aliasing={{}: (7, {})} | custom-call | flops 402653184 | bytes 2359296 | tf_op jit(solution)/shard_map/finish/pallas_call | solution.py:372
  (20 shorter events, 0.0 us)
Async XLA Ops:
  0.0 0.7 copy-start.5
  0.7 82.1 %copy-start = (bf16[256,1024]{1,0:T(8,128)(2,1)S(1)}, bf16[256,1024]{1,0:T(8,128)(2,1)}, u32[]{:S(2)}) copy-start(bf16[256,1024]{1,0:T(8,128)(2,1)} %constant.73.clone.place) | copy-start | bytes 1572868
  0.7 82.2 %copy-start.1 = (bf16[256,512]{1,0:T(8,128)(2,1)S(1)}, bf16[256,512]{1,0:T(8,128)(2,1)}, u32[]{:S(2)}) copy-start(bf16[256,512]{1,0:T(8,128)(2,1)} %w3.5) | copy-start | bytes 786436
  0.7 82.2 %copy-start.4 = (f32[512]{0:T(512)S(1)}, f32[512]{0:T(512)}, u32[]{:S(2)}) copy-start(f32[512]{0:T(512)} %param.19) | copy-start | bytes 6148
  13.6 6.0 %collective-permute-start = (bf16[528,256]{1,0:T(8,128)(2,1)S(1)}, bf16[528,256]{1,0:T(8,128)(2,1)S(1)}, u32[]{:S(2)}, u32[]{:S(2)}) collective-permute-start(bf16[528,256]{1,0:T(8,128)(2,1)S(1)} %get-tuple-element.29), channel_id=1, source_target_pairs={{0,1},{1,0},{2,3},{3,2},{4,5},{5,4},{6,7},{7,6},{8,9},{9,8},{10,11... | collective-permute-start | bytes 811016 | tf_op jit(solution)/shard_map/ppermute | solution.py:413
  14.2 5.6 %collective-permute-start.1 = (bf16[528,256]{1,0:T(8,128)(2,1)S(1)}, bf16[528,256]{1,0:T(8,128)(2,1)S(1)}, u32[]{:S(2)}, u32[]{:S(2)}) collective-permute-start(bf16[528,256]{1,0:T(8,128)(2,1)S(1)} %get-tuple-element.30), channel_id=1, source_target_pairs={{0,1},{1,0},{2,3},{3,2},{4,5},{5,4},{6,7},{7,6},{8,9},{9,8},{10,11... | collective-permute-start | bytes 811016 | tf_op jit(solution)/shard_map/ppermute | solution.py:413
  14.2 23.9 %collective-permute-start.3 = (bf16[528,256]{1,0:T(8,128)(2,1)S(1)}, bf16[528,256]{1,0:T(8,128)(2,1)S(1)}, u32[]{:S(2)}, u32[]{:S(2)}) collective-permute-start(bf16[528,256]{1,0:T(8,128)(2,1)S(1)} %get-tuple-element.32.rest_2_), channel_id=1, source_target_pairs={{0,18},{1,19},{2,16},{3,17},{4,22},{5,23},{6,20},{7,21},{8,26},{9,... | collective-permute-start | bytes 811016 | tf_op jit(solution)/shard_map/ppermute | solution.py:413
  19.2 24.3 %collective-permute-start.2 = (bf16[528,256]{1,0:T(8,128)(2,1)S(1)}, bf16[528,256]{1,0:T(8,128)(2,1)S(1)}, u32[]{:S(2)}, u32[]{:S(2)}) collective-permute-start(bf16[528,256]{1,0:T(8,128)(2,1)S(1)} %get-tuple-element.31.rest_0_), channel_id=1, source_target_pairs={{0,16},{1,17},{2,18},{3,19},{4,20},{5,21},{6,22},{7,23},{8,24},{9,... | collective-permute-start | bytes 811016 | tf_op jit(solution)/shard_map/ppermute | solution.py:413
  20.6 23.4 %collective-permute-start.4 = (bf16[528,256]{1,0:T(8,128)(2,1)S(1)}, bf16[528,256]{1,0:T(8,128)(2,1)S(1)}, u32[]{:S(2)}, u32[]{:S(2)}) collective-permute-start(bf16[528,256]{1,0:T(8,128)(2,1)S(1)} %get-tuple-element.40), channel_id=1, source_target_pairs={{0,14},{1,15},{2,12},{3,13},{4,10},{5,11},{6,8},{7,9},{8,6},{9,7},... | collective-permute-start | bytes 811016 | tf_op jit(solution)/shard_map/ppermute | solution.py:413
  23.1 23.4 %collective-permute-start.10 = (bf16[528,256]{1,0:T(8,128)(2,1)S(1)}, bf16[528,256]{1,0:T(8,128)(2,1)S(1)}, u32[]{:S(2)}, u32[]{:S(2)}) collective-permute-start(bf16[528,256]{1,0:T(8,128)(2,1)S(1)} %get-tuple-element.34), channel_id=1, source_target_pairs={{0,4},{1,5},{2,6},{3,7},{4,0},{5,1},{6,2},{7,3},{8,12},{9,13},{10,... | collective-permute-start | bytes 811016 | tf_op jit(solution)/shard_map/ppermute | solution.py:413
  23.6 23.6 %collective-permute-start.11 = (bf16[528,256]{1,0:T(8,128)(2,1)S(1)}, bf16[528,256]{1,0:T(8,128)(2,1)S(1)}, u32[]{:S(2)}, u32[]{:S(2)}) collective-permute-start(bf16[528,256]{1,0:T(8,128)(2,1)S(1)} %get-tuple-element.35), channel_id=1, source_target_pairs={{0,8},{1,9},{2,10},{3,11},{4,12},{5,13},{6,14},{7,15},{8,0},{9,1},... | collective-permute-start | bytes 811016 | tf_op jit(solution)/shard_map/ppermute | solution.py:413
  38.2 20.3 %collective-permute-start.12 = (bf16[528,256]{1,0:T(8,128)(2,1)S(1)}, bf16[528,256]{1,0:T(8,128)(2,1)S(1)}, u32[]{:S(2)}, u32[]{:S(2)}) collective-permute-start(bf16[528,256]{1,0:T(8,128)(2,1)S(1)} %get-tuple-element.36), channel_id=1, source_target_pairs={{0,12},{1,13},{2,14},{3,15},{4,8},{5,9},{6,10},{7,11},{8,4},{9,5},... | collective-permute-start | bytes 811016 | tf_op jit(solution)/shard_map/ppermute | solution.py:413
  43.5 20.7 %collective-permute-start.7 = (bf16[528,256]{1,0:T(8,128)(2,1)S(1)}, bf16[528,256]{1,0:T(8,128)(2,1)S(1)}, u32[]{:S(2)}, u32[]{:S(2)}) collective-permute-start(bf16[528,256]{1,0:T(8,128)(2,1)S(1)} %get-tuple-element.37), channel_id=1, source_target_pairs={{0,2},{1,3},{2,0},{3,1},{4,6},{5,7},{6,4},{7,5},{8,10},{9,11},{10,... | collective-permute-start | bytes 811016 | tf_op jit(solution)/shard_map/ppermute | solution.py:413
  44.0 20.7 %collective-permute-start.8 = (bf16[528,256]{1,0:T(8,128)(2,1)S(1)}, bf16[528,256]{1,0:T(8,128)(2,1)S(1)}, u32[]{:S(2)}, u32[]{:S(2)}) collective-permute-start(bf16[528,256]{1,0:T(8,128)(2,1)S(1)} %get-tuple-element.38), channel_id=1, source_target_pairs={{0,6},{1,7},{2,4},{3,5},{4,2},{5,3},{6,0},{7,1},{8,14},{9,15},{10,... | collective-permute-start | bytes 811016 | tf_op jit(solution)/shard_map/ppermute | solution.py:413
  46.4 21.7 %collective-permute-start.9 = (bf16[528,256]{1,0:T(8,128)(2,1)S(1)}, bf16[528,256]{1,0:T(8,128)(2,1)S(1)}, u32[]{:S(2)}, u32[]{:S(2)}) collective-permute-start(bf16[528,256]{1,0:T(8,128)(2,1)S(1)} %get-tuple-element.39), channel_id=1, source_target_pairs={{0,10},{1,11},{2,8},{3,9},{4,14},{5,15},{6,12},{7,13},{8,2},{9,3},... | collective-permute-start | bytes 811016 | tf_op jit(solution)/shard_map/ppermute | solution.py:413
  47.2 21.0 %collective-permute-start.5 = (bf16[528,256]{1,0:T(8,128)(2,1)S(1)}, bf16[528,256]{1,0:T(8,128)(2,1)S(1)}, u32[]{:S(2)}, u32[]{:S(2)}) collective-permute-start(bf16[528,256]{1,0:T(8,128)(2,1)S(1)} %collective-permute-done.rest_1_), channel_id=1, source_target_pairs={{0,16},{1,17},{2,18},{3,19},{4,20},{5,21},{6,22},{7,23},{8,24},{9,... | collective-permute-start | bytes 811016 | tf_op jit(solution)/shard_map/ppermute | solution.py:413
  58.5 18.0 %collective-permute-start.6 = (bf16[528,256]{1,0:T(8,128)(2,1)S(1)}, bf16[528,256]{1,0:T(8,128)(2,1)S(1)}, u32[]{:S(2)}, u32[]{:S(2)}) collective-permute-start(bf16[528,256]{1,0:T(8,128)(2,1)S(1)} %collective-permute-done.1.rest_3_), channel_id=1, source_target_pairs={{0,18},{1,19},{2,16},{3,17},{4,22},{5,23},{6,20},{7,21},{8,26},{9,... | collective-permute-start | bytes 811016 | tf_op jit(solution)/shard_map/ppermute | solution.py:413
  64.1 16.4 %collective-permute-start.16 = (bf16[528,256]{1,0:T(8,128)(2,1)S(1)}, bf16[528,256]{1,0:T(8,128)(2,1)S(1)}, u32[]{:S(2)}, u32[]{:S(2)}) collective-permute-start(bf16[528,256]{1,0:T(8,128)(2,1)S(1)} %get-tuple-element.49), channel_id=1, source_target_pairs={{0,4},{1,5},{2,6},{3,7},{4,0},{5,1},{6,2},{7,3},{8,12},{9,13},{10,... | collective-permute-start | bytes 811016 | tf_op jit(solution)/shard_map/ppermute | solution.py:413
  64.7 21.1 %collective-permute-start.17 = (bf16[528,256]{1,0:T(8,128)(2,1)}, bf16[528,256]{1,0:T(8,128)(2,1)}, u32[]{:S(2)}, u32[]{:S(2)}) collective-permute-start(bf16[528,256]{1,0:T(8,128)(2,1)} %get-tuple-element.50), channel_id=1, source_target_pairs={{0,8},{1,9},{2,10},{3,11},{4,12},{5,13},{6,14},{7,15},{8,0},{9,1},... | collective-permute-start | bytes 811016 | tf_op jit(solution)/shard_map/ppermute | solution.py:413
  68.1 17.7 %collective-permute-start.18 = (bf16[528,256]{1,0:T(8,128)(2,1)}, bf16[528,256]{1,0:T(8,128)(2,1)}, u32[]{:S(2)}, u32[]{:S(2)}) collective-permute-start(bf16[528,256]{1,0:T(8,128)(2,1)} %get-tuple-element.51), channel_id=1, source_target_pairs={{0,12},{1,13},{2,14},{3,15},{4,8},{5,9},{6,10},{7,11},{8,4},{9,5},... | collective-permute-start | bytes 811016 | tf_op jit(solution)/shard_map/ppermute | solution.py:413
  78.3 0.7 copy-start.2
  79.0 10.4 %collective-permute-start.13 = (bf16[528,256]{1,0:T(8,128)(2,1)}, bf16[528,256]{1,0:T(8,128)(2,1)}, u32[]{:S(2)}, u32[]{:S(2)}) collective-permute-start(bf16[528,256]{1,0:T(8,128)(2,1)} %get-tuple-element.45), channel_id=1, source_target_pairs={{0,4},{1,5},{2,6},{3,7},{4,0},{5,1},{6,2},{7,3},{8,12},{9,13},{10,... | collective-permute-start | bytes 811016 | tf_op jit(solution)/shard_map/ppermute | solution.py:413
  80.5 9.7 %collective-permute-start.14 = (bf16[528,256]{1,0:T(8,128)(2,1)}, bf16[528,256]{1,0:T(8,128)(2,1)}, u32[]{:S(2)}, u32[]{:S(2)}) collective-permute-start(bf16[528,256]{1,0:T(8,128)(2,1)} %get-tuple-element.46), channel_id=1, source_target_pairs={{0,8},{1,9},{2,10},{3,11},{4,12},{5,13},{6,14},{7,15},{8,0},{9,1},... | collective-permute-start | bytes 811016 | tf_op jit(solution)/shard_map/ppermute | solution.py:413
  80.5 14.2 %collective-permute-start.15 = (bf16[528,256]{1,0:T(8,128)(2,1)}, bf16[528,256]{1,0:T(8,128)(2,1)}, u32[]{:S(2)}, u32[]{:S(2)}) collective-permute-start(bf16[528,256]{1,0:T(8,128)(2,1)} %get-tuple-element.47), channel_id=1, source_target_pairs={{0,12},{1,13},{2,14},{3,15},{4,8},{5,9},{6,10},{7,11},{8,4},{9,5},... | collective-permute-start | bytes 811016 | tf_op jit(solution)/shard_map/ppermute | solution.py:413
  82.8 3.1 %copy-start.3 = (bf16[528,256]{1,0:T(8,128)(2,1)S(1)}, bf16[528,256]{1,0:T(8,128)(2,1)}, u32[]{:S(2)}) copy-start(bf16[528,256]{1,0:T(8,128)(2,1)} %copy-done.2) | copy-start | bytes 811012

commit v6 on v5

--- a/solution.py
+++ b/solution.py
@@ -422,7 +422,7 @@
     crossed = [send(held[0][k], half, 2 * k) for k in range(lines)]
     arrived = [[send(own[k][s], s, 2 * k) for s in range(half)] for k in range(lines)]
     pieces = [((me // 2) ^ k, 0, node ^ s, arrived[k][s]) for k in range(lines) for s in range(half)]
-    beyond = after(held[1], *crossed, *[a for line in own for a in line], arrived[1][half - 1])
+    beyond = after(held[1], crossed[0], *[a for line in own for a in line], arrived[1][half - 1])
     beyond = [send(beyond[k], half, 2 * k) for k in range(lines)]
     early, late = [], []
     for b, far in enumerate((crossed, beyond)):

time: 98.1 us -> 96.8 us (0.987)
  starting transfers between devices: 28.3 us -> 27.1 us
    ppermute x19, starting transfers between devices: 28.3 us -> 27.1 us  [send(): return lax.ppermute(array, ('clip', 'patch'), pairs)]
where the time goes in v6:
time: 96.8 us; the launch traced here: 96.6 us
  waiting for transfers between devices  40.3 us (42%)
  starting transfers between devices  27.1 us (28%)
  Pallas kernels  26.7 us (28%)
  local copies, waits for them, and re-layouts  2.03 us (2%)
    ppermute x19, waiting for transfers between devices, send(): return lax.ppermute(array, ('clip', 'patch'), pairs)  40.3 us
    ppermute x19, starting transfers between devices, send(): return lax.ppermute(array, ('clip', 'patch'), pairs)  27.1 us
    pallas_call x1, Pallas kernels, encode(): pl.pallas_call(functools.partial(encode_kernel, starts=starts, shares=sha...  13 us
    pallas_call x3, Pallas kernels, finish(): pl.pallas_call(functools.partial(finish_kernel, count=count), grid_spec=p...  9.7 us
    pallas_call x3, Pallas kernels, pack(): pl.pallas_call(functools.partial(pack_kernel, half=half, jobs=jobs, pick=...  4.07 us
  transfers between devices with their start and end apart: 19, of which 7 were waited for; matrix products, arithmetic and copies ran while one was open for 1% of the time, Pallas kernels for 11%

profile of v6, /device:TPU:0, one launch (start us, length us, event | category | flops | bytes accessed | tf_op | source)
XLA Modules:
  0.0 96.6 jit_solution(13216797172150806930)
XLA Ops:
  0.0 0.7 copy-done.5
  0.7 13.0 %encode.1 = (bf16[528,256]{1,0:T(8,128)(2,1)S(1)}, bf16[528,256]{1,0:T(8,128)(2,1)S(1)}, bf16[528,256]{1,0:T(8,128)(2,1)S(1)}, bf16[528,256]{1,0:T(8,128)(2,1)S(1)}) custom-call(s32[4]{0:T(128)S(1)} %bitcast.33, bf16[4,16,64,384]{3,2,1,0:T(8,128)(2,1)} %x.1, bf16[384,128]{1,0:T(8,128)(2,1)} %rest_0_.1, f32[1,128]{1,0:T(1,128)} %bitcast.36, ...), custom_call_target="tpu_custom_call" | custom-call | flops 4563402752 | bytes 3145728 | tf_op jit(solution)/shard_map/encode/pallas_call | solution.py:247
  13.6 0.5 collective-permute-start
  14.2 0.1 collective-permute-start.1
  14.2 4.0 %collective-permute-start.2 = (bf16[528,256]{1,0:T(8,128)(2,1)S(1)}, bf16[528,256]{1,0:T(8,128)(2,1)S(1)}, u32[]{:S(2)}, u32[]{:S(2)}) collective-permute-start(bf16[528,256]{1,0:T(8,128)(2,1)S(1)} %get-tuple-element.31.rest_0_), channel_id=1, source_target_pairs={{0,16},{1,17},{2,18},{3,19},{4,20},{5,21},{6,22},{7,23},{8,24},{9,... | collective-permute-start | bytes 811016 | tf_op jit(solution)/shard_map/ppermute | solution.py:413
  18.2 0.1 slice_bitcast_fusion.5
  18.3 0.0 collective-permute-done.rest_1_
  18.3 0.1 slice_bitcast_fusion.2
  18.4 0.1 maximum_convert_fusion.ints
  18.5 0.8 pack.3
  19.3 3.5 %collective-permute-start.3 = (bf16[528,256]{1,0:T(8,128)(2,1)S(1)}, bf16[528,256]{1,0:T(8,128)(2,1)S(1)}, u32[]{:S(2)}, u32[]{:S(2)}) collective-permute-start(bf16[528,256]{1,0:T(8,128)(2,1)S(1)} %get-tuple-element.40), channel_id=1, source_target_pairs={{0,14},{1,15},{2,12},{3,13},{4,10},{5,11},{6,8},{7,9},{8,6},{9,7},... | collective-permute-start | bytes 811016 | tf_op jit(solution)/shard_map/ppermute | solution.py:413
  22.8 1.1 %collective-permute-start.15 = (bf16[528,256]{1,0:T(8,128)(2,1)S(1)}, bf16[528,256]{1,0:T(8,128)(2,1)S(1)}, u32[]{:S(2)}, u32[]{:S(2)}) collective-permute-start(bf16[528,256]{1,0:T(8,128)(2,1)S(1)} %get-tuple-element.32.rest_2_), channel_id=1, source_target_pairs={{0,18},{1,19},{2,16},{3,17},{4,22},{5,23},{6,20},{7,21},{8,26},{9,... | collective-permute-start | bytes 811016 | tf_op jit(solution)/shard_map/ppermute | solution.py:413
  23.9 0.5 collective-permute-start.9
  24.4 0.4 collective-permute-start.10
  24.9 6.8 %collective-permute-done.2.rest_0_ = bf16[528,256]{1,0:T(8,128)(2,1)S(1)} collective-permute-done((bf16[528,256]{1,0:T(8,128)(2,1)S(1)}, bf16[528,256]{1,0:T(8,128)(2,1)S(1)}, u32[]{:S(2)}, u32[]{:S(2)}) %collective-permute-start.2) | collective-permute-done | bytes 270368 | tf_op jit(solution)/shard_map/ppermute | solution.py:413
  31.7 1.5 %collective-permute-start.11 = (bf16[528,256]{1,0:T(8,128)(2,1)S(1)}, bf16[528,256]{1,0:T(8,128)(2,1)S(1)}, u32[]{:S(2)}, u32[]{:S(2)}) collective-permute-start(bf16[528,256]{1,0:T(8,128)(2,1)S(1)} %get-tuple-element.36), channel_id=1, source_target_pairs={{0,12},{1,13},{2,14},{3,15},{4,8},{5,9},{6,10},{7,11},{8,4},{9,5},... | collective-permute-start | bytes 811016 | tf_op jit(solution)/shard_map/ppermute | solution.py:413
  33.1 0.1 slice_bitcast_fusion.1
  33.2 3.1 %collective-permute-done.3.rest_7_ = bf16[528,256]{1,0:T(8,128)(2,1)S(1)} collective-permute-done((bf16[528,256]{1,0:T(8,128)(2,1)S(1)}, bf16[528,256]{1,0:T(8,128)(2,1)S(1)}, u32[]{:S(2)}, u32[]{:S(2)}) %collective-permute-start.3) | collective-permute-done | bytes 270368 | tf_op jit(solution)/shard_map/ppermute | solution.py:413
  36.3 1.6 %collective-permute-start.6 = (bf16[528,256]{1,0:T(8,128)(2,1)S(1)}, bf16[528,256]{1,0:T(8,128)(2,1)S(1)}, u32[]{:S(2)}, u32[]{:S(2)}) collective-permute-start(bf16[528,256]{1,0:T(8,128)(2,1)S(1)} %get-tuple-element.37), channel_id=1, source_target_pairs={{0,2},{1,3},{2,0},{3,1},{4,6},{5,7},{6,4},{7,5},{8,10},{9,11},{10,... | collective-permute-start | bytes 811016 | tf_op jit(solution)/shard_map/ppermute | solution.py:413
  37.9 5.7 %collective-permute-done.15.rest_1_ = bf16[528,256]{1,0:T(8,128)(2,1)S(1)} collective-permute-done((bf16[528,256]{1,0:T(8,128)(2,1)S(1)}, bf16[528,256]{1,0:T(8,128)(2,1)S(1)}, u32[]{:S(2)}, u32[]{:S(2)}) %collective-permute-start.15) | collective-permute-done | bytes 270368 | tf_op jit(solution)/shard_map/ppermute | solution.py:413
  43.6 1.4 %collective-permute-start.7 = (bf16[528,256]{1,0:T(8,128)(2,1)S(1)}, bf16[528,256]{1,0:T(8,128)(2,1)S(1)}, u32[]{:S(2)}, u32[]{:S(2)}) collective-permute-start(bf16[528,256]{1,0:T(8,128)(2,1)S(1)} %get-tuple-element.38), channel_id=1, source_target_pairs={{0,6},{1,7},{2,4},{3,5},{4,2},{5,3},{6,0},{7,1},{8,14},{9,15},{10,... | collective-permute-start | bytes 811016 | tf_op jit(solution)/shard_map/ppermute | solution.py:413
  45.0 0.5 collective-permute-start.8
  45.6 1.2 %collective-permute-done.10.rest_2_ = bf16[528,256]{1,0:T(8,128)(2,1)S(1)} collective-permute-done((bf16[528,256]{1,0:T(8,128)(2,1)S(1)}, bf16[528,256]{1,0:T(8,128)(2,1)S(1)}, u32[]{:S(2)}, u32[]{:S(2)}) %collective-permute-start.10) | collective-permute-done | bytes 270368 | tf_op jit(solution)/shard_map/ppermute | solution.py:413
  46.8 3.2 %collective-permute-start.4 = (bf16[528,256]{1,0:T(8,128)(2,1)S(1)}, bf16[528,256]{1,0:T(8,128)(2,1)S(1)}, u32[]{:S(2)}, u32[]{:S(2)}) collective-permute-start(bf16[528,256]{1,0:T(8,128)(2,1)S(1)} %collective-permute-done.rest_1_), channel_id=1, source_target_pairs={{0,16},{1,17},{2,18},{3,19},{4,20},{5,21},{6,22},{7,23},{8,24},{9,... | collective-permute-start | bytes 811016 | tf_op jit(solution)/shard_map/ppermute | solution.py:413
  50.0 8.4 %collective-permute-done.11.rest_3_ = bf16[528,256]{1,0:T(8,128)(2,1)S(1)} collective-permute-done((bf16[528,256]{1,0:T(8,128)(2,1)S(1)}, bf16[528,256]{1,0:T(8,128)(2,1)S(1)}, u32[]{:S(2)}, u32[]{:S(2)}) %collective-permute-start.11) | collective-permute-done | bytes 270368 | tf_op jit(solution)/shard_map/ppermute | solution.py:413
  58.5 1.2 %collective-permute-start.5 = (bf16[528,256]{1,0:T(8,128)(2,1)S(1)}, bf16[528,256]{1,0:T(8,128)(2,1)S(1)}, u32[]{:S(2)}, u32[]{:S(2)}) collective-permute-start(bf16[528,256]{1,0:T(8,128)(2,1)S(1)} %collective-permute-done.1.rest_3_), channel_id=1, source_target_pairs={{0,18},{1,19},{2,16},{3,17},{4,22},{5,23},{6,20},{7,21},{8,26},{9,... | collective-permute-start | bytes 811016 | tf_op jit(solution)/shard_map/ppermute | solution.py:413
  59.7 0.1 slice_bitcast_fusion
  59.7 0.1 maximum_convert_fusion.2.ints
  59.8 1.6 %pack.5 = (bf16[528,256]{1,0:T(8,128)(2,1)S(1)}, bf16[528,256]{1,0:T(8,128)(2,1)S(1)}, bf16[528,256]{1,0:T(8,128)(2,1)}, bf16[528,256]{1,0:T(8,128)(2,1)}) custom-call(s32[8]{0:T(128)S(1)} %maximum_convert_fusion.2.ints, bf16[528,256]{1,0:T(8,128)(2,1)S(1)} %collective-permute-done.2.rest_0_, bf16[528,256]{1,0:T(8,128)(2,1)S(1)} %collective-permute-done.15.rest_1_), custom_call_target="tpu_custom_call" | custom-call | bytes 1081344 | tf_op jit(solution)/shard_map/pack/pallas_call | solution.py:312
  61.4 0.0 collective-permute-done.6.rest_4_
  61.4 0.5 collective-permute-start.16
  62.0 3.4 %collective-permute-start.17 = (bf16[528,256]{1,0:T(8,128)(2,1)}, bf16[528,256]{1,0:T(8,128)(2,1)}, u32[]{:S(2)}, u32[]{:S(2)}) collective-permute-start(bf16[528,256]{1,0:T(8,128)(2,1)} %get-tuple-element.50), channel_id=1, source_target_pairs={{0,8},{1,9},{2,10},{3,11},{4,12},{5,13},{6,14},{7,15},{8,0},{9,1},... | collective-permute-start | bytes 811016 | tf_op jit(solution)/shard_map/ppermute | solution.py:413
  65.4 0.0 collective-permute-done.8.rest_6_
  65.4 0.0 collective-permute-start.18
  65.4 11.1 %collective-permute-done.5.rest_1_ = bf16[528,256]{1,0:T(8,128)(2,1)S(1)} collective-permute-done((bf16[528,256]{1,0:T(8,128)(2,1)S(1)}, bf16[528,256]{1,0:T(8,128)(2,1)S(1)}, u32[]{:S(2)}, u32[]{:S(2)}) %collective-permute-start.5) | collective-permute-done | bytes 270368 | tf_op jit(solution)/shard_map/ppermute | solution.py:413
  76.5 0.1 slice_bitcast_fusion.3
  76.6 0.1 maximum_convert_fusion.1.ints
  76.7 1.6 %pack.4 = (bf16[528,256]{1,0:T(8,128)(2,1)S(1)}, bf16[528,256]{1,0:T(8,128)(2,1)}, bf16[528,256]{1,0:T(8,128)(2,1)}, bf16[528,256]{1,0:T(8,128)(2,1)}) custom-call(s32[8]{0:T(128)S(1)} %maximum_convert_fusion.1.ints, bf16[528,256]{1,0:T(8,128)(2,1)S(1)} %collective-permute-done.4.rest_0_, bf16[528,256]{1,0:T(8,128)(2,1)S(1)} %collective-permute-done.5.rest_1_), custom_call_target="tpu_custom_call" | custom-call | bytes 1081344 | tf_op jit(solution)/shard_map/pack/pallas_call | solution.py:312
  78.3 0.7 copy-done.2
  79.0 0.5 collective-permute-start.12
  79.5 3.0 %collective-permute-start.14 = (bf16[528,256]{1,0:T(8,128)(2,1)}, bf16[528,256]{1,0:T(8,128)(2,1)}, u32[]{:S(2)}, u32[]{:S(2)}) collective-permute-start(bf16[528,256]{1,0:T(8,128)(2,1)} %get-tuple-element.47), channel_id=1, source_target_pairs={{0,12},{1,13},{2,14},{3,15},{4,8},{5,9},{6,10},{7,11},{8,4},{9,5},... | collective-permute-start | bytes 811016 | tf_op jit(solution)/shard_map/ppermute | solution.py:413
  82.5 0.1 stack.34.places
  82.6 0.1 stack.72.places
  82.7 0.1 stack.79.places
  82.8 3.0 %finish.3.rest_5_ = bf16[2,2,8,2,8,16,512]{6,5,4,3,2,1,0:T(8,128)(2,1)} custom-call(s32[24]{0:T(128)S(1)} %stack.79.places, bf16[256,512]{1,0:T(8,128)(2,1)S(1)} %copy-done.1, f32[1,512]{1,0:T(1,128)S(1)} %bitcast.30, bf16[256,1024]{1,0:T(8,128)(2,1)S(1)} %copy-done, bf16[528,256]{1,0:T(8,128)(2,1)S(1)} %get-tuple-element.33.rest_0_, ...), custom_call_target="tpu_custom_call" | custom-call | flops 1073741824 | bytes 6291456 | tf_op jit(solution)/shard_map/finish/pallas_call | solution.py:372
  85.9 3.5 %finish.4.rest_3_ = bf16[2,2,8,2,8,16,512]{6,5,4,3,2,1,0:T(8,128)(2,1)} custom-call(s32[15]{0:T(128)S(1)} %stack.72.places, bf16[256,512]{1,0:T(8,128)(2,1)S(1)} %copy-done.1, f32[1,512]{1,0:T(1,128)S(1)} %bitcast.31, bf16[256,1024]{1,0:T(8,128)(2,1)S(1)} %copy-done, bf16[528,256]{1,0:T(8,128)(2,1)S(1)} %get-tuple-element.48.rest_0_, ...), custom_call_target="tpu_custom_call", output_to_operand_aliasing={{}: (9, {})} | custom-call | flops 671088640 | bytes 3932160 | tf_op jit(solution)/shard_map/finish/pallas_call | solution.py:372
  89.4 4.0 %collective-permute-done.14.rest_2_ = bf16[528,256]{1,0:T(8,128)(2,1)} collective-permute-done((bf16[528,256]{1,0:T(8,128)(2,1)}, bf16[528,256]{1,0:T(8,128)(2,1)}, u32[]{:S(2)}, u32[]{:S(2)}) %collective-permute-start.14) | collective-permute-done | bytes 270368 | tf_op jit(solution)/shard_map/ppermute | solution.py:413
  93.4 3.2 %finish.5 = bf16[2,2,8,2,8,16,512]{6,5,4,3,2,1,0:T(8,128)(2,1)} custom-call(s32[9]{0:T(128)S(1)} %stack.34.places, bf16[256,512]{1,0:T(8,128)(2,1)S(1)} %copy-done.1, f32[1,512]{1,0:T(1,128)S(1)} %bitcast.32, bf16[256,1024]{1,0:T(8,128)(2,1)S(1)} %copy-done, bf16[528,256]{1,0:T(8,128)(2,1)} %collective-permute-done.12.rest_0_, ...), custom_call_target="tpu_custom_call", output_to_operand_aliasing={{}: (7, {})} | custom-call | flops 402653184 | bytes 2359296 | tf_op jit(solution)/shard_map/finish/pallas_call | solution.py:372
  (20 shorter events, 0.0 us)
Async XLA Ops:
  0.0 0.7 copy-start.5
  0.7 82.2 %copy-start = (bf16[256,1024]{1,0:T(8,128)(2,1)S(1)}, bf16[256,1024]{1,0:T(8,128)(2,1)}, u32[]{:S(2)}) copy-start(bf16[256,1024]{1,0:T(8,128)(2,1)} %constant.73.clone.place) | copy-start | bytes 1572868
  0.7 82.2 %copy-start.1 = (bf16[256,512]{1,0:T(8,128)(2,1)S(1)}, bf16[256,512]{1,0:T(8,128)(2,1)}, u32[]{:S(2)}) copy-start(bf16[256,512]{1,0:T(8,128)(2,1)} %w3.5) | copy-start | bytes 786436
  0.7 82.2 %copy-start.4 = (f32[512]{0:T(512)S(1)}, f32[512]{0:T(512)}, u32[]{:S(2)}) copy-start(f32[512]{0:T(512)} %param.19) | copy-start | bytes 6148
  13.6 4.7 %collective-permute-start = (bf16[528,256]{1,0:T(8,128)(2,1)S(1)}, bf16[528,256]{1,0:T(8,128)(2,1)S(1)}, u32[]{:S(2)}, u32[]{:S(2)}) collective-permute-start(bf16[528,256]{1,0:T(8,128)(2,1)S(1)} %get-tuple-element.29), channel_id=1, source_target_pairs={{0,1},{1,0},{2,3},{3,2},{4,5},{5,4},{6,7},{7,6},{8,9},{9,8},{10,11... | collective-permute-start | bytes 811016 | tf_op jit(solution)/shard_map/ppermute | solution.py:413
  14.2 4.3 %collective-permute-start.1 = (bf16[528,256]{1,0:T(8,128)(2,1)S(1)}, bf16[528,256]{1,0:T(8,128)(2,1)S(1)}, u32[]{:S(2)}, u32[]{:S(2)}) collective-permute-start(bf16[528,256]{1,0:T(8,128)(2,1)S(1)} %get-tuple-element.30), channel_id=1, source_target_pairs={{0,1},{1,0},{2,3},{3,2},{4,5},{5,4},{6,7},{7,6},{8,9},{9,8},{10,11... | collective-permute-start | bytes 811016 | tf_op jit(solution)/shard_map/ppermute | solution.py:413
  14.2 17.4 %collective-permute-start.2 = (bf16[528,256]{1,0:T(8,128)(2,1)S(1)}, bf16[528,256]{1,0:T(8,128)(2,1)S(1)}, u32[]{:S(2)}, u32[]{:S(2)}) collective-permute-start(bf16[528,256]{1,0:T(8,128)(2,1)S(1)} %get-tuple-element.31.rest_0_), channel_id=1, source_target_pairs={{0,16},{1,17},{2,18},{3,19},{4,20},{5,21},{6,22},{7,23},{8,24},{9,... | collective-permute-start | bytes 811016 | tf_op jit(solution)/shard_map/ppermute | solution.py:413
  19.3 17.0 %collective-permute-start.3 = (bf16[528,256]{1,0:T(8,128)(2,1)S(1)}, bf16[528,256]{1,0:T(8,128)(2,1)S(1)}, u32[]{:S(2)}, u32[]{:S(2)}) collective-permute-start(bf16[528,256]{1,0:T(8,128)(2,1)S(1)} %get-tuple-element.40), channel_id=1, source_target_pairs={{0,14},{1,15},{2,12},{3,13},{4,10},{5,11},{6,8},{7,9},{8,6},{9,7},... | collective-permute-start | bytes 811016 | tf_op jit(solution)/shard_map/ppermute | solution.py:413
  22.8 20.8 %collective-permute-start.15 = (bf16[528,256]{1,0:T(8,128)(2,1)S(1)}, bf16[528,256]{1,0:T(8,128)(2,1)S(1)}, u32[]{:S(2)}, u32[]{:S(2)}) collective-permute-start(bf16[528,256]{1,0:T(8,128)(2,1)S(1)} %get-tuple-element.32.rest_2_), channel_id=1, source_target_pairs={{0,18},{1,19},{2,16},{3,17},{4,22},{5,23},{6,20},{7,21},{8,26},{9,... | collective-permute-start | bytes 811016 | tf_op jit(solution)/shard_map/ppermute | solution.py:413
  23.9 21.1 %collective-permute-start.9 = (bf16[528,256]{1,0:T(8,128)(2,1)S(1)}, bf16[528,256]{1,0:T(8,128)(2,1)S(1)}, u32[]{:S(2)}, u32[]{:S(2)}) collective-permute-start(bf16[528,256]{1,0:T(8,128)(2,1)S(1)} %get-tuple-element.34), channel_id=1, source_target_pairs={{0,4},{1,5},{2,6},{3,7},{4,0},{5,1},{6,2},{7,3},{8,12},{9,13},{10,... | collective-permute-start | bytes 811016 | tf_op jit(solution)/shard_map/ppermute | solution.py:413
  24.4 22.3 %collective-permute-start.10 = (bf16[528,256]{1,0:T(8,128)(2,1)S(1)}, bf16[528,256]{1,0:T(8,128)(2,1)S(1)}, u32[]{:S(2)}, u32[]{:S(2)}) collective-permute-start(bf16[528,256]{1,0:T(8,128)(2,1)S(1)} %get-tuple-element.35), channel_id=1, source_target_pairs={{0,8},{1,9},{2,10},{3,11},{4,12},{5,13},{6,14},{7,15},{8,0},{9,1},... | collective-permute-start | bytes 811016 | tf_op jit(solution)/shard_map/ppermute | solution.py:413
  31.7 26.8 %collective-permute-start.11 = (bf16[528,256]{1,0:T(8,128)(2,1)S(1)}, bf16[528,256]{1,0:T(8,128)(2,1)S(1)}, u32[]{:S(2)}, u32[]{:S(2)}) collective-permute-start(bf16[528,256]{1,0:T(8,128)(2,1)S(1)} %get-tuple-element.36), channel_id=1, source_target_pairs={{0,12},{1,13},{2,14},{3,15},{4,8},{5,9},{6,10},{7,11},{8,4},{9,5},... | collective-permute-start | bytes 811016 | tf_op jit(solution)/shard_map/ppermute | solution.py:413
  36.3 25.1 %collective-permute-start.6 = (bf16[528,256]{1,0:T(8,128)(2,1)S(1)}, bf16[528,256]{1,0:T(8,128)(2,1)S(1)}, u32[]{:S(2)}, u32[]{:S(2)}) collective-permute-start(bf16[528,256]{1,0:T(8,128)(2,1)S(1)} %get-tuple-element.37), channel_id=1, source_target_pairs={{0,2},{1,3},{2,0},{3,1},{4,6},{5,7},{6,4},{7,5},{8,10},{9,11},{10,... | collective-permute-start | bytes 811016 | tf_op jit(solution)/shard_map/ppermute | solution.py:413
  43.6 18.4 %collective-permute-start.7 = (bf16[528,256]{1,0:T(8,128)(2,1)S(1)}, bf16[528,256]{1,0:T(8,128)(2,1)S(1)}, u32[]{:S(2)}, u32[]{:S(2)}) collective-permute-start(bf16[528,256]{1,0:T(8,128)(2,1)S(1)} %get-tuple-element.38), channel_id=1, source_target_pairs={{0,6},{1,7},{2,4},{3,5},{4,2},{5,3},{6,0},{7,1},{8,14},{9,15},{10,... | collective-permute-start | bytes 811016 | tf_op jit(solution)/shard_map/ppermute | solution.py:413
  45.0 20.4 %collective-permute-start.8 = (bf16[528,256]{1,0:T(8,128)(2,1)S(1)}, bf16[528,256]{1,0:T(8,128)(2,1)S(1)}, u32[]{:S(2)}, u32[]{:S(2)}) collective-permute-start(bf16[528,256]{1,0:T(8,128)(2,1)S(1)} %get-tuple-element.39), channel_id=1, source_target_pairs={{0,10},{1,11},{2,8},{3,9},{4,14},{5,15},{6,12},{7,13},{8,2},{9,3},... | collective-permute-start | bytes 811016 | tf_op jit(solution)/shard_map/ppermute | solution.py:413
  46.8 18.6 %collective-permute-start.4 = (bf16[528,256]{1,0:T(8,128)(2,1)S(1)}, bf16[528,256]{1,0:T(8,128)(2,1)S(1)}, u32[]{:S(2)}, u32[]{:S(2)}) collective-permute-start(bf16[528,256]{1,0:T(8,128)(2,1)S(1)} %collective-permute-done.rest_1_), channel_id=1, source_target_pairs={{0,16},{1,17},{2,18},{3,19},{4,20},{5,21},{6,22},{7,23},{8,24},{9,... | collective-permute-start | bytes 811016 | tf_op jit(solution)/shard_map/ppermute | solution.py:413
  58.5 18.1 %collective-permute-start.5 = (bf16[528,256]{1,0:T(8,128)(2,1)S(1)}, bf16[528,256]{1,0:T(8,128)(2,1)S(1)}, u32[]{:S(2)}, u32[]{:S(2)}) collective-permute-start(bf16[528,256]{1,0:T(8,128)(2,1)S(1)} %collective-permute-done.1.rest_3_), channel_id=1, source_target_pairs={{0,18},{1,19},{2,16},{3,17},{4,22},{5,23},{6,20},{7,21},{8,26},{9,... | collective-permute-start | bytes 811016 | tf_op jit(solution)/shard_map/ppermute | solution.py:413
  61.4 18.1 %collective-permute-start.16 = (bf16[528,256]{1,0:T(8,128)(2,1)S(1)}, bf16[528,256]{1,0:T(8,128)(2,1)S(1)}, u32[]{:S(2)}, u32[]{:S(2)}) collective-permute-start(bf16[528,256]{1,0:T(8,128)(2,1)S(1)} %get-tuple-element.49), channel_id=1, source_target_pairs={{0,4},{1,5},{2,6},{3,7},{4,0},{5,1},{6,2},{7,3},{8,12},{9,13},{10,... | collective-permute-start | bytes 811016 | tf_op jit(solution)/shard_map/ppermute | solution.py:413
  62.0 23.9 %collective-permute-start.17 = (bf16[528,256]{1,0:T(8,128)(2,1)}, bf16[528,256]{1,0:T(8,128)(2,1)}, u32[]{:S(2)}, u32[]{:S(2)}) collective-permute-start(bf16[528,256]{1,0:T(8,128)(2,1)} %get-tuple-element.50), channel_id=1, source_target_pairs={{0,8},{1,9},{2,10},{3,11},{4,12},{5,13},{6,14},{7,15},{8,0},{9,1},... | collective-permute-start | bytes 811016 | tf_op jit(solution)/shard_map/ppermute | solution.py:413
  65.4 20.5 %collective-permute-start.18 = (bf16[528,256]{1,0:T(8,128)(2,1)}, bf16[528,256]{1,0:T(8,128)(2,1)}, u32[]{:S(2)}, u32[]{:S(2)}) collective-permute-start(bf16[528,256]{1,0:T(8,128)(2,1)} %get-tuple-element.51), channel_id=1, source_target_pairs={{0,12},{1,13},{2,14},{3,15},{4,8},{5,9},{6,10},{7,11},{8,4},{9,5},... | collective-permute-start | bytes 811016 | tf_op jit(solution)/shard_map/ppermute | solution.py:413
  78.3 0.7 copy-start.2
  79.0 10.4 %collective-permute-start.12 = (bf16[528,256]{1,0:T(8,128)(2,1)}, bf16[528,256]{1,0:T(8,128)(2,1)}, u32[]{:S(2)}, u32[]{:S(2)}) collective-permute-start(bf16[528,256]{1,0:T(8,128)(2,1)} %get-tuple-element.45), channel_id=1, source_target_pairs={{0,4},{1,5},{2,6},{3,7},{4,0},{5,1},{6,2},{7,3},{8,12},{9,13},{10,... | collective-permute-start | bytes 811016 | tf_op jit(solution)/shard_map/ppermute | solution.py:413
  79.5 9.9 %collective-permute-start.13 = (bf16[528,256]{1,0:T(8,128)(2,1)}, bf16[528,256]{1,0:T(8,128)(2,1)}, u32[]{:S(2)}, u32[]{:S(2)}) collective-permute-start(bf16[528,256]{1,0:T(8,128)(2,1)} %get-tuple-element.46), channel_id=1, source_target_pairs={{0,8},{1,9},{2,10},{3,11},{4,12},{5,13},{6,14},{7,15},{8,0},{9,1},... | collective-permute-start | bytes 811016 | tf_op jit(solution)/shard_map/ppermute | solution.py:413
  79.5 13.9 %collective-permute-start.14 = (bf16[528,256]{1,0:T(8,128)(2,1)}, bf16[528,256]{1,0:T(8,128)(2,1)}, u32[]{:S(2)}, u32[]{:S(2)}) collective-permute-start(bf16[528,256]{1,0:T(8,128)(2,1)} %get-tuple-element.47), channel_id=1, source_target_pairs={{0,12},{1,13},{2,14},{3,15},{4,8},{5,9},{6,10},{7,11},{8,4},{9,5},... | collective-permute-start | bytes 811016 | tf_op jit(solution)/shard_map/ppermute | solution.py:413
  82.8 3.1 %copy-start.3 = (bf16[528,256]{1,0:T(8,128)(2,1)S(1)}, bf16[528,256]{1,0:T(8,128)(2,1)}, u32[]{:S(2)}) copy-start(bf16[528,256]{1,0:T(8,128)(2,1)} %copy-done.2) | copy-start | bytes 811012

commit v7 on v6

--- a/solution.py
+++ b/solution.py
@@ -266,7 +266,7 @@
             flops=owned * flops, bytes_accessed=owned * frames * places * breadth * 2, transcendentals=0
         ),
         name="encode",
-    )(named, *[pltpu.with_memory_space_constraint(o, pltpu.HBM) for o in (pixels, *operands)])
+    )(*[pltpu.with_memory_space_constraint(o, pltpu.HBM) for o in (named, pixels, *operands)])
 
 
 def pack_kernel(ints, *rest, half, jobs, pick, owned, share):

time: 96.8 us -> 96.4 us (level)
  no operation moved by 1% of the time
where the time goes in v7:
time: 96.4 us; the launch traced here: 96.2 us
  waiting for transfers between devices  40.3 us (42%)
  starting transfers between devices  27.1 us (28%)
  Pallas kernels  27 us (28%)
  local copies, waits for them, and re-layouts  1.36 us (1%)
    ppermute x19, waiting for transfers between devices, send(): return lax.ppermute(array, ('clip', 'patch'), pairs)  40.3 us
    ppermute x19, starting transfers between devices, send(): return lax.ppermute(array, ('clip', 'patch'), pairs)  27.1 us
    pallas_call x1, Pallas kernels, encode(): pl.pallas_call(functools.partial(encode_kernel, starts=starts, shares=sha...  13.2 us
    pallas_call x3, Pallas kernels, finish(): pl.pallas_call(functools.partial(finish_kernel, count=count), grid_spec=p...  9.7 us
    pallas_call x3, Pallas kernels, pack(): pl.pallas_call(functools.partial(pack_kernel, half=half, jobs=jobs, pick=...  4.07 us
  transfers between devices with their start and end apart: 19, of which 7 were waited for; matrix products, arithmetic and copies ran while one was open for 1% of the time, Pallas kernels for 11%

profile of v7, /device:TPU:0, one launch (start us, length us, event | category | flops | bytes accessed | tf_op | source)
XLA Modules:
  0.0 96.2 jit_solution(14352318137389090741)
XLA Ops:
  0.0 13.2 %encode.1 = (bf16[528,256]{1,0:T(8,128)(2,1)S(1)}, bf16[528,256]{1,0:T(8,128)(2,1)S(1)}, bf16[528,256]{1,0:T(8,128)(2,1)S(1)}, bf16[528,256]{1,0:T(8,128)(2,1)S(1)}) custom-call(s32[4]{0:T(128)} %bitcast.35, bf16[4,16,64,384]{3,2,1,0:T(8,128)(2,1)} %x.1, bf16[384,128]{1,0:T(8,128)(2,1)} %rest_0_.1, f32[1,128]{1,0:T(1,128)} %bitcast.36, ...), custom_call_target="tpu_custom_call" | custom-call | flops 4563402752 | bytes 3145728 | tf_op jit(solution)/shard_map/encode/pallas_call | solution.py:247
  13.2 0.5 collective-permute-start
  13.8 0.1 collective-permute-start.1
  13.8 4.0 %collective-permute-start.2 = (bf16[528,256]{1,0:T(8,128)(2,1)S(1)}, bf16[528,256]{1,0:T(8,128)(2,1)S(1)}, u32[]{:S(2)}, u32[]{:S(2)}) collective-permute-start(bf16[528,256]{1,0:T(8,128)(2,1)S(1)} %get-tuple-element.31.rest_0_), channel_id=1, source_target_pairs={{0,16},{1,17},{2,18},{3,19},{4,20},{5,21},{6,22},{7,23},{8,24},{9,... | collective-permute-start | bytes 811016 | tf_op jit(solution)/shard_map/ppermute | solution.py:413
  17.9 0.1 slice_bitcast_fusion.5
  17.9 0.1 slice_bitcast_fusion.2
  18.0 0.1 maximum_convert_fusion.ints
  18.1 0.8 pack.3
  18.9 3.5 %collective-permute-start.3 = (bf16[528,256]{1,0:T(8,128)(2,1)S(1)}, bf16[528,256]{1,0:T(8,128)(2,1)S(1)}, u32[]{:S(2)}, u32[]{:S(2)}) collective-permute-start(bf16[528,256]{1,0:T(8,128)(2,1)S(1)} %get-tuple-element.40), channel_id=1, source_target_pairs={{0,14},{1,15},{2,12},{3,13},{4,10},{5,11},{6,8},{7,9},{8,6},{9,7},... | collective-permute-start | bytes 811016 | tf_op jit(solution)/shard_map/ppermute | solution.py:413
  22.4 1.1 %collective-permute-start.15 = (bf16[528,256]{1,0:T(8,128)(2,1)S(1)}, bf16[528,256]{1,0:T(8,128)(2,1)S(1)}, u32[]{:S(2)}, u32[]{:S(2)}) collective-permute-start(bf16[528,256]{1,0:T(8,128)(2,1)S(1)} %get-tuple-element.32.rest_2_), channel_id=1, source_target_pairs={{0,18},{1,19},{2,16},{3,17},{4,22},{5,23},{6,20},{7,21},{8,26},{9,... | collective-permute-start | bytes 811016 | tf_op jit(solution)/shard_map/ppermute | solution.py:413
  23.5 0.5 collective-permute-start.9
  24.1 0.5 collective-permute-start.10
  24.5 6.8 %collective-permute-done.2.rest_0_ = bf16[528,256]{1,0:T(8,128)(2,1)S(1)} collective-permute-done((bf16[528,256]{1,0:T(8,128)(2,1)S(1)}, bf16[528,256]{1,0:T(8,128)(2,1)S(1)}, u32[]{:S(2)}, u32[]{:S(2)}) %collective-permute-start.2) | collective-permute-done | bytes 270368 | tf_op jit(solution)/shard_map/ppermute | solution.py:413
  31.3 1.5 %collective-permute-start.11 = (bf16[528,256]{1,0:T(8,128)(2,1)S(1)}, bf16[528,256]{1,0:T(8,128)(2,1)S(1)}, u32[]{:S(2)}, u32[]{:S(2)}) collective-permute-start(bf16[528,256]{1,0:T(8,128)(2,1)S(1)} %get-tuple-element.36), channel_id=1, source_target_pairs={{0,12},{1,13},{2,14},{3,15},{4,8},{5,9},{6,10},{7,11},{8,4},{9,5},... | collective-permute-start | bytes 811016 | tf_op jit(solution)/shard_map/ppermute | solution.py:413
  32.8 0.1 slice_bitcast_fusion.1
  32.8 3.1 %collective-permute-done.3.rest_7_ = bf16[528,256]{1,0:T(8,128)(2,1)S(1)} collective-permute-done((bf16[528,256]{1,0:T(8,128)(2,1)S(1)}, bf16[528,256]{1,0:T(8,128)(2,1)S(1)}, u32[]{:S(2)}, u32[]{:S(2)}) %collective-permute-start.3) | collective-permute-done | bytes 270368 | tf_op jit(solution)/shard_map/ppermute | solution.py:413
  35.9 1.6 %collective-permute-start.6 = (bf16[528,256]{1,0:T(8,128)(2,1)S(1)}, bf16[528,256]{1,0:T(8,128)(2,1)S(1)}, u32[]{:S(2)}, u32[]{:S(2)}) collective-permute-start(bf16[528,256]{1,0:T(8,128)(2,1)S(1)} %get-tuple-element.37), channel_id=1, source_target_pairs={{0,2},{1,3},{2,0},{3,1},{4,6},{5,7},{6,4},{7,5},{8,10},{9,11},{10,... | collective-permute-start | bytes 811016 | tf_op jit(solution)/shard_map/ppermute | solution.py:413
  37.5 5.7 %collective-permute-done.15.rest_1_ = bf16[528,256]{1,0:T(8,128)(2,1)S(1)} collective-permute-done((bf16[528,256]{1,0:T(8,128)(2,1)S(1)}, bf16[528,256]{1,0:T(8,128)(2,1)S(1)}, u32[]{:S(2)}, u32[]{:S(2)}) %collective-permute-start.15) | collective-permute-done | bytes 270368 | tf_op jit(solution)/shard_map/ppermute | solution.py:413
  43.2 1.4 %collective-permute-start.7 = (bf16[528,256]{1,0:T(8,128)(2,1)S(1)}, bf16[528,256]{1,0:T(8,128)(2,1)S(1)}, u32[]{:S(2)}, u32[]{:S(2)}) collective-permute-start(bf16[528,256]{1,0:T(8,128)(2,1)S(1)} %get-tuple-element.38), channel_id=1, source_target_pairs={{0,6},{1,7},{2,4},{3,5},{4,2},{5,3},{6,0},{7,1},{8,14},{9,15},{10,... | collective-permute-start | bytes 811016 | tf_op jit(solution)/shard_map/ppermute | solution.py:413
  44.6 0.0 collective-permute-done.9.rest_1_
  44.6 0.6 collective-permute-start.8
  45.2 1.2 %collective-permute-done.10.rest_2_ = bf16[528,256]{1,0:T(8,128)(2,1)S(1)} collective-permute-done((bf16[528,256]{1,0:T(8,128)(2,1)S(1)}, bf16[528,256]{1,0:T(8,128)(2,1)S(1)}, u32[]{:S(2)}, u32[]{:S(2)}) %collective-permute-start.10) | collective-permute-done | bytes 270368 | tf_op jit(solution)/shard_map/ppermute | solution.py:413
  46.4 3.2 %collective-permute-start.4 = (bf16[528,256]{1,0:T(8,128)(2,1)S(1)}, bf16[528,256]{1,0:T(8,128)(2,1)S(1)}, u32[]{:S(2)}, u32[]{:S(2)}) collective-permute-start(bf16[528,256]{1,0:T(8,128)(2,1)S(1)} %collective-permute-done.rest_1_), channel_id=1, source_target_pairs={{0,16},{1,17},{2,18},{3,19},{4,20},{5,21},{6,22},{7,23},{8,24},{9,... | collective-permute-start | bytes 811016 | tf_op jit(solution)/shard_map/ppermute | solution.py:413
  49.6 8.4 %collective-permute-done.11.rest_3_ = bf16[528,256]{1,0:T(8,128)(2,1)S(1)} collective-permute-done((bf16[528,256]{1,0:T(8,128)(2,1)S(1)}, bf16[528,256]{1,0:T(8,128)(2,1)S(1)}, u32[]{:S(2)}, u32[]{:S(2)}) %collective-permute-start.11) | collective-permute-done | bytes 270368 | tf_op jit(solution)/shard_map/ppermute | solution.py:413
  58.1 1.2 %collective-permute-start.5 = (bf16[528,256]{1,0:T(8,128)(2,1)S(1)}, bf16[528,256]{1,0:T(8,128)(2,1)S(1)}, u32[]{:S(2)}, u32[]{:S(2)}) collective-permute-start(bf16[528,256]{1,0:T(8,128)(2,1)S(1)} %collective-permute-done.1.rest_3_), channel_id=1, source_target_pairs={{0,18},{1,19},{2,16},{3,17},{4,22},{5,23},{6,20},{7,21},{8,26},{9,... | collective-permute-start | bytes 811016 | tf_op jit(solution)/shard_map/ppermute | solution.py:413
  59.3 0.1 slice_bitcast_fusion
  59.3 0.1 maximum_convert_fusion.2.ints
  59.4 1.6 %pack.5 = (bf16[528,256]{1,0:T(8,128)(2,1)S(1)}, bf16[528,256]{1,0:T(8,128)(2,1)S(1)}, bf16[528,256]{1,0:T(8,128)(2,1)}, bf16[528,256]{1,0:T(8,128)(2,1)}) custom-call(s32[8]{0:T(128)S(1)} %maximum_convert_fusion.2.ints, bf16[528,256]{1,0:T(8,128)(2,1)S(1)} %collective-permute-done.2.rest_0_, bf16[528,256]{1,0:T(8,128)(2,1)S(1)} %collective-permute-done.15.rest_1_), custom_call_target="tpu_custom_call" | custom-call | bytes 1081344 | tf_op jit(solution)/shard_map/pack/pallas_call | solution.py:312
  61.0 0.0 collective-permute-done.6.rest_4_
  61.0 0.5 collective-permute-start.16
  61.6 0.0 collective-permute-done.7.rest_5_
  61.6 3.4 %collective-permute-start.17 = (bf16[528,256]{1,0:T(8,128)(2,1)}, bf16[528,256]{1,0:T(8,128)(2,1)}, u32[]{:S(2)}, u32[]{:S(2)}) collective-permute-start(bf16[528,256]{1,0:T(8,128)(2,1)} %get-tuple-element.50), channel_id=1, source_target_pairs={{0,8},{1,9},{2,10},{3,11},{4,12},{5,13},{6,14},{7,15},{8,0},{9,1},... | collective-permute-start | bytes 811016 | tf_op jit(solution)/shard_map/ppermute | solution.py:413
  65.0 0.0 collective-permute-done.8.rest_6_
  65.0 0.0 collective-permute-start.18
  65.0 11.1 %collective-permute-done.5.rest_1_ = bf16[528,256]{1,0:T(8,128)(2,1)S(1)} collective-permute-done((bf16[528,256]{1,0:T(8,128)(2,1)S(1)}, bf16[528,256]{1,0:T(8,128)(2,1)S(1)}, u32[]{:S(2)}, u32[]{:S(2)}) %collective-permute-start.5) | collective-permute-done | bytes 270368 | tf_op jit(solution)/shard_map/ppermute | solution.py:413
  76.1 0.1 slice_bitcast_fusion.3
  76.2 0.1 maximum_convert_fusion.1.ints
  76.3 1.6 %pack.4 = (bf16[528,256]{1,0:T(8,128)(2,1)S(1)}, bf16[528,256]{1,0:T(8,128)(2,1)}, bf16[528,256]{1,0:T(8,128)(2,1)}, bf16[528,256]{1,0:T(8,128)(2,1)}) custom-call(s32[8]{0:T(128)S(1)} %maximum_convert_fusion.1.ints, bf16[528,256]{1,0:T(8,128)(2,1)S(1)} %collective-permute-done.4.rest_0_, bf16[528,256]{1,0:T(8,128)(2,1)S(1)} %collective-permute-done.5.rest_1_), custom_call_target="tpu_custom_call" | custom-call | bytes 1081344 | tf_op jit(solution)/shard_map/pack/pallas_call | solution.py:312
  77.9 0.7 copy-done.2
  78.6 0.5 collective-permute-start.12
  79.1 3.0 %collective-permute-start.14 = (bf16[528,256]{1,0:T(8,128)(2,1)}, bf16[528,256]{1,0:T(8,128)(2,1)}, u32[]{:S(2)}, u32[]{:S(2)}) collective-permute-start(bf16[528,256]{1,0:T(8,128)(2,1)} %get-tuple-element.47), channel_id=1, source_target_pairs={{0,12},{1,13},{2,14},{3,15},{4,8},{5,9},{6,10},{7,11},{8,4},{9,5},... | collective-permute-start | bytes 811016 | tf_op jit(solution)/shard_map/ppermute | solution.py:413
  82.1 0.1 stack.34.places
  82.2 0.1 stack.72.places
  82.3 0.1 stack.79.places
  82.4 3.0 %finish.3.rest_5_ = bf16[2,2,8,2,8,16,512]{6,5,4,3,2,1,0:T(8,128)(2,1)} custom-call(s32[24]{0:T(128)S(1)} %stack.79.places, bf16[256,512]{1,0:T(8,128)(2,1)S(1)} %copy-done.1, f32[1,512]{1,0:T(1,128)S(1)} %bitcast.30, bf16[256,1024]{1,0:T(8,128)(2,1)S(1)} %copy-done, bf16[528,256]{1,0:T(8,128)(2,1)S(1)} %get-tuple-element.33.rest_0_, ...), custom_call_target="tpu_custom_call" | custom-call | flops 1073741824 | bytes 6291456 | tf_op jit(solution)/shard_map/finish/pallas_call | solution.py:372
  85.5 3.5 %finish.4.rest_3_ = bf16[2,2,8,2,8,16,512]{6,5,4,3,2,1,0:T(8,128)(2,1)} custom-call(s32[15]{0:T(128)S(1)} %stack.72.places, bf16[256,512]{1,0:T(8,128)(2,1)S(1)} %copy-done.1, f32[1,512]{1,0:T(1,128)S(1)} %bitcast.31, bf16[256,1024]{1,0:T(8,128)(2,1)S(1)} %copy-done, bf16[528,256]{1,0:T(8,128)(2,1)S(1)} %get-tuple-element.48.rest_0_, ...), custom_call_target="tpu_custom_call", output_to_operand_aliasing={{}: (9, {})} | custom-call | flops 671088640 | bytes 3932160 | tf_op jit(solution)/shard_map/finish/pallas_call | solution.py:372
  89.0 4.0 %collective-permute-done.14.rest_2_ = bf16[528,256]{1,0:T(8,128)(2,1)} collective-permute-done((bf16[528,256]{1,0:T(8,128)(2,1)}, bf16[528,256]{1,0:T(8,128)(2,1)}, u32[]{:S(2)}, u32[]{:S(2)}) %collective-permute-start.14) | collective-permute-done | bytes 270368 | tf_op jit(solution)/shard_map/ppermute | solution.py:413
  93.0 3.2 %finish.5 = bf16[2,2,8,2,8,16,512]{6,5,4,3,2,1,0:T(8,128)(2,1)} custom-call(s32[9]{0:T(128)S(1)} %stack.34.places, bf16[256,512]{1,0:T(8,128)(2,1)S(1)} %copy-done.1, f32[1,512]{1,0:T(1,128)S(1)} %bitcast.32, bf16[256,1024]{1,0:T(8,128)(2,1)S(1)} %copy-done, bf16[528,256]{1,0:T(8,128)(2,1)} %collective-permute-done.12.rest_0_, ...), custom_call_target="tpu_custom_call", output_to_operand_aliasing={{}: (7, {})} | custom-call | flops 402653184 | bytes 2359296 | tf_op jit(solution)/shard_map/finish/pallas_call | solution.py:372
  (18 shorter events, 0.0 us)
Async XLA Ops:
  0.0 82.4 %copy-start = (bf16[256,1024]{1,0:T(8,128)(2,1)S(1)}, bf16[256,1024]{1,0:T(8,128)(2,1)}, u32[]{:S(2)}) copy-start(bf16[256,1024]{1,0:T(8,128)(2,1)} %constant.73.clone.place) | copy-start | bytes 1572868
  0.0 82.4 %copy-start.1 = (bf16[256,512]{1,0:T(8,128)(2,1)S(1)}, bf16[256,512]{1,0:T(8,128)(2,1)}, u32[]{:S(2)}) copy-start(bf16[256,512]{1,0:T(8,128)(2,1)} %w3.5) | copy-start | bytes 786436
  0.0 82.4 %copy-start.4 = (f32[512]{0:T(512)S(1)}, f32[512]{0:T(512)}, u32[]{:S(2)}) copy-start(f32[512]{0:T(512)} %param.19) | copy-start | bytes 6148
  13.2 4.7 %collective-permute-start = (bf16[528,256]{1,0:T(8,128)(2,1)S(1)}, bf16[528,256]{1,0:T(8,128)(2,1)S(1)}, u32[]{:S(2)}, u32[]{:S(2)}) collective-permute-start(bf16[528,256]{1,0:T(8,128)(2,1)S(1)} %get-tuple-element.29), channel_id=1, source_target_pairs={{0,1},{1,0},{2,3},{3,2},{4,5},{5,4},{6,7},{7,6},{8,9},{9,8},{10,11... | collective-permute-start | bytes 811016 | tf_op jit(solution)/shard_map/ppermute | solution.py:413
  13.8 4.3 %collective-permute-start.1 = (bf16[528,256]{1,0:T(8,128)(2,1)S(1)}, bf16[528,256]{1,0:T(8,128)(2,1)S(1)}, u32[]{:S(2)}, u32[]{:S(2)}) collective-permute-start(bf16[528,256]{1,0:T(8,128)(2,1)S(1)} %get-tuple-element.30), channel_id=1, source_target_pairs={{0,1},{1,0},{2,3},{3,2},{4,5},{5,4},{6,7},{7,6},{8,9},{9,8},{10,11... | collective-permute-start | bytes 811016 | tf_op jit(solution)/shard_map/ppermute | solution.py:413
  13.8 17.4 %collective-permute-start.2 = (bf16[528,256]{1,0:T(8,128)(2,1)S(1)}, bf16[528,256]{1,0:T(8,128)(2,1)S(1)}, u32[]{:S(2)}, u32[]{:S(2)}) collective-permute-start(bf16[528,256]{1,0:T(8,128)(2,1)S(1)} %get-tuple-element.31.rest_0_), channel_id=1, source_target_pairs={{0,16},{1,17},{2,18},{3,19},{4,20},{5,21},{6,22},{7,23},{8,24},{9,... | collective-permute-start | bytes 811016 | tf_op jit(solution)/shard_map/ppermute | solution.py:413
  18.9 17.0 %collective-permute-start.3 = (bf16[528,256]{1,0:T(8,128)(2,1)S(1)}, bf16[528,256]{1,0:T(8,128)(2,1)S(1)}, u32[]{:S(2)}, u32[]{:S(2)}) collective-permute-start(bf16[528,256]{1,0:T(8,128)(2,1)S(1)} %get-tuple-element.40), channel_id=1, source_target_pairs={{0,14},{1,15},{2,12},{3,13},{4,10},{5,11},{6,8},{7,9},{8,6},{9,7},... | collective-permute-start | bytes 811016 | tf_op jit(solution)/shard_map/ppermute | solution.py:413
  22.4 20.8 %collective-permute-start.15 = (bf16[528,256]{1,0:T(8,128)(2,1)S(1)}, bf16[528,256]{1,0:T(8,128)(2,1)S(1)}, u32[]{:S(2)}, u32[]{:S(2)}) collective-permute-start(bf16[528,256]{1,0:T(8,128)(2,1)S(1)} %get-tuple-element.32.rest_2_), channel_id=1, source_target_pairs={{0,18},{1,19},{2,16},{3,17},{4,22},{5,23},{6,20},{7,21},{8,26},{9,... | collective-permute-start | bytes 811016 | tf_op jit(solution)/shard_map/ppermute | solution.py:413
  23.5 21.1 %collective-permute-start.9 = (bf16[528,256]{1,0:T(8,128)(2,1)S(1)}, bf16[528,256]{1,0:T(8,128)(2,1)S(1)}, u32[]{:S(2)}, u32[]{:S(2)}) collective-permute-start(bf16[528,256]{1,0:T(8,128)(2,1)S(1)} %get-tuple-element.34), channel_id=1, source_target_pairs={{0,4},{1,5},{2,6},{3,7},{4,0},{5,1},{6,2},{7,3},{8,12},{9,13},{10,... | collective-permute-start | bytes 811016 | tf_op jit(solution)/shard_map/ppermute | solution.py:413
  24.1 22.3 %collective-permute-start.10 = (bf16[528,256]{1,0:T(8,128)(2,1)S(1)}, bf16[528,256]{1,0:T(8,128)(2,1)S(1)}, u32[]{:S(2)}, u32[]{:S(2)}) collective-permute-start(bf16[528,256]{1,0:T(8,128)(2,1)S(1)} %get-tuple-element.35), channel_id=1, source_target_pairs={{0,8},{1,9},{2,10},{3,11},{4,12},{5,13},{6,14},{7,15},{8,0},{9,1},... | collective-permute-start | bytes 811016 | tf_op jit(solution)/shard_map/ppermute | solution.py:413
  31.3 26.8 %collective-permute-start.11 = (bf16[528,256]{1,0:T(8,128)(2,1)S(1)}, bf16[528,256]{1,0:T(8,128)(2,1)S(1)}, u32[]{:S(2)}, u32[]{:S(2)}) collective-permute-start(bf16[528,256]{1,0:T(8,128)(2,1)S(1)} %get-tuple-element.36), channel_id=1, source_target_pairs={{0,12},{1,13},{2,14},{3,15},{4,8},{5,9},{6,10},{7,11},{8,4},{9,5},... | collective-permute-start | bytes 811016 | tf_op jit(solution)/shard_map/ppermute | solution.py:413
  35.9 25.1 %collective-permute-start.6 = (bf16[528,256]{1,0:T(8,128)(2,1)S(1)}, bf16[528,256]{1,0:T(8,128)(2,1)S(1)}, u32[]{:S(2)}, u32[]{:S(2)}) collective-permute-start(bf16[528,256]{1,0:T(8,128)(2,1)S(1)} %get-tuple-element.37), channel_id=1, source_target_pairs={{0,2},{1,3},{2,0},{3,1},{4,6},{5,7},{6,4},{7,5},{8,10},{9,11},{10,... | collective-permute-start | bytes 811016 | tf_op jit(solution)/shard_map/ppermute | solution.py:413
  43.2 18.4 %collective-permute-start.7 = (bf16[528,256]{1,0:T(8,128)(2,1)S(1)}, bf16[528,256]{1,0:T(8,128)(2,1)S(1)}, u32[]{:S(2)}, u32[]{:S(2)}) collective-permute-start(bf16[528,256]{1,0:T(8,128)(2,1)S(1)} %get-tuple-element.38), channel_id=1, source_target_pairs={{0,6},{1,7},{2,4},{3,5},{4,2},{5,3},{6,0},{7,1},{8,14},{9,15},{10,... | collective-permute-start | bytes 811016 | tf_op jit(solution)/shard_map/ppermute | solution.py:413
  44.6 20.4 %collective-permute-start.8 = (bf16[528,256]{1,0:T(8,128)(2,1)S(1)}, bf16[528,256]{1,0:T(8,128)(2,1)S(1)}, u32[]{:S(2)}, u32[]{:S(2)}) collective-permute-start(bf16[528,256]{1,0:T(8,128)(2,1)S(1)} %get-tuple-element.39), channel_id=1, source_target_pairs={{0,10},{1,11},{2,8},{3,9},{4,14},{5,15},{6,12},{7,13},{8,2},{9,3},... | collective-permute-start | bytes 811016 | tf_op jit(solution)/shard_map/ppermute | solution.py:413
  46.4 18.6 %collective-permute-start.4 = (bf16[528,256]{1,0:T(8,128)(2,1)S(1)}, bf16[528,256]{1,0:T(8,128)(2,1)S(1)}, u32[]{:S(2)}, u32[]{:S(2)}) collective-permute-start(bf16[528,256]{1,0:T(8,128)(2,1)S(1)} %collective-permute-done.rest_1_), channel_id=1, source_target_pairs={{0,16},{1,17},{2,18},{3,19},{4,20},{5,21},{6,22},{7,23},{8,24},{9,... | collective-permute-start | bytes 811016 | tf_op jit(solution)/shard_map/ppermute | solution.py:413
  58.1 18.1 %collective-permute-start.5 = (bf16[528,256]{1,0:T(8,128)(2,1)S(1)}, bf16[528,256]{1,0:T(8,128)(2,1)S(1)}, u32[]{:S(2)}, u32[]{:S(2)}) collective-permute-start(bf16[528,256]{1,0:T(8,128)(2,1)S(1)} %collective-permute-done.1.rest_3_), channel_id=1, source_target_pairs={{0,18},{1,19},{2,16},{3,17},{4,22},{5,23},{6,20},{7,21},{8,26},{9,... | collective-permute-start | bytes 811016 | tf_op jit(solution)/shard_map/ppermute | solution.py:413
  61.0 18.1 %collective-permute-start.16 = (bf16[528,256]{1,0:T(8,128)(2,1)S(1)}, bf16[528,256]{1,0:T(8,128)(2,1)S(1)}, u32[]{:S(2)}, u32[]{:S(2)}) collective-permute-start(bf16[528,256]{1,0:T(8,128)(2,1)S(1)} %get-tuple-element.49), channel_id=1, source_target_pairs={{0,4},{1,5},{2,6},{3,7},{4,0},{5,1},{6,2},{7,3},{8,12},{9,13},{10,... | collective-permute-start | bytes 811016 | tf_op jit(solution)/shard_map/ppermute | solution.py:413
  61.6 23.9 %collective-permute-start.17 = (bf16[528,256]{1,0:T(8,128)(2,1)}, bf16[528,256]{1,0:T(8,128)(2,1)}, u32[]{:S(2)}, u32[]{:S(2)}) collective-permute-start(bf16[528,256]{1,0:T(8,128)(2,1)} %get-tuple-element.50), channel_id=1, source_target_pairs={{0,8},{1,9},{2,10},{3,11},{4,12},{5,13},{6,14},{7,15},{8,0},{9,1},... | collective-permute-start | bytes 811016 | tf_op jit(solution)/shard_map/ppermute | solution.py:413
  65.0 20.5 %collective-permute-start.18 = (bf16[528,256]{1,0:T(8,128)(2,1)}, bf16[528,256]{1,0:T(8,128)(2,1)}, u32[]{:S(2)}, u32[]{:S(2)}) collective-permute-start(bf16[528,256]{1,0:T(8,128)(2,1)} %get-tuple-element.51), channel_id=1, source_target_pairs={{0,12},{1,13},{2,14},{3,15},{4,8},{5,9},{6,10},{7,11},{8,4},{9,5},... | collective-permute-start | bytes 811016 | tf_op jit(solution)/shard_map/ppermute | solution.py:413
  77.9 0.7 copy-start.2
  78.6 10.4 %collective-permute-start.12 = (bf16[528,256]{1,0:T(8,128)(2,1)}, bf16[528,256]{1,0:T(8,128)(2,1)}, u32[]{:S(2)}, u32[]{:S(2)}) collective-permute-start(bf16[528,256]{1,0:T(8,128)(2,1)} %get-tuple-element.45), channel_id=1, source_target_pairs={{0,4},{1,5},{2,6},{3,7},{4,0},{5,1},{6,2},{7,3},{8,12},{9,13},{10,... | collective-permute-start | bytes 811016 | tf_op jit(solution)/shard_map/ppermute | solution.py:413
  79.1 9.9 %collective-permute-start.13 = (bf16[528,256]{1,0:T(8,128)(2,1)}, bf16[528,256]{1,0:T(8,128)(2,1)}, u32[]{:S(2)}, u32[]{:S(2)}) collective-permute-start(bf16[528,256]{1,0:T(8,128)(2,1)} %get-tuple-element.46), channel_id=1, source_target_pairs={{0,8},{1,9},{2,10},{3,11},{4,12},{5,13},{6,14},{7,15},{8,0},{9,1},... | collective-permute-start | bytes 811016 | tf_op jit(solution)/shard_map/ppermute | solution.py:413
  79.1 13.9 %collective-permute-start.14 = (bf16[528,256]{1,0:T(8,128)(2,1)}, bf16[528,256]{1,0:T(8,128)(2,1)}, u32[]{:S(2)}, u32[]{:S(2)}) collective-permute-start(bf16[528,256]{1,0:T(8,128)(2,1)} %get-tuple-element.47), channel_id=1, source_target_pairs={{0,12},{1,13},{2,14},{3,15},{4,8},{5,9},{6,10},{7,11},{8,4},{9,5},... | collective-permute-start | bytes 811016 | tf_op jit(solution)/shard_map/ppermute | solution.py:413
  82.4 3.1 %copy-start.3 = (bf16[528,256]{1,0:T(8,128)(2,1)S(1)}, bf16[528,256]{1,0:T(8,128)(2,1)}, u32[]{:S(2)}) copy-start(bf16[528,256]{1,0:T(8,128)(2,1)} %copy-done.2) | copy-start | bytes 811012
